TPU v7x, 128 devices: a whole 4x4x4 slice. The times are simulated.
128 devices in a mesh: region: 8 (over z, core), dev: 16 (over x, y).
Axes of the slice: x: 4, y: 4, z: 4, core: 2. Of those that a mesh axis runs over, the one named last changes fastest.
Arguments:
- loads: float32 [1024, 32, 1024], P(('region', 'dev')), may hold values from -50 to 50
- factor: bfloat16 [1024, 1024, 1024], P(('region', 'dev')), may hold values from -1 to 1, as said below
- pivots: float32 [1024, 1024], P(('region', 'dev')), may hold values from 0.04 to 0.14, as said below
- lower: float32 [1024, 1024], P(('region', 'dev')), may hold values from -1 to -0.2
- upper: float32 [1024, 1024], P(('region', 'dev')), may hold values from 0.2 to 1
- incidence: int32 [1024, 16], P(('region', 'dev')), may hold values from 0 to 2047, as said below
- counts: int32 [1024], P(('region', 'dev')), may hold values from 8 to 16, as said below
Outputs:
- dispatch: float32 [1024, 32, 1024], P(('region', 'dev'))
- duals: float32 [1024, 16, 128], P(('region', 'dev'))
- residuals: float32 [14, 2], replicated
Inputs may be any that keep to these rules, and one draw needn't show every extreme that they name: `incidence`: slot j of area a is live when j < counts[a]. Bus b is owned by device b // 16, devices numbered region-major. The live slots of one device name at most 8 buses owned by any one device of its own region and at most 8 buses owned in any one other region; in every draw every device reaches both bounds. A bus owned in another region is owned by the device with the same dev index there. `counts`: among the 8 areas of each device one has 16 live slots and the others at least 8. `factor`: unit lower triangular: ones on the diagonal, zeros above it. Rows below 64 of every area have inverse pivots of 0.10 or more; the other rows have them up to 0.14 as well.
All inputs are finite; a program needn't handle non-finite values.
Results may differ from a plain program's by a relative error of at most 0.005.
Values sent between devices are 32-bit elements; how exact they have to be, the bound alone decides.
No kernel may reach another device: no remote copies, remote signals or barrier semaphores. Data moves between devices by JAX's collectives and lax.ppermute only.
A program may use at most 64 MiB of HBM per device.

v0:
```python
import jax
import jax.numpy as jnp
from jax import lax
from jax.sharding import PartitionSpec as P

ROWS_SLOT = 4
BLK = 128
BUS_DEV = 16
CAP_X = 8
ITERS = 14


RHO = 4.0
SIGMA = 1.0
HIGH = lax.Precision.HIGHEST


def to_blocks(state_field, slot_count, row_group):
    area_count, scenarios, system_order = state_field.shape
    leading = state_field[:, :, : slot_count * row_group].reshape(
        area_count, scenarios, slot_count, row_group
    )
    return jnp.transpose(leading, (0, 2, 1, 3)).reshape(
        area_count, slot_count, scenarios * row_group
    )


def from_blocks(blocks, scenarios, row_group, system_order):
    area_count, slot_count, block_values = blocks.shape
    leading = jnp.transpose(
        blocks.reshape(area_count, slot_count, scenarios, row_group), (0, 2, 1, 3)
    )
    leading = leading.reshape(area_count, scenarios, slot_count * row_group)
    return jnp.pad(leading, ((0, 0), (0, 0), (0, system_order - slot_count * row_group)))


def apply_inverse(right_side, factor, pivots, block_width):
    rounded = right_side.astype(jnp.bfloat16)
    system_order = factor.shape[1]
    block_count = system_order // block_width
    pieces = []
    for index_row in range(block_count):
        finish = (index_row + 1) * block_width
        pieces.append(
            jnp.einsum(
                "ask,aik->asi",
                rounded[:, :, :finish],
                factor[:, index_row * block_width : finish, :finish],
                preferred_element_type=jnp.float32,
            )
        )
    forward = jnp.concatenate(pieces, axis=2)
    scaled = (forward * pivots[:, None, :]).astype(jnp.bfloat16)
    results = []
    for index_col in range(block_count):
        begin = index_col * block_width
        results.append(
            jnp.einsum(
                "asi,aik->ask",
                scaled[:, :, begin:],
                factor[:, begin:, begin : begin + block_width],
                preferred_element_type=jnp.float32,
            )
        )
    return jnp.concatenate(results, axis=2)


def select(selector, values):
    return jnp.dot(selector, values, precision=HIGH, preferred_element_type=jnp.float32)


def on_device(loads, factor, pivots, lower, upper, incidence, counts):
    area_count, scenarios, system_order = loads.shape
    slot_count = incidence.shape[1]
    item_count = area_count * slot_count
    block_values = scenarios * ROWS_SLOT
    n_dev = lax.axis_size("dev")
    n_region = lax.axis_size("region")
    cap_near = max(item_count // n_dev, 2)
    my_region = lax.axis_index("region")
    live_slot = (jnp.arange(slot_count)[None, :] < counts[:, None]).reshape(item_count)
    bus_ids = incidence.reshape(item_count)
    owner_dev = bus_ids // BUS_DEV
    owner_region = owner_dev // n_dev
    owner_peer = owner_dev % n_dev
    near_live = live_slot & (owner_region == my_region)
    far_live = live_slot & (owner_region != my_region)
    earlier = jnp.arange(item_count)[None, :] < jnp.arange(item_count)[:, None]
    rank_near = jnp.sum(
        near_live[None, :] & (owner_peer[None, :] == owner_peer[:, None]) & earlier, axis=1
    )
    rank_far = jnp.sum(
        far_live[None, :] & (owner_region[None, :] == owner_region[:, None]) & earlier, axis=1
    )
    slot_near = jnp.where(near_live, owner_peer * cap_near + rank_near, -1)
    slot_far = jnp.where(far_live, owner_region * CAP_X + rank_far, -1)
    near_hits = jnp.arange(n_dev * cap_near)[:, None] == slot_near[None, :]
    far_hits = jnp.arange(n_region * CAP_X)[:, None] == slot_far[None, :]
    pick_near = near_hits.astype(jnp.float32)
    pick_far = far_hits.astype(jnp.float32)
    far_tags = jnp.sum(jnp.where(far_hits, bus_ids[None, :] + 1, 0), axis=1) - 1
    got_far_tags = lax.all_to_all(far_tags, "region", split_axis=0, concat_axis=0, tiled=True)
    near_tags = jnp.sum(jnp.where(near_hits, bus_ids[None, :] + 1, 0), axis=1) - 1
    got_near_tags = lax.all_to_all(near_tags, "dev", split_axis=0, concat_axis=0, tiled=True)
    listed_tags = jnp.concatenate([got_near_tags, got_far_tags])
    same_bus = (
        (listed_tags[:, None] == listed_tags[None, :]) & (listed_tags[:, None] >= 0)
    ).astype(jnp.float32)
    far_start = n_dev * cap_near
    members = jnp.maximum(jnp.sum(same_bus, axis=1), 1.0)
    live_col = live_slot.astype(jnp.float32)[:, None]
    floor_box = lower[:, None, :]
    ceil_box = upper[:, None, :]
    total_cells = float(area_count * n_dev * n_region * block_values)

    def iterate(step_num, state_now):
        dispatch, clipped, offset, duals, z_slot, z_prev, record = state_now
        pushed = from_blocks(
            ((z_slot - duals) * live_col).reshape(area_count, slot_count, block_values),
            scenarios,
            ROWS_SLOT,
            system_order,
        )
        right_side = loads + RHO * pushed + SIGMA * (clipped - offset)
        dispatch = apply_inverse(right_side, factor, pivots, BLK)
        clipped_new = jnp.clip(dispatch + offset, floor_box, ceil_box)
        offset = offset + dispatch - clipped_new
        blocks = to_blocks(dispatch, slot_count, ROWS_SLOT).reshape(item_count, block_values)
        values = (blocks + duals) * live_col
        got_far = lax.all_to_all(
            select(pick_far, values), "region", split_axis=0, concat_axis=0, tiled=True
        )
        got_near = lax.all_to_all(
            select(pick_near, values), "dev", split_axis=0, concat_axis=0, tiled=True
        )
        z_list = select(same_bus, jnp.concatenate([got_near, got_far])) / members[:, None]
        back_near = lax.all_to_all(
            z_list[:far_start], "dev", split_axis=0, concat_axis=0, tiled=True
        )
        near_part = select(pick_near.T, back_near)
        back_far = lax.all_to_all(
            z_list[far_start:], "region", split_axis=0, concat_axis=0, tiled=True
        )
        z_slot = near_part + select(pick_far.T, back_far)
        misfit = (blocks - z_slot) * live_col
        duals = duals + misfit
        change = z_list - z_prev
        partial_value = (
            jnp.stack(
                [jnp.sum(misfit * misfit), RHO * RHO * jnp.sum(change * change / members[:, None])]
            )
            / total_cells
        )
        partial_value = lax.psum(partial_value, ("region", "dev"))
        record = record.at[step_num].set(partial_value)
        return (dispatch, clipped_new, offset, duals, z_slot, z_list, record)

    start_state = (
        jnp.zeros_like(loads),
        jnp.zeros_like(loads),
        jnp.zeros_like(loads),
        jnp.zeros((item_count, block_values), jnp.float32),
        jnp.zeros((item_count, block_values), jnp.float32),
        jnp.zeros((same_bus.shape[0], block_values), jnp.float32),
        jnp.zeros((ITERS, 2), jnp.float32),
    )
    final_state = lax.fori_loop(0, ITERS, iterate, start_state)
    dispatch = final_state[0]
    duals = final_state[3].reshape(area_count, slot_count, block_values)
    record = final_state[6]
    return (dispatch, duals, record)


def solution(mesh):
    placed = (
        P(("region", "dev"), None, None),
        P(("region", "dev"), None, None),
        P(("region", "dev"), None),
        P(("region", "dev"), None),
        P(("region", "dev"), None),
        P(("region", "dev"), None),
        P(("region", "dev")),
    )
    return jax.shard_map(
        on_device,
        mesh=mesh,
        in_specs=placed,
        out_specs=(P(("region", "dev"), None, None), P(("region", "dev"), None, None), P()),
        check_vma=False,
    )
```

profile of v0, /device:TPU:1, one launch (start us, length us, event | category | flops | bytes accessed | tf_op | source)
XLA Modules:
  0.0 2063.5 jit_solution(16268525831127423452)
XLA Ops:
  3.6 6.8 all-to-all-start.5
  14.9 6.8 all-to-all-start.4
  23.1 4.9 all-to-all-done.4
  35.9 2025.5 %while.29 = (s32[]{:T(128)}, f32[8,32,1024]{2,1,0:T(8,128)}, f32[8,32,1024]{2,1,0:T(8,128)}, f32[8,32,1024]{2,1,0:T(8,128)S(1)}, f32[128,128]{0,1:T(8,128)S(1)},...) while((s32[]{:T(128)}, f32[8,32,1024]{2,1,0:T(8,128)}, ...), condition=%wide.region_10.11_spmd.clone, body=%wide.region_5.10_spmd.clone.sunk | while | flops 740389120 | bytes 42671920 | solution.py:167
  58.2 5.4 all-to-all-start
  82.2 5.7 all-to-all-done.1
  97.3 4.5 all-to-all-done.2
  101.8 7.1 all-to-all-start.3
  115.8 62.7 %psum.16 = f32[1,2]{1,0:T(1,128)S(1)} all-reduce(f32[1,2]{1,0:T(1,128)S(1)} %fusion.197), channel_id=1, replica_groups=mesh['region'=8,'dev'=16] {'region','dev'}, use_global_device_ids=true, to_apply=%region_9.9 | all-reduce | flops 2 | bytes 16 | tf_op jit(solution)/shard_map/while/body/eval_jaxpr/psum | solution.py:154
  226.5 5.7 all-to-all-done.1
  241.6 4.5 all-to-all-done.2
  246.2 7.4 all-to-all-start.3
  253.9 4.4 all-to-all-done.3
  260.4 62.7 %psum.16 = f32[1,2]{1,0:T(1,128)S(1)} all-reduce(f32[1,2]{1,0:T(1,128)S(1)} %fusion.197), channel_id=1, replica_groups=mesh['region'=8,'dev'=16] {'region','dev'}, use_global_device_ids=true, to_apply=%region_9.9 | all-reduce | flops 2 | bytes 16 | tf_op jit(solution)/shard_map/while/body/eval_jaxpr/psum | solution.py:154
  371.2 5.7 all-to-all-done.1
  386.3 4.5 all-to-all-done.2
  390.8 7.4 all-to-all-start.3
  398.5 4.4 all-to-all-done.3
  405.1 62.7 %psum.16 = f32[1,2]{1,0:T(1,128)S(1)} all-reduce(f32[1,2]{1,0:T(1,128)S(1)} %fusion.197), channel_id=1, replica_groups=mesh['region'=8,'dev'=16] {'region','dev'}, use_global_device_ids=true, to_apply=%region_9.9 | all-reduce | flops 2 | bytes 16 | tf_op jit(solution)/shard_map/while/body/eval_jaxpr/psum | solution.py:154
  515.8 5.7 all-to-all-done.1
  530.9 4.5 all-to-all-done.2
  535.4 7.4 all-to-all-start.3
  543.1 4.4 all-to-all-done.3
  549.7 62.7 %psum.16 = f32[1,2]{1,0:T(1,128)S(1)} all-reduce(f32[1,2]{1,0:T(1,128)S(1)} %fusion.197), channel_id=1, replica_groups=mesh['region'=8,'dev'=16] {'region','dev'}, use_global_device_ids=true, to_apply=%region_9.9 | all-reduce | flops 2 | bytes 16 | tf_op jit(solution)/shard_map/while/body/eval_jaxpr/psum | solution.py:154
  660.4 5.7 all-to-all-done.1
  675.6 4.5 all-to-all-done.2
  680.1 7.4 all-to-all-start.3
  694.4 62.7 %psum.16 = f32[1,2]{1,0:T(1,128)S(1)} all-reduce(f32[1,2]{1,0:T(1,128)S(1)} %fusion.197), channel_id=1, replica_groups=mesh['region'=8,'dev'=16] {'region','dev'}, use_global_device_ids=true, to_apply=%region_9.9 | all-reduce | flops 2 | bytes 16 | tf_op jit(solution)/shard_map/while/body/eval_jaxpr/psum | solution.py:154
  805.1 5.7 all-to-all-done.1
  820.2 4.5 all-to-all-done.2
  824.7 7.4 all-to-all-start.3
  839.0 62.7 %psum.16 = f32[1,2]{1,0:T(1,128)S(1)} all-reduce(f32[1,2]{1,0:T(1,128)S(1)} %fusion.197), channel_id=1, replica_groups=mesh['region'=8,'dev'=16] {'region','dev'}, use_global_device_ids=true, to_apply=%region_9.9 | all-reduce | flops 2 | bytes 16 | tf_op jit(solution)/shard_map/while/body/eval_jaxpr/psum | solution.py:154
  949.7 5.7 all-to-all-done.1
  964.8 4.5 all-to-all-done.2
  969.4 7.4 all-to-all-start.3
  983.6 62.7 %psum.16 = f32[1,2]{1,0:T(1,128)S(1)} all-reduce(f32[1,2]{1,0:T(1,128)S(1)} %fusion.197), channel_id=1, replica_groups=mesh['region'=8,'dev'=16] {'region','dev'}, use_global_device_ids=true, to_apply=%region_9.9 | all-reduce | flops 2 | bytes 16 | tf_op jit(solution)/shard_map/while/body/eval_jaxpr/psum | solution.py:154
  1094.4 5.7 all-to-all-done.1
  1109.5 4.5 all-to-all-done.2
  1114.0 7.4 all-to-all-start.3
  1128.3 62.7 %psum.16 = f32[1,2]{1,0:T(1,128)S(1)} all-reduce(f32[1,2]{1,0:T(1,128)S(1)} %fusion.197), channel_id=1, replica_groups=mesh['region'=8,'dev'=16] {'region','dev'}, use_global_device_ids=true, to_apply=%region_9.9 | all-reduce | flops 2 | bytes 16 | tf_op jit(solution)/shard_map/while/body/eval_jaxpr/psum | solution.py:154
  1239.0 5.7 all-to-all-done.1
  1254.1 4.5 all-to-all-done.2
  1258.6 7.4 all-to-all-start.3
  1272.9 62.7 %psum.16 = f32[1,2]{1,0:T(1,128)S(1)} all-reduce(f32[1,2]{1,0:T(1,128)S(1)} %fusion.197), channel_id=1, replica_groups=mesh['region'=8,'dev'=16] {'region','dev'}, use_global_device_ids=true, to_apply=%region_9.9 | all-reduce | flops 2 | bytes 16 | tf_op jit(solution)/shard_map/while/body/eval_jaxpr/psum | solution.py:154
  1383.6 5.7 all-to-all-done.1
  1398.8 4.5 all-to-all-done.2
  1403.3 7.4 all-to-all-start.3
  1417.6 62.7 %psum.16 = f32[1,2]{1,0:T(1,128)S(1)} all-reduce(f32[1,2]{1,0:T(1,128)S(1)} %fusion.197), channel_id=1, replica_groups=mesh['region'=8,'dev'=16] {'region','dev'}, use_global_device_ids=true, to_apply=%region_9.9 | all-reduce | flops 2 | bytes 16 | tf_op jit(solution)/shard_map/while/body/eval_jaxpr/psum | solution.py:154
  1528.3 5.7 all-to-all-done.1
  1543.4 4.5 all-to-all-done.2
  1547.9 7.4 all-to-all-start.3
  1562.2 62.7 %psum.16 = f32[1,2]{1,0:T(1,128)S(1)} all-reduce(f32[1,2]{1,0:T(1,128)S(1)} %fusion.197), channel_id=1, replica_groups=mesh['region'=8,'dev'=16] {'region','dev'}, use_global_device_ids=true, to_apply=%region_9.9 | all-reduce | flops 2 | bytes 16 | tf_op jit(solution)/shard_map/while/body/eval_jaxpr/psum | solution.py:154
  1672.9 5.7 all-to-all-done.1
  1688.0 4.5 all-to-all-done.2
  1692.5 7.4 all-to-all-start.3
  1706.8 62.7 %psum.16 = f32[1,2]{1,0:T(1,128)S(1)} all-reduce(f32[1,2]{1,0:T(1,128)S(1)} %fusion.197), channel_id=1, replica_groups=mesh['region'=8,'dev'=16] {'region','dev'}, use_global_device_ids=true, to_apply=%region_9.9 | all-reduce | flops 2 | bytes 16 | tf_op jit(solution)/shard_map/while/body/eval_jaxpr/psum | solution.py:154
  1817.5 5.7 all-to-all-done.1
  1832.7 4.5 all-to-all-done.2
  1837.2 7.4 all-to-all-start.3
  1851.5 62.7 %psum.16 = f32[1,2]{1,0:T(1,128)S(1)} all-reduce(f32[1,2]{1,0:T(1,128)S(1)} %fusion.197), channel_id=1, replica_groups=mesh['region'=8,'dev'=16] {'region','dev'}, use_global_device_ids=true, to_apply=%region_9.9 | all-reduce | flops 2 | bytes 16 | tf_op jit(solution)/shard_map/while/body/eval_jaxpr/psum | solution.py:154
  1962.2 5.7 all-to-all-done.1
  1977.3 4.5 all-to-all-done.2
  1981.8 7.4 all-to-all-start.3
  1996.1 62.7 %psum.16 = f32[1,2]{1,0:T(1,128)S(1)} all-reduce(f32[1,2]{1,0:T(1,128)S(1)} %fusion.197), channel_id=1, replica_groups=mesh['region'=8,'dev'=16] {'region','dev'}, use_global_device_ids=true, to_apply=%region_9.9 | all-reduce | flops 2 | bytes 16 | tf_op jit(solution)/shard_map/while/body/eval_jaxpr/psum | solution.py:154
  (733 shorter events, 890.9 us)
Async XLA Ops:
  3.6 11.3 all-to-all-start.5
  14.9 13.1 all-to-all-start.4
  58.2 19.6 all-to-all-start
  77.9 10.0 all-to-all-start.1
  91.9 10.0 all-to-all-start.2
  101.8 11.8 all-to-all-start.3
  203.8 18.4 all-to-all-start
  218.8 107.0 %copy-start = (f32[8,32,1024]{2,1,0:T(8,128)}, f32[8,32,1024]{2,1,0:T(8,128)S(1)}, u32[]{:S(2)}) copy-start(f32[8,32,1024]{2,1,0:T(8,128)S(1)} %convolution_dynamic-update-slice_fusion.23) | copy-start | bytes 3145732 | tf_op jit(solution)/shard_map/while
  222.2 10.0 all-to-all-start.1
  236.2 10.0 all-to-all-start.2
  246.2 12.1 all-to-all-start.3
  348.4 18.4 all-to-all-start
  363.4 107.0 %copy-start = (f32[8,32,1024]{2,1,0:T(8,128)}, f32[8,32,1024]{2,1,0:T(8,128)S(1)}, u32[]{:S(2)}) copy-start(f32[8,32,1024]{2,1,0:T(8,128)S(1)} %convolution_dynamic-update-slice_fusion.23) | copy-start | bytes 3145732 | tf_op jit(solution)/shard_map/while
  366.8 10.0 all-to-all-start.1
  380.8 10.0 all-to-all-start.2
  390.8 12.1 all-to-all-start.3
  493.1 18.4 all-to-all-start
  508.0 107.0 %copy-start = (f32[8,32,1024]{2,1,0:T(8,128)}, f32[8,32,1024]{2,1,0:T(8,128)S(1)}, u32[]{:S(2)}) copy-start(f32[8,32,1024]{2,1,0:T(8,128)S(1)} %convolution_dynamic-update-slice_fusion.23) | copy-start | bytes 3145732 | tf_op jit(solution)/shard_map/while
  511.5 10.0 all-to-all-start.1
  525.5 10.0 all-to-all-start.2
  535.4 12.1 all-to-all-start.3
  637.7 18.4 all-to-all-start
  652.7 107.0 %copy-start = (f32[8,32,1024]{2,1,0:T(8,128)}, f32[8,32,1024]{2,1,0:T(8,128)S(1)}, u32[]{:S(2)}) copy-start(f32[8,32,1024]{2,1,0:T(8,128)S(1)} %convolution_dynamic-update-slice_fusion.23) | copy-start | bytes 3145732 | tf_op jit(solution)/shard_map/while
  656.1 10.0 all-to-all-start.1
  670.1 10.0 all-to-all-start.2
  680.1 12.1 all-to-all-start.3
  782.3 18.4 all-to-all-start
  797.3 107.0 %copy-start = (f32[8,32,1024]{2,1,0:T(8,128)}, f32[8,32,1024]{2,1,0:T(8,128)S(1)}, u32[]{:S(2)}) copy-start(f32[8,32,1024]{2,1,0:T(8,128)S(1)} %convolution_dynamic-update-slice_fusion.23) | copy-start | bytes 3145732 | tf_op jit(solution)/shard_map/while
  800.8 10.0 all-to-all-start.1
  814.8 10.0 all-to-all-start.2
  824.7 12.1 all-to-all-start.3
  927.0 18.4 all-to-all-start
  942.0 107.0 %copy-start = (f32[8,32,1024]{2,1,0:T(8,128)}, f32[8,32,1024]{2,1,0:T(8,128)S(1)}, u32[]{:S(2)}) copy-start(f32[8,32,1024]{2,1,0:T(8,128)S(1)} %convolution_dynamic-update-slice_fusion.23) | copy-start | bytes 3145732 | tf_op jit(solution)/shard_map/while
  945.4 10.0 all-to-all-start.1
  959.4 10.0 all-to-all-start.2
  969.4 12.1 all-to-all-start.3
  1071.6 18.4 all-to-all-start
  1090.0 10.0 all-to-all-start.1
  1104.0 10.0 all-to-all-start.2
  1114.0 12.1 all-to-all-start.3
  1216.3 18.4 all-to-all-start
  1234.7 10.0 all-to-all-start.1
  1248.7 10.0 all-to-all-start.2
  1258.6 12.1 all-to-all-start.3
  1360.9 18.4 all-to-all-start
  1379.3 10.0 all-to-all-start.1
  1393.3 10.0 all-to-all-start.2
  1403.3 12.1 all-to-all-start.3
  1505.5 18.4 all-to-all-start
  1523.9 10.0 all-to-all-start.1
  1537.9 10.0 all-to-all-start.2
  1547.9 12.1 all-to-all-start.3
  1650.2 18.4 all-to-all-start
  1668.6 10.0 all-to-all-start.1
  1682.6 10.0 all-to-all-start.2
  1692.5 12.1 all-to-all-start.3
  1794.8 18.4 all-to-all-start
  1813.2 10.0 all-to-all-start.1
  1827.2 10.0 all-to-all-start.2
  1837.2 12.1 all-to-all-start.3
  1939.4 18.4 all-to-all-start
  1957.8 10.0 all-to-all-start.1
  1971.8 10.0 all-to-all-start.2
  1981.8 12.1 all-to-all-start.3
  (36 other events, 1625.7 us)
where the time goes:
time: 2080 us; the launch traced here: 2060 us
  blocking collectives  878 us (42%)
  matrix products  466 us (22%)
  starting transfers between devices  274 us (13%)
  waiting for transfers between devices  214 us (10%)
  other arithmetic  130 us (6%)
  local copies, waits for them, and re-layouts  89.8 us (4%)
    psum x14, blocking collectives, iterate(): partial_value = lax.psum(partial_value, ('region', 'dev'))  878 us
    dot_general x112, matrix products, apply_inverse(): jnp.einsum('ask,aik->asi', rounded[:, :, :finish], factor[:, index_row *...  202 us
    dot_general x112, matrix products, apply_inverse(): jnp.einsum('asi,aik->ask', scaled[:, :, begin:], factor[:, begin:, begin:...  179 us
    all_to_all x14, starting transfers between devices, iterate(): lax.all_to_all(z_list[far_start:], 'region', split_axis=0, concat_axis=0,...  103 us
    dot_general x70, matrix products, select(): jnp.dot(selector, values, precision=HIGH, preferred_element_type=jnp.floa...  84.9 us
    all_to_all x14, waiting for transfers between devices, iterate(): lax.all_to_all(select(pick_near, values), 'dev', split_axis=0, concat_axi...  79.8 us
    all_to_all x14, waiting for transfers between devices, iterate(): lax.all_to_all(z_list[:far_start], 'dev', split_axis=0, concat_axis=0, ti...  63.2 us
    all_to_all x14, waiting for transfers between devices, iterate(): lax.all_to_all(z_list[far_start:], 'region', split_axis=0, concat_axis=0,...  62 us
  transfers between devices with their start and end apart: 58, of which 44 were waited for; matrix products, arithmetic and copies ran while one was open for 11% of the time, Pallas kernels for 0%

commit v1 on v0

v1 whole, which is shorter than its diff:
```python
import jax
import jax.numpy as jnp
from jax import lax
from jax.experimental import pallas as pl
from jax.experimental.pallas import tpu as pltpu
from jax.sharding import PartitionSpec as P

K = 1024
S = 32
AREA = 8
NB = 16
ITEMS = AREA * NB
ROWS = 4
EDGE = NB * ROWS
CAP = 8
N_REGION = 8
N_DEV = 16
WORLD = N_REGION * N_DEV
BUS_DEV = 16
ITERS = 14
RHO = 4.0
SIGMA = 1.0
CELLS = 1024.0 * 128.0
BOTH = ("region", "dev")
F32 = jnp.float32
BF16 = jnp.bfloat16
VMEM_LIMIT = 56 * 1024 * 1024


def dot(left, right):
    return jnp.dot(left, right, preferred_element_type=F32)


def split3(x):
    high = x.astype(BF16)
    rest = x - high.astype(F32)
    middle = rest.astype(BF16)
    low = (rest - middle.astype(F32)).astype(BF16)
    return high, middle, low


def pick(x, onehot):
    count = x.shape[0]
    got = dot(jnp.concatenate(split3(x), axis=0), onehot)
    return got[:count] + got[count : 2 * count] + got[2 * count :]


def iota(shape, dim):
    return lax.broadcasted_iota(jnp.int32, shape, dim)


def edge_perm(area):
    row = iota((128, ROWS * ITEMS), 0)
    col = iota((128, ROWS * ITEMS), 1)
    target = (row & 3) * ITEMS + area * NB + (row >> 2)
    return jnp.where((row < EDGE) & (col == target), 1.0, 0.0).astype(BF16)


def edge_perm_t(area):
    row = iota((ROWS * ITEMS, 128), 0)
    col = iota((ROWS * ITEMS, 128), 1)
    target = (col & 3) * ITEMS + area * NB + (col >> 2)
    return jnp.where((col < EDGE) & (row == target), 1.0, 0.0).astype(BF16)


def call(kernel, out_shape, **kw):
    params = dict(vmem_limit_bytes=kw.pop("limit", VMEM_LIMIT))
    return pl.pallas_call(
        kernel,
        out_shape=out_shape,
        compiler_params=pltpu.CompilerParams(**params),
        **kw,
    )


def struct(shape, dtype=F32):
    return jax.ShapeDtypeStruct(shape, dtype)


def route_kernel(me_ref, ids_col, ids_row, live_col, live_row, p_ref, pt_ref, tag_ref):
    me = me_ref[0]

    def key_of(ids, live):
        region = ids >> 8
        peer = (ids >> 4) & 15
        return jnp.where(live > 0, jnp.where(region == me, peer, 16 + region), -1)

    key_c = key_of(ids_col[...], live_col[...])
    key_r = key_of(ids_row[...], live_row[...])
    same = (key_c == key_r) & (key_r >= 0)
    sub = iota((ITEMS, ITEMS), 0)
    lane = iota((ITEMS, ITEMS), 1)
    rank_c = jnp.sum(jnp.where(same & (lane < sub), 1.0, 0.0), axis=1, keepdims=True)
    rank_r = jnp.sum(jnp.where(same & (sub < lane), 1.0, 0.0), axis=0, keepdims=True)

    def place(key, rank):
        rank = rank.astype(jnp.int32)
        far = ITEMS + rank * N_REGION + key - 16
        return jnp.where(key < 0, -1, jnp.where(key < 16, rank * N_DEV + key, far))

    hit = iota((ITEMS, 256), 1) == place(key_c, rank_c)
    p_ref[...] = jnp.where(hit, 1.0, 0.0).astype(BF16)
    hit_t = iota((256, ITEMS), 0) == place(key_r, rank_r)
    pt_ref[...] = jnp.where(hit_t, 1.0, 0.0).astype(BF16)
    local = ((ids_col[...] & 15) + 1).astype(F32)
    tag = jnp.sum(jnp.where(hit, local, 0.0), axis=0, keepdims=True) - 1.0
    odd = iota((256, ITEMS), 0) & 1
    tag_ref[...] = jnp.where(odd == 0, tag[:, :ITEMS], tag[:, ITEMS:]).astype(jnp.int32)


def near_tile(ref, dev):
    return ref[pl.ds(2 * dev, N_REGION, stride=2 * N_DEV), :]


def far_tile(ref, region):
    return ref[pl.ds(2 * N_DEV * region + 1, N_DEV, stride=2), :]


def bus_sums(near, far, near_tags, far_tags):
    group = iota((N_REGION, 128), 1) >> 4
    halves = []
    far_sums = []
    for half in range(2):
        total = jnp.zeros((N_REGION, 128), F32)
        for low in range(8):
            bus = 8 * half + low
            acc = jnp.zeros((N_REGION, 128), F32)
            for dev in range(N_DEV):
                acc = acc + jnp.where(near_tags[dev] == bus, near[dev], 0.0)
            for shift in (16, 32, 64):
                acc = acc + pltpu.roll(acc, shift, 1)
            total = jnp.where(group == low, acc, total)
        halves.append(total)
        rows = []
        for low in range(8):
            bus = 8 * half + low
            acc = jnp.zeros((N_DEV, 128), F32)
            for region in range(N_REGION):
                acc = acc + jnp.where(far_tags[region] == bus, far[region], 0.0)
            rows.append(acc)
        turned = jnp.transpose(jnp.concatenate(rows, axis=0))
        total = turned[:8]
        for c in range(1, CAP):
            total = total + turned[8 * c : 8 * c + 8]
        far_sums.append(total)
    return jnp.concatenate([halves[0] + far_sums[0], halves[1] + far_sums[1]], axis=1)


def count_kernel(tag_ref, inv_ref):
    near_tags = [near_tile(tag_ref, d) for d in range(N_DEV)]
    far_tags = [far_tile(tag_ref, r) for r in range(N_REGION)]
    one_n = jnp.ones((N_REGION, 128), F32)
    one_f = jnp.ones((N_DEV, 128), F32)
    counts = bus_sums([one_n] * N_DEV, [one_f] * N_REGION, near_tags, far_tags)
    inv_ref[...] = 1.0 / jnp.maximum(counts, 1.0)


def owner_kernel(step_ref, got_ref, tag_ref, inv_ref, prev_ref, rec_in, out_ref, z_ref, rec_ref):
    near_tags = [near_tile(tag_ref, d) for d in range(N_DEV)]
    far_tags = [far_tile(tag_ref, r) for r in range(N_REGION)]
    near = [near_tile(got_ref, d) for d in range(N_DEV)]
    far = [far_tile(got_ref, r) for r in range(N_REGION)]
    z = bus_sums(near, far, near_tags, far_tags) * inv_ref[...]
    change = z - prev_ref[...]
    change = change * change
    row = jnp.sum(change[:, :128] + change[:, 128:], axis=0, keepdims=True)
    rec_ref[...] = rec_in[...]
    rec_ref[pl.ds(step_ref[0], 1), :] = row * (RHO * RHO / CELLS)
    z_ref[...] = z
    group = iota((N_REGION, 128), 1) >> 4
    spread = []
    turned = []
    for half in range(2):
        part = z[:, 128 * half : 128 * half + 128]
        for low in range(8):
            one = jnp.where(group == low, part, 0.0)
            for shift in (16, 32, 64):
                one = one + pltpu.roll(one, shift, 1)
            spread.append(one)
        turned.append(jnp.transpose(jnp.concatenate([part] * 16, axis=0)))
    for dev in range(N_DEV):
        tag = near_tags[dev]
        val = jnp.zeros((N_REGION, 128), F32)
        for bus in range(BUS_DEV):
            val = jnp.where(tag == bus, spread[bus], val)
        out_ref[pl.ds(2 * dev, N_REGION, stride=2 * N_DEV), :] = val
    for region in range(N_REGION):
        tag = far_tags[region]
        val = jnp.zeros((N_DEV, 128), F32)
        for bus in range(BUS_DEV):
            low = bus % 8
            val = jnp.where(tag == bus, turned[bus // 8][16 * low : 16 * low + 16], val)
        out_ref[pl.ds(2 * N_DEV * region + 1, N_DEV, stride=2), :] = val


def slot_kernel(
    step_ref, z_ref, p_ref, pt_ref, live_ref, blk_in, u_in, c_ref, bdh_ref, bdl_ref, rec_in,
    send_ref, e_ref, blk_ref, u_ref, rec_ref,
):
    z_got = jnp.concatenate(
        [z_ref[pl.ds(0, WORLD, stride=2), :], z_ref[pl.ds(1, WORLD, stride=2), :]], axis=1
    )
    z_slot = pick(z_got, pt_ref[...])
    gap = (blk_in[...] - z_slot) * live_ref[...]
    u = u_in[...] + gap
    u_ref[...] = u
    rec_ref[...] = rec_in[...]
    rec_ref[pl.ds(step_ref[0], 1), :] = jnp.sum(gap * gap, axis=0, keepdims=True) * (1.0 / CELLS)
    push = RHO * (z_slot - u)
    e = jnp.concatenate([push[S * r : S * r + S] for r in range(ROWS)], axis=1)
    e_ref[...] = e
    e_high = e.astype(BF16)
    e_low = (e - e_high.astype(F32)).astype(BF16)
    both = dot(jnp.concatenate([e_high, e_low], axis=0), bdh_ref[...])
    edge = c_ref[...] + both[:S] + both[S:] + dot(e_high, bdl_ref[...])
    blk = jnp.concatenate([edge[:, ITEMS * r : ITEMS * r + ITEMS] for r in range(ROWS)], axis=0)
    blk_ref[...] = blk
    send = pick(blk + u, p_ref[...])
    send_ref[pl.ds(0, WORLD, stride=2), :] = send[:, :128]
    send_ref[pl.ds(1, WORLD, stride=2), :] = send[:, 128:]


def edge_part(right_side, m_edge, diag_edge):
    return dot(right_side.astype(BF16), m_edge) + right_side[:, :128] * diag_edge


def setup_kernel(f_ref, p_ref, load_ref, m_ref, diag_ref, c_ref, bdh_ref, bdl_ref, acc, bd):
    area = pl.program_id(0)
    piv = p_ref[0]
    piv_col = jnp.transpose(jnp.broadcast_to(piv, (128, K)))
    step = 256
    for i in reversed(range(K // step)):
        w = (i + 1) * step
        rows = f_ref[0, i * step : w, :w]
        col = piv_col[i * step : w, :]
        scaled = jnp.concatenate(
            [
                (rows[:, 128 * q : 128 * q + 128].astype(F32) * col).astype(BF16)
                for q in range(w // 128)
            ],
            axis=1,
        )
        part = lax.dot_general(
            rows, scaled, (((0,), (0,)), ((), ())), preferred_element_type=F32
        )
        if w == K:
            acc[...] = part
        else:
            acc[:w, :w] = acc[:w, :w] + part
    eye = iota((step, step), 0) == iota((step, step), 1)
    fix = piv - piv.astype(BF16).astype(F32)
    diags = []
    for i in range(K // step):
        at = slice(i * step, (i + 1) * step)
        block = acc[at, at]
        diags.append(jnp.sum(jnp.where(eye, block, 0.0), axis=0, keepdims=True))
        acc[at, at] = jnp.where(eye, 0.0, block)
    diag = jnp.concatenate(diags, axis=1) + fix
    diag_ref[0] = diag
    m_ref[0] = acc[...].astype(BF16)
    edge_diag = diag[:, :128]
    perm = edge_perm(area)
    small_eye = iota((128, 128), 0) == iota((128, 128), 1)
    m_ee = jnp.where(small_eye, edge_diag, acc[:128, :128])
    spread = pick(m_ee, perm)
    block = dot(edge_perm_t(area), jnp.concatenate(split3(spread), axis=1))
    wide = ROWS * ITEMS
    block = block[:, :wide] + block[:, wide : 2 * wide] + block[:, 2 * wide :]
    c = pick(edge_part(load_ref[0], m_ref[0, :, :128], edge_diag), perm)

    @pl.when(area == 0)
    def _():
        bd[...] = block
        c_ref[...] = c

    @pl.when(area > 0)
    def _():
        bd[...] = bd[...] + block
        c_ref[...] = c_ref[...] + c

    @pl.when(area == AREA - 1)
    def _():
        full = bd[...]
        high = full.astype(BF16)
        bdh_ref[...] = high
        bdl_ref[...] = (full - high.astype(F32)).astype(BF16)


def area_kernel(
    m_ref, diag_ref, load_ref, lo_ref, hi_ref, e_ref, w_in, b_in, x_ref, w_ref, b_ref, c_ref, e_all
):
    area = pl.program_id(0)

    @pl.when(area == 0)
    def _():
        e3 = jnp.concatenate(split3(e_ref[...]), axis=0)
        for a in range(AREA):
            got = dot(e3, edge_perm_t(a))
            e_all[a] = got[:S] + got[S : 2 * S] + got[2 * S :]
        c_ref[...] = jnp.zeros_like(c_ref)

    base = b_in[0]
    right_side = jnp.concatenate([base[:, :128] + e_all[area], base[:, 128:]], axis=1)
    diag = diag_ref[0]
    x = dot(right_side.astype(BF16), m_ref[0]) + right_side * diag
    x_ref[0] = x
    moved = x + w_in[0]
    y = jnp.clip(moved, lo_ref[0], hi_ref[0])
    w = moved - y
    w_ref[0] = w
    b = load_ref[0] + SIGMA * (y - w)
    b_ref[0] = b
    c = edge_part(b, m_ref[0, :, :128], diag[:, :128])
    c_ref[...] = c_ref[...] + pick(c, edge_perm(area))


def area_block(rows):
    return pl.BlockSpec((1, rows, K), lambda a: (a, 0, 0))


def whole(shape):
    return pl.BlockSpec(shape, lambda a: (0,) * len(shape))


def cost(flops, nbytes):
    return pl.CostEstimate(flops=flops, bytes_accessed=nbytes, transcendentals=0)


SMEM = pl.BlockSpec(memory_space=pltpu.SMEM)
VM = pl.BlockSpec(memory_space=pltpu.VMEM)


def on_device(loads, factor, pivots, lower, upper, incidence, counts):
    wide = ROWS * ITEMS
    exchange = lambda x: lax.all_to_all(x, BOTH, split_axis=0, concat_axis=0, tiled=True)
    me = lax.axis_index("region").astype(jnp.int32).reshape(1)
    live = (jnp.arange(NB)[None, :] < counts[:, None]).astype(jnp.int32).reshape(1, ITEMS)
    ids = incidence.reshape(1, ITEMS)
    place, place_t, tags = call(
        route_kernel,
        (struct((ITEMS, 256), BF16), struct((256, ITEMS), BF16), struct((256, ITEMS), jnp.int32)),
        in_specs=[SMEM, VM, VM, VM, VM],
    )(me, ids.reshape(ITEMS, 1), ids, live.reshape(ITEMS, 1), live)
    live_row = live.astype(F32)
    tags = exchange(tags)

    matrix, diag, c_now, bd_high, bd_low = call(
        setup_kernel,
        (
            struct((AREA, K, K), BF16),
            struct((AREA, 1, K)),
            struct((S, wide)),
            struct((wide, wide), BF16),
            struct((wide, wide), BF16),
        ),
        grid=(AREA,),
        in_specs=[area_block(K), area_block(1), area_block(S)],
        out_specs=(
            area_block(K), area_block(1), whole((S, wide)), whole((wide, wide)), whole((wide, wide)),
        ),
        scratch_shapes=[pltpu.VMEM((K, K), F32), pltpu.VMEM((wide, wide), F32)],
        cost_estimate=cost(8 * 10**9, 34 * 2**20),
    )(factor, pivots.reshape(AREA, 1, K), loads)

    inverse = call(count_kernel, struct((N_REGION, 256)))(tags)
    floor_box = lower.reshape(AREA, 1, K)
    ceil_box = upper.reshape(AREA, 1, K)

    run_slots = call(
        slot_kernel,
        (
            struct((256, 128)),
            struct((S, wide)),
            struct((128, 128)),
            struct((128, 128)),
            struct((16, 128)),
        ),
        in_specs=[SMEM] + [VM] * 10,
        input_output_aliases={5: 2, 6: 3, 10: 4},
        cost_estimate=cost(10**8, 3 * 2**20),
        limit=16 * 2**20,
    )
    run_owner = call(
        owner_kernel,
        (struct((256, 128)), struct((N_REGION, 256)), struct((16, 128))),
        in_specs=[SMEM] + [VM] * 5,
        input_output_aliases={4: 1, 5: 2},
        cost_estimate=cost(10**7, 2**20),
        limit=16 * 2**20,
    )
    run_areas = call(
        area_kernel,
        (
            struct((AREA, S, K)), struct((AREA, S, K)), struct((AREA, S, K)), struct((S, wide)),
        ),
        grid=(AREA,),
        in_specs=[
            area_block(K), area_block(1), area_block(S), area_block(1), area_block(1),
            whole((S, wide)), area_block(S), area_block(S),
        ],
        out_specs=(area_block(S), area_block(S), area_block(S), whole((S, wide))),
        scratch_shapes=[pltpu.VMEM((AREA, S, 128), F32)],
        input_output_aliases={6: 1, 7: 2},
        cost_estimate=cost(6 * 10**8, 22 * 2**20),
        limit=24 * 2**20,
    )

    def slots(step, z_back, blk, u, c, rec):
        return run_slots(
            step.reshape(1), z_back, place, place_t, live_row, blk, u, c, bd_high, bd_low, rec
        )

    zero = jnp.zeros((128, 128), F32)
    rec = jnp.zeros((16, 128), F32)
    send, e, blk, u, prim = slots(
        jnp.int32(15), jnp.zeros((256, 128), F32), zero, zero, c_now, rec
    )

    def iterate(step, state):
        _, send, e, blk, u, prim, dual, z_prev, w, b = state
        got = exchange(send)
        x, w, b, c = run_areas(matrix, diag, loads, floor_box, ceil_box, e, w, b)
        step = step.astype(jnp.int32)
        back, z_prev, dual = run_owner(step.reshape(1), got, tags, inverse, z_prev, dual)
        z_back = exchange(back)
        send, e, blk, u, prim = slots(step, z_back, blk, u, c, prim)
        return (x, send, e, blk, u, prim, dual, z_prev, w, b)

    state = (
        jnp.zeros_like(loads), send, e, blk, u, prim, rec,
        jnp.zeros((N_REGION, 256), F32), jnp.zeros_like(loads), loads,
    )
    state = lax.fori_loop(0, ITERS, iterate, state)
    x, u, prim, dual = state[0], state[4], state[5], state[6]
    duals = jnp.transpose(u.reshape(ROWS, S, ITEMS), (2, 1, 0)).reshape(AREA, NB, 128)
    sums = jnp.concatenate(
        [jnp.sum(prim, axis=1)[:ITERS], jnp.sum(dual, axis=1)[:ITERS], jnp.zeros((100,), F32)]
    )
    shared = exchange(jnp.broadcast_to(sums[None, :], (WORLD, 128)))
    total = jnp.sum(shared, axis=0)
    record = jnp.stack([total[:ITERS], total[ITERS : 2 * ITERS]], axis=1)
    return (x, duals, record)


def solution(mesh):
    area_split = (
        P(BOTH, None, None),
        P(BOTH, None, None),
        P(BOTH, None),
        P(BOTH, None),
        P(BOTH, None),
        P(BOTH, None),
        P(BOTH),
    )
    return jax.shard_map(
        on_device,
        mesh=mesh,
        in_specs=area_split,
        out_specs=(P(BOTH, None, None), P(BOTH, None, None), P()),
        check_vma=False,
    )
```

time: 2080 us -> 644 us (0.31)
  blocking collectives: 878 us -> 0 us
  matrix products: 466 us -> 0 us
  Pallas kernels: 0 us -> 257 us
  other arithmetic: 130 us -> 3.5 us
  local copies, waits for them, and re-layouts: 89.8 us -> 12.7 us
  waiting for transfers between devices: 214 us -> 149 us
  starting transfers between devices: 274 us -> 216 us
    psum x14 -> x0, blocking collectives: 878 us -> none  [iterate(): partial_value = lax.psum(partial_value, ('region', 'dev'))]
    dot_general x294 -> x0, matrix products: 466 us -> none  [the longest x112 202 us: apply_inverse(): jnp.einsum('ask,aik->asi', rounded[:, :, :finish], factor[:, index_row *...]
    pallas_call x0 -> x46, Pallas kernels: none -> 257 us  [the longest x14 161 us: iterate(): x, w, b, c = run_areas(matrix, diag, loads, floor_box, ceil_box, e, w, b)]
    all_to_all x58 -> x30, waiting for transfers between devices: 214 us -> 149 us  [on_device(): lax.all_to_all(x, BOTH, split_axis=0, concat_axis=0, tiled=True)]
    all_to_all x58 -> x30, starting transfers between devices: 274 us -> 216 us  [on_device(): lax.all_to_all(x, BOTH, split_axis=0, concat_axis=0, tiled=True)]
    all_to_all x31 -> x0, local copies, waits for them, and re-layouts: 40.5 us -> none  [the longest x14 20.6 us: iterate(): lax.all_to_all(z_list[:far_start], 'dev', split_axis=0, concat_axis=0, ti...]
    another operation x43 -> x2, other arithmetic: 39.1 us -> 0.57 us  [the longest x1 0.57 us: on_device(): record = jnp.stack([total[:ITERS], total[ITERS:2 * ITERS]], axis=1)]
    convert_element_type x42 -> x30, other arithmetic: 37.9 us -> 1.9 us  [the longest x15 1.81 us: on_device(): (jnp.arange(NB)[None, :] < counts[:, None]).astype(jnp.int32)]
  transfers between devices with their start and end apart: 58 -> 30, of which waited for: 44 -> 15; matrix products, arithmetic and copies ran while one was open for 11% -> 1% of each run, Pallas kernels for 0% -> 29%
where the time goes in v1:
time: 644 us; the launch traced here: 640 us
  Pallas kernels  257 us (40%)
  starting transfers between devices  216 us (34%)
  waiting for transfers between devices  149 us (23%)
  local copies, waits for them, and re-layouts  12.7 us (2%)
    all_to_all x30, starting transfers between devices, on_device(): lax.all_to_all(x, BOTH, split_axis=0, concat_axis=0, tiled=True)  216 us
    pallas_call x14, Pallas kernels, iterate(): x, w, b, c = run_areas(matrix, diag, loads, floor_box, ceil_box, e, w, b)  161 us
    all_to_all x30, waiting for transfers between devices, on_device(): lax.all_to_all(x, BOTH, split_axis=0, concat_axis=0, tiled=True)  149 us
    pallas_call x15, Pallas kernels, slots(): run_slots(step.reshape(1), z_back, place, place_t, live_row, blk, u, c, b...  40.4 us
    pallas_call x14, Pallas kernels, iterate(): run_owner(step.reshape(1), got, tags, inverse, z_prev, dual)  30.1 us
    pallas_call x1, Pallas kernels, on_device(): call(setup_kernel, (struct((AREA, K, K), BF16), struct((AREA, 1, K)), str...  23 us
  transfers between devices with their start and end apart: 30, of which 15 were waited for; matrix products, arithmetic and copies ran while one was open for 1% of the time, Pallas kernels for 29%

profile of v1, /device:TPU:1, one launch (start us, length us, event | category | flops | bytes accessed | tf_op | source)
XLA Modules:
  0.0 639.8 jit_solution(9358524836627475896)
XLA Ops:
  8.7 11.5 %all-to-all-start.2 = ((s32[128,2,128]{2,1,0:T(2,128)}), s32[128,2,128]{2,1,0:T(2,128)S(1)}, u32[]{:S(2)}, u32[]{:S(2)}) async-start(s32[128,2,128]{2,1,0:T(2,128)} %bitcast.38), calls=%async_computation.2 | async-start | bytes 262144 | tf_op jit(solution)/shard_map/all_to_all | solution.py:335
  20.2 23.0 %shard_map.95 = (bf16[8,1024,1024]{2,1,0:T(8,128)(2,1)}, f32[8,1,1024]{2,1,0:T(1,128)}, f32[32,512]{1,0:T(8,128)}, bf16[512,512]{1,0:T(8,128)(2,1)S(1)}, bf16[512,512]{1,0:T(8,128)(2,1)S(1)}) custom-call(bf16[8,1024,1024]{2,1,0:T(8,128)(2,1)} %f_ref.1, f32[8,1,1024]{2,1,0:T(1,128)} %reshape.124.p_ref, f32[8,32,1024]{2,1,0:T(8,128)} %load_ref.1), custom_call_target="tpu_custom_call" | custom-call | flops 8000000000 | bytes 35651584 | tf_op jit(solution)/shard_map/pallas_call | solution.py:347
  51.0 567.1 %while.32 = (s32[]{:T(128)}, f32[8,32,1024]{2,1,0:T(8,128)}, f32[256,128]{1,0:T(8,128)}, f32[32,512]{1,0:T(8,128)}, f32[128,128]{1,0:T(8,128)}, /*index=5*/f32[1...) while((s32[]{:T(128)}, f32[8,32,1024]{2,1,0:T(8,128)}, ...), condition=%wide.region_1.0_spmd.clone, body=%wide.region_0.0_spmd.clone.sunk | while | flops 710000384 | bytes 28052284 | solution.py:433
  51.0 9.8 %all-to-all-start = ((f32[128,2,128]{2,1,0:T(2,128)}), f32[128,2,128]{2,1,0:T(2,128)S(1)}, u32[]{:S(2)}, u32[]{:S(2)}) async-start(f32[128,2,128]{2,1,0:T(2,128)} %bitcast.27), calls=%async_computation | async-start | bytes 262144 | tf_op jit(solution)/shard_map/while/body/eval_jaxpr/all_to_all | solution.py:335
  60.8 10.1 %all-to-all-done = f32[128,2,128]{2,1,0:T(2,128)S(1)} async-done(((f32[128,2,128]{2,1,0:T(2,128)}), f32[128,2,128]{2,1,0:T(2,128)S(1)}, u32[]{:S(2)}, u32[]{:S(2)}) %all-to-all-start) | async-done | bytes 131104 | tf_op jit(solution)/shard_map/while/body/eval_jaxpr/all_to_all | solution.py:335
  73.0 4.1 all-to-all-start.1
  77.3 11.5 %eval_jaxpr.15 = (f32[8,32,1024]{2,1,0:T(8,128)}, f32[8,32,1024]{2,1,0:T(8,128)S(1)}, f32[8,32,1024]{2,1,0:T(8,128)S(1)}, f32[32,512]{1,0:T(8,128)S(1)}) custom-call(bf16[8,1024,1024]{2,1,0:T(8,128)(2,1)} %get-tuple-element.716.m_ref, f32[8,1,1024]{2,1,0:T(1,128)} %get-tuple-element.717.diag_ref, ...), custom_call_target="tpu_custom_call", output_to_operand_aliasing={{1}: (6, {}), {2}: (7, {})} | custom-call | flops 600000000 | bytes 23068672 | tf_op jit(solution)/shard_map/while/body/eval_jaxpr/pallas_call | solution.py:422
  91.5 9.8 %all-to-all-start = ((f32[128,2,128]{2,1,0:T(2,128)}), f32[128,2,128]{2,1,0:T(2,128)S(1)}, u32[]{:S(2)}, u32[]{:S(2)}) async-start(f32[128,2,128]{2,1,0:T(2,128)} %bitcast.27), calls=%async_computation | async-start | bytes 262144 | tf_op jit(solution)/shard_map/while/body/eval_jaxpr/all_to_all | solution.py:335
  101.3 10.1 %all-to-all-done = f32[128,2,128]{2,1,0:T(2,128)S(1)} async-done(((f32[128,2,128]{2,1,0:T(2,128)}), f32[128,2,128]{2,1,0:T(2,128)S(1)}, u32[]{:S(2)}, u32[]{:S(2)}) %all-to-all-start) | async-done | bytes 131104 | tf_op jit(solution)/shard_map/while/body/eval_jaxpr/all_to_all | solution.py:335
  113.5 4.1 all-to-all-start.1
  117.8 11.5 %eval_jaxpr.15 = (f32[8,32,1024]{2,1,0:T(8,128)}, f32[8,32,1024]{2,1,0:T(8,128)S(1)}, f32[8,32,1024]{2,1,0:T(8,128)S(1)}, f32[32,512]{1,0:T(8,128)S(1)}) custom-call(bf16[8,1024,1024]{2,1,0:T(8,128)(2,1)} %get-tuple-element.716.m_ref, f32[8,1,1024]{2,1,0:T(1,128)} %get-tuple-element.717.diag_ref, ...), custom_call_target="tpu_custom_call", output_to_operand_aliasing={{1}: (6, {}), {2}: (7, {})} | custom-call | flops 600000000 | bytes 23068672 | tf_op jit(solution)/shard_map/while/body/eval_jaxpr/pallas_call | solution.py:422
  129.3 2.7 eval_jaxpr.17
  132.0 9.8 %all-to-all-start = ((f32[128,2,128]{2,1,0:T(2,128)}), f32[128,2,128]{2,1,0:T(2,128)S(1)}, u32[]{:S(2)}, u32[]{:S(2)}) async-start(f32[128,2,128]{2,1,0:T(2,128)} %bitcast.27), calls=%async_computation | async-start | bytes 262144 | tf_op jit(solution)/shard_map/while/body/eval_jaxpr/all_to_all | solution.py:335
  141.8 10.1 %all-to-all-done = f32[128,2,128]{2,1,0:T(2,128)S(1)} async-done(((f32[128,2,128]{2,1,0:T(2,128)}), f32[128,2,128]{2,1,0:T(2,128)S(1)}, u32[]{:S(2)}, u32[]{:S(2)}) %all-to-all-start) | async-done | bytes 131104 | tf_op jit(solution)/shard_map/while/body/eval_jaxpr/all_to_all | solution.py:335
  154.0 4.1 all-to-all-start.1
  158.3 11.5 %eval_jaxpr.15 = (f32[8,32,1024]{2,1,0:T(8,128)}, f32[8,32,1024]{2,1,0:T(8,128)S(1)}, f32[8,32,1024]{2,1,0:T(8,128)S(1)}, f32[32,512]{1,0:T(8,128)S(1)}) custom-call(bf16[8,1024,1024]{2,1,0:T(8,128)(2,1)} %get-tuple-element.716.m_ref, f32[8,1,1024]{2,1,0:T(1,128)} %get-tuple-element.717.diag_ref, ...), custom_call_target="tpu_custom_call", output_to_operand_aliasing={{1}: (6, {}), {2}: (7, {})} | custom-call | flops 600000000 | bytes 23068672 | tf_op jit(solution)/shard_map/while/body/eval_jaxpr/pallas_call | solution.py:422
  169.8 2.7 eval_jaxpr.17
  172.5 9.8 %all-to-all-start = ((f32[128,2,128]{2,1,0:T(2,128)}), f32[128,2,128]{2,1,0:T(2,128)S(1)}, u32[]{:S(2)}, u32[]{:S(2)}) async-start(f32[128,2,128]{2,1,0:T(2,128)} %bitcast.27), calls=%async_computation | async-start | bytes 262144 | tf_op jit(solution)/shard_map/while/body/eval_jaxpr/all_to_all | solution.py:335
  182.3 10.1 %all-to-all-done = f32[128,2,128]{2,1,0:T(2,128)S(1)} async-done(((f32[128,2,128]{2,1,0:T(2,128)}), f32[128,2,128]{2,1,0:T(2,128)S(1)}, u32[]{:S(2)}, u32[]{:S(2)}) %all-to-all-start) | async-done | bytes 131104 | tf_op jit(solution)/shard_map/while/body/eval_jaxpr/all_to_all | solution.py:335
  194.5 4.1 all-to-all-start.1
  198.8 11.5 %eval_jaxpr.15 = (f32[8,32,1024]{2,1,0:T(8,128)}, f32[8,32,1024]{2,1,0:T(8,128)S(1)}, f32[8,32,1024]{2,1,0:T(8,128)S(1)}, f32[32,512]{1,0:T(8,128)S(1)}) custom-call(bf16[8,1024,1024]{2,1,0:T(8,128)(2,1)} %get-tuple-element.716.m_ref, f32[8,1,1024]{2,1,0:T(1,128)} %get-tuple-element.717.diag_ref, ...), custom_call_target="tpu_custom_call", output_to_operand_aliasing={{1}: (6, {}), {2}: (7, {})} | custom-call | flops 600000000 | bytes 23068672 | tf_op jit(solution)/shard_map/while/body/eval_jaxpr/pallas_call | solution.py:422
  213.0 9.8 %all-to-all-start = ((f32[128,2,128]{2,1,0:T(2,128)}), f32[128,2,128]{2,1,0:T(2,128)S(1)}, u32[]{:S(2)}, u32[]{:S(2)}) async-start(f32[128,2,128]{2,1,0:T(2,128)} %bitcast.27), calls=%async_computation | async-start | bytes 262144 | tf_op jit(solution)/shard_map/while/body/eval_jaxpr/all_to_all | solution.py:335
  222.8 10.1 %all-to-all-done = f32[128,2,128]{2,1,0:T(2,128)S(1)} async-done(((f32[128,2,128]{2,1,0:T(2,128)}), f32[128,2,128]{2,1,0:T(2,128)S(1)}, u32[]{:S(2)}, u32[]{:S(2)}) %all-to-all-start) | async-done | bytes 131104 | tf_op jit(solution)/shard_map/while/body/eval_jaxpr/all_to_all | solution.py:335
  235.0 4.1 all-to-all-start.1
  239.3 11.5 %eval_jaxpr.15 = (f32[8,32,1024]{2,1,0:T(8,128)}, f32[8,32,1024]{2,1,0:T(8,128)S(1)}, f32[8,32,1024]{2,1,0:T(8,128)S(1)}, f32[32,512]{1,0:T(8,128)S(1)}) custom-call(bf16[8,1024,1024]{2,1,0:T(8,128)(2,1)} %get-tuple-element.716.m_ref, f32[8,1,1024]{2,1,0:T(1,128)} %get-tuple-element.717.diag_ref, ...), custom_call_target="tpu_custom_call", output_to_operand_aliasing={{1}: (6, {}), {2}: (7, {})} | custom-call | flops 600000000 | bytes 23068672 | tf_op jit(solution)/shard_map/while/body/eval_jaxpr/pallas_call | solution.py:422
  250.8 2.7 eval_jaxpr.17
  253.5 9.8 %all-to-all-start = ((f32[128,2,128]{2,1,0:T(2,128)}), f32[128,2,128]{2,1,0:T(2,128)S(1)}, u32[]{:S(2)}, u32[]{:S(2)}) async-start(f32[128,2,128]{2,1,0:T(2,128)} %bitcast.27), calls=%async_computation | async-start | bytes 262144 | tf_op jit(solution)/shard_map/while/body/eval_jaxpr/all_to_all | solution.py:335
  263.3 10.1 %all-to-all-done = f32[128,2,128]{2,1,0:T(2,128)S(1)} async-done(((f32[128,2,128]{2,1,0:T(2,128)}), f32[128,2,128]{2,1,0:T(2,128)S(1)}, u32[]{:S(2)}, u32[]{:S(2)}) %all-to-all-start) | async-done | bytes 131104 | tf_op jit(solution)/shard_map/while/body/eval_jaxpr/all_to_all | solution.py:335
  275.5 4.1 all-to-all-start.1
  279.8 11.5 %eval_jaxpr.15 = (f32[8,32,1024]{2,1,0:T(8,128)}, f32[8,32,1024]{2,1,0:T(8,128)S(1)}, f32[8,32,1024]{2,1,0:T(8,128)S(1)}, f32[32,512]{1,0:T(8,128)S(1)}) custom-call(bf16[8,1024,1024]{2,1,0:T(8,128)(2,1)} %get-tuple-element.716.m_ref, f32[8,1,1024]{2,1,0:T(1,128)} %get-tuple-element.717.diag_ref, ...), custom_call_target="tpu_custom_call", output_to_operand_aliasing={{1}: (6, {}), {2}: (7, {})} | custom-call | flops 600000000 | bytes 23068672 | tf_op jit(solution)/shard_map/while/body/eval_jaxpr/pallas_call | solution.py:422
  294.0 9.8 %all-to-all-start = ((f32[128,2,128]{2,1,0:T(2,128)}), f32[128,2,128]{2,1,0:T(2,128)S(1)}, u32[]{:S(2)}, u32[]{:S(2)}) async-start(f32[128,2,128]{2,1,0:T(2,128)} %bitcast.27), calls=%async_computation | async-start | bytes 262144 | tf_op jit(solution)/shard_map/while/body/eval_jaxpr/all_to_all | solution.py:335
  303.8 10.1 %all-to-all-done = f32[128,2,128]{2,1,0:T(2,128)S(1)} async-done(((f32[128,2,128]{2,1,0:T(2,128)}), f32[128,2,128]{2,1,0:T(2,128)S(1)}, u32[]{:S(2)}, u32[]{:S(2)}) %all-to-all-start) | async-done | bytes 131104 | tf_op jit(solution)/shard_map/while/body/eval_jaxpr/all_to_all | solution.py:335
  316.0 4.1 all-to-all-start.1
  320.3 11.5 %eval_jaxpr.15 = (f32[8,32,1024]{2,1,0:T(8,128)}, f32[8,32,1024]{2,1,0:T(8,128)S(1)}, f32[8,32,1024]{2,1,0:T(8,128)S(1)}, f32[32,512]{1,0:T(8,128)S(1)}) custom-call(bf16[8,1024,1024]{2,1,0:T(8,128)(2,1)} %get-tuple-element.716.m_ref, f32[8,1,1024]{2,1,0:T(1,128)} %get-tuple-element.717.diag_ref, ...), custom_call_target="tpu_custom_call", output_to_operand_aliasing={{1}: (6, {}), {2}: (7, {})} | custom-call | flops 600000000 | bytes 23068672 | tf_op jit(solution)/shard_map/while/body/eval_jaxpr/pallas_call | solution.py:422
  334.6 9.8 %all-to-all-start = ((f32[128,2,128]{2,1,0:T(2,128)}), f32[128,2,128]{2,1,0:T(2,128)S(1)}, u32[]{:S(2)}, u32[]{:S(2)}) async-start(f32[128,2,128]{2,1,0:T(2,128)} %bitcast.27), calls=%async_computation | async-start | bytes 262144 | tf_op jit(solution)/shard_map/while/body/eval_jaxpr/all_to_all | solution.py:335
  344.3 10.1 %all-to-all-done = f32[128,2,128]{2,1,0:T(2,128)S(1)} async-done(((f32[128,2,128]{2,1,0:T(2,128)}), f32[128,2,128]{2,1,0:T(2,128)S(1)}, u32[]{:S(2)}, u32[]{:S(2)}) %all-to-all-start) | async-done | bytes 131104 | tf_op jit(solution)/shard_map/while/body/eval_jaxpr/all_to_all | solution.py:335
  356.6 4.1 all-to-all-start.1
  360.8 11.5 %eval_jaxpr.15 = (f32[8,32,1024]{2,1,0:T(8,128)}, f32[8,32,1024]{2,1,0:T(8,128)S(1)}, f32[8,32,1024]{2,1,0:T(8,128)S(1)}, f32[32,512]{1,0:T(8,128)S(1)}) custom-call(bf16[8,1024,1024]{2,1,0:T(8,128)(2,1)} %get-tuple-element.716.m_ref, f32[8,1,1024]{2,1,0:T(1,128)} %get-tuple-element.717.diag_ref, ...), custom_call_target="tpu_custom_call", output_to_operand_aliasing={{1}: (6, {}), {2}: (7, {})} | custom-call | flops 600000000 | bytes 23068672 | tf_op jit(solution)/shard_map/while/body/eval_jaxpr/pallas_call | solution.py:422
  375.1 9.8 %all-to-all-start = ((f32[128,2,128]{2,1,0:T(2,128)}), f32[128,2,128]{2,1,0:T(2,128)S(1)}, u32[]{:S(2)}, u32[]{:S(2)}) async-start(f32[128,2,128]{2,1,0:T(2,128)} %bitcast.27), calls=%async_computation | async-start | bytes 262144 | tf_op jit(solution)/shard_map/while/body/eval_jaxpr/all_to_all | solution.py:335
  384.9 10.1 %all-to-all-done = f32[128,2,128]{2,1,0:T(2,128)S(1)} async-done(((f32[128,2,128]{2,1,0:T(2,128)}), f32[128,2,128]{2,1,0:T(2,128)S(1)}, u32[]{:S(2)}, u32[]{:S(2)}) %all-to-all-start) | async-done | bytes 131104 | tf_op jit(solution)/shard_map/while/body/eval_jaxpr/all_to_all | solution.py:335
  397.1 4.1 all-to-all-start.1
  401.4 11.5 %eval_jaxpr.15 = (f32[8,32,1024]{2,1,0:T(8,128)}, f32[8,32,1024]{2,1,0:T(8,128)S(1)}, f32[8,32,1024]{2,1,0:T(8,128)S(1)}, f32[32,512]{1,0:T(8,128)S(1)}) custom-call(bf16[8,1024,1024]{2,1,0:T(8,128)(2,1)} %get-tuple-element.716.m_ref, f32[8,1,1024]{2,1,0:T(1,128)} %get-tuple-element.717.diag_ref, ...), custom_call_target="tpu_custom_call", output_to_operand_aliasing={{1}: (6, {}), {2}: (7, {})} | custom-call | flops 600000000 | bytes 23068672 | tf_op jit(solution)/shard_map/while/body/eval_jaxpr/pallas_call | solution.py:422
  415.6 9.8 %all-to-all-start = ((f32[128,2,128]{2,1,0:T(2,128)}), f32[128,2,128]{2,1,0:T(2,128)S(1)}, u32[]{:S(2)}, u32[]{:S(2)}) async-start(f32[128,2,128]{2,1,0:T(2,128)} %bitcast.27), calls=%async_computation | async-start | bytes 262144 | tf_op jit(solution)/shard_map/while/body/eval_jaxpr/all_to_all | solution.py:335
  425.4 10.1 %all-to-all-done = f32[128,2,128]{2,1,0:T(2,128)S(1)} async-done(((f32[128,2,128]{2,1,0:T(2,128)}), f32[128,2,128]{2,1,0:T(2,128)S(1)}, u32[]{:S(2)}, u32[]{:S(2)}) %all-to-all-start) | async-done | bytes 131104 | tf_op jit(solution)/shard_map/while/body/eval_jaxpr/all_to_all | solution.py:335
  437.6 4.1 all-to-all-start.1
  441.9 11.5 %eval_jaxpr.15 = (f32[8,32,1024]{2,1,0:T(8,128)}, f32[8,32,1024]{2,1,0:T(8,128)S(1)}, f32[8,32,1024]{2,1,0:T(8,128)S(1)}, f32[32,512]{1,0:T(8,128)S(1)}) custom-call(bf16[8,1024,1024]{2,1,0:T(8,128)(2,1)} %get-tuple-element.716.m_ref, f32[8,1,1024]{2,1,0:T(1,128)} %get-tuple-element.717.diag_ref, ...), custom_call_target="tpu_custom_call", output_to_operand_aliasing={{1}: (6, {}), {2}: (7, {})} | custom-call | flops 600000000 | bytes 23068672 | tf_op jit(solution)/shard_map/while/body/eval_jaxpr/pallas_call | solution.py:422
  456.1 9.8 %all-to-all-start = ((f32[128,2,128]{2,1,0:T(2,128)}), f32[128,2,128]{2,1,0:T(2,128)S(1)}, u32[]{:S(2)}, u32[]{:S(2)}) async-start(f32[128,2,128]{2,1,0:T(2,128)} %bitcast.27), calls=%async_computation | async-start | bytes 262144 | tf_op jit(solution)/shard_map/while/body/eval_jaxpr/all_to_all | solution.py:335
  465.9 10.1 %all-to-all-done = f32[128,2,128]{2,1,0:T(2,128)S(1)} async-done(((f32[128,2,128]{2,1,0:T(2,128)}), f32[128,2,128]{2,1,0:T(2,128)S(1)}, u32[]{:S(2)}, u32[]{:S(2)}) %all-to-all-start) | async-done | bytes 131104 | tf_op jit(solution)/shard_map/while/body/eval_jaxpr/all_to_all | solution.py:335
  478.1 4.1 all-to-all-start.1
  482.4 11.5 %eval_jaxpr.15 = (f32[8,32,1024]{2,1,0:T(8,128)}, f32[8,32,1024]{2,1,0:T(8,128)S(1)}, f32[8,32,1024]{2,1,0:T(8,128)S(1)}, f32[32,512]{1,0:T(8,128)S(1)}) custom-call(bf16[8,1024,1024]{2,1,0:T(8,128)(2,1)} %get-tuple-element.716.m_ref, f32[8,1,1024]{2,1,0:T(1,128)} %get-tuple-element.717.diag_ref, ...), custom_call_target="tpu_custom_call", output_to_operand_aliasing={{1}: (6, {}), {2}: (7, {})} | custom-call | flops 600000000 | bytes 23068672 | tf_op jit(solution)/shard_map/while/body/eval_jaxpr/pallas_call | solution.py:422
  496.6 9.8 %all-to-all-start = ((f32[128,2,128]{2,1,0:T(2,128)}), f32[128,2,128]{2,1,0:T(2,128)S(1)}, u32[]{:S(2)}, u32[]{:S(2)}) async-start(f32[128,2,128]{2,1,0:T(2,128)} %bitcast.27), calls=%async_computation | async-start | bytes 262144 | tf_op jit(solution)/shard_map/while/body/eval_jaxpr/all_to_all | solution.py:335
  506.4 10.1 %all-to-all-done = f32[128,2,128]{2,1,0:T(2,128)S(1)} async-done(((f32[128,2,128]{2,1,0:T(2,128)}), f32[128,2,128]{2,1,0:T(2,128)S(1)}, u32[]{:S(2)}, u32[]{:S(2)}) %all-to-all-start) | async-done | bytes 131104 | tf_op jit(solution)/shard_map/while/body/eval_jaxpr/all_to_all | solution.py:335
  518.6 4.1 all-to-all-start.1
  522.9 11.5 %eval_jaxpr.15 = (f32[8,32,1024]{2,1,0:T(8,128)}, f32[8,32,1024]{2,1,0:T(8,128)S(1)}, f32[8,32,1024]{2,1,0:T(8,128)S(1)}, f32[32,512]{1,0:T(8,128)S(1)}) custom-call(bf16[8,1024,1024]{2,1,0:T(8,128)(2,1)} %get-tuple-element.716.m_ref, f32[8,1,1024]{2,1,0:T(1,128)} %get-tuple-element.717.diag_ref, ...), custom_call_target="tpu_custom_call", output_to_operand_aliasing={{1}: (6, {}), {2}: (7, {})} | custom-call | flops 600000000 | bytes 23068672 | tf_op jit(solution)/shard_map/while/body/eval_jaxpr/pallas_call | solution.py:422
  537.1 9.8 %all-to-all-start = ((f32[128,2,128]{2,1,0:T(2,128)}), f32[128,2,128]{2,1,0:T(2,128)S(1)}, u32[]{:S(2)}, u32[]{:S(2)}) async-start(f32[128,2,128]{2,1,0:T(2,128)} %bitcast.27), calls=%async_computation | async-start | bytes 262144 | tf_op jit(solution)/shard_map/while/body/eval_jaxpr/all_to_all | solution.py:335
  546.9 10.1 %all-to-all-done = f32[128,2,128]{2,1,0:T(2,128)S(1)} async-done(((f32[128,2,128]{2,1,0:T(2,128)}), f32[128,2,128]{2,1,0:T(2,128)S(1)}, u32[]{:S(2)}, u32[]{:S(2)}) %all-to-all-start) | async-done | bytes 131104 | tf_op jit(solution)/shard_map/while/body/eval_jaxpr/all_to_all | solution.py:335
  559.1 4.1 all-to-all-start.1
  563.4 11.5 %eval_jaxpr.15 = (f32[8,32,1024]{2,1,0:T(8,128)}, f32[8,32,1024]{2,1,0:T(8,128)S(1)}, f32[8,32,1024]{2,1,0:T(8,128)S(1)}, f32[32,512]{1,0:T(8,128)S(1)}) custom-call(bf16[8,1024,1024]{2,1,0:T(8,128)(2,1)} %get-tuple-element.716.m_ref, f32[8,1,1024]{2,1,0:T(1,128)} %get-tuple-element.717.diag_ref, ...), custom_call_target="tpu_custom_call", output_to_operand_aliasing={{1}: (6, {}), {2}: (7, {})} | custom-call | flops 600000000 | bytes 23068672 | tf_op jit(solution)/shard_map/while/body/eval_jaxpr/pallas_call | solution.py:422
  577.6 9.8 %all-to-all-start = ((f32[128,2,128]{2,1,0:T(2,128)}), f32[128,2,128]{2,1,0:T(2,128)S(1)}, u32[]{:S(2)}, u32[]{:S(2)}) async-start(f32[128,2,128]{2,1,0:T(2,128)} %bitcast.27), calls=%async_computation | async-start | bytes 262144 | tf_op jit(solution)/shard_map/while/body/eval_jaxpr/all_to_all | solution.py:335
  587.4 10.1 %all-to-all-done = f32[128,2,128]{2,1,0:T(2,128)S(1)} async-done(((f32[128,2,128]{2,1,0:T(2,128)}), f32[128,2,128]{2,1,0:T(2,128)S(1)}, u32[]{:S(2)}, u32[]{:S(2)}) %all-to-all-start) | async-done | bytes 131104 | tf_op jit(solution)/shard_map/while/body/eval_jaxpr/all_to_all | solution.py:335
  599.6 4.1 all-to-all-start.1
  603.9 11.5 %eval_jaxpr.15 = (f32[8,32,1024]{2,1,0:T(8,128)}, f32[8,32,1024]{2,1,0:T(8,128)S(1)}, f32[8,32,1024]{2,1,0:T(8,128)S(1)}, f32[32,512]{1,0:T(8,128)S(1)}) custom-call(bf16[8,1024,1024]{2,1,0:T(8,128)(2,1)} %get-tuple-element.716.m_ref, f32[8,1,1024]{2,1,0:T(1,128)} %get-tuple-element.717.diag_ref, ...), custom_call_target="tpu_custom_call", output_to_operand_aliasing={{1}: (6, {}), {2}: (7, {})} | custom-call | flops 600000000 | bytes 23068672 | tf_op jit(solution)/shard_map/while/body/eval_jaxpr/pallas_call | solution.py:422
  619.8 9.8 %all-to-all-start.3 = ((f32[128,1,128]{2,1,0:T(1,128)}), f32[128,1,128]{2,1,0:T(1,128)S(1)}, u32[]{:S(2)}, u32[]{:S(2)}) async-start(f32[128,1,128]{2,1,0:T(1,128)} %broadcast_in_dim.28), calls=%async_computation.3 | async-start | bytes 131072 | tf_op jit(solution)/shard_map/all_to_all | solution.py:335
  630.7 8.5 %all-to-all-done.3 = f32[128,1,128]{2,1,0:T(1,128)S(1)} async-done(((f32[128,1,128]{2,1,0:T(1,128)}), f32[128,1,128]{2,1,0:T(1,128)S(1)}, u32[]{:S(2)}, u32[]{:S(2)}) %all-to-all-start.3) | async-done | bytes 65568 | tf_op jit(solution)/shard_map/all_to_all | solution.py:335
  (130 shorter events, 81.4 us)
Async XLA Ops:
  0.6 42.6 %copy-start.1 = (f32[8,32,1024]{2,1,0:T(8,128)S(1)}, f32[8,32,1024]{2,1,0:T(8,128)}, u32[]{:S(2)}) copy-start(f32[8,32,1024]{2,1,0:T(8,128)} %load_ref.1) | copy-start | bytes 3145732
  0.6 42.7 %copy-start.4 = (f32[8,1024]{1,0:T(8,128)S(1)}, f32[8,1024]{1,0:T(8,128)}, u32[]{:S(2)}) copy-start(f32[8,1024]{1,0:T(8,128)} %param.12) | copy-start | bytes 98308
  0.7 43.6 %copy-start.5 = (f32[8,1024]{1,0:T(8,128)S(1)}, f32[8,1024]{1,0:T(8,128)}, u32[]{:S(2)}) copy-start(f32[8,1024]{1,0:T(8,128)} %param.13) | copy-start | bytes 98308
  2.1 41.1 %copy-start.7 = (s32[1,128]{1,0:T(1,128)S(1)}, s32[1,128]{1,0:T(1,128)}, u32[]{:S(2)}) copy-start(s32[1,128]{1,0:T(1,128)} %reshape.130.live_row) | copy-start | bytes 1540
  8.7 40.0 %all-to-all-start.2 = ((s32[128,2,128]{2,1,0:T(2,128)}), s32[128,2,128]{2,1,0:T(2,128)S(1)}, u32[]{:S(2)}, u32[]{:S(2)}) async-start(s32[128,2,128]{2,1,0:T(2,128)} %bitcast.38), calls=%async_computation.2 | async-start | bytes 262144 | tf_op jit(solution)/shard_map/all_to_all | solution.py:335
  20.2 30.8 %copy-start.6 = (s32[8]{0:T(128)S(1)}, s32[8]{0:T(128)}, u32[]{:S(2)}) copy-start(s32[8]{0:T(128)} %param.15) | copy-start | bytes 100
  43.2 6.5 %copy-start.2 = (bf16[512,512]{1,0:T(8,128)(2,1)}, bf16[512,512]{1,0:T(8,128)(2,1)S(1)}, u32[]{:S(2)}) copy-start(bf16[512,512]{1,0:T(8,128)(2,1)S(1)} %get-tuple-element.677.bdh_ref) | copy-start | bytes 1572868
  43.2 6.5 %copy-start.3 = (bf16[512,512]{1,0:T(8,128)(2,1)}, bf16[512,512]{1,0:T(8,128)(2,1)S(1)}, u32[]{:S(2)}) copy-start(bf16[512,512]{1,0:T(8,128)(2,1)S(1)} %get-tuple-element.678.bdl_ref) | copy-start | bytes 1572868
  45.5 0.8 copy-start
  51.0 19.8 %all-to-all-start = ((f32[128,2,128]{2,1,0:T(2,128)}), f32[128,2,128]{2,1,0:T(2,128)S(1)}, u32[]{:S(2)}, u32[]{:S(2)}) async-start(f32[128,2,128]{2,1,0:T(2,128)} %bitcast.27), calls=%async_computation | async-start | bytes 262144 | tf_op jit(solution)/shard_map/while/body/eval_jaxpr/all_to_all | solution.py:335
  73.0 15.8 %all-to-all-start.1 = ((f32[128,2,128]{2,1,0:T(2,128)}), f32[128,2,128]{2,1,0:T(2,128)S(1)}, u32[]{:S(2)}, u32[]{:S(2)}) async-start(f32[128,2,128]{2,1,0:T(2,128)} %bitcast.29), calls=%async_computation.1 | async-start | bytes 262144 | tf_op jit(solution)/shard_map/while/body/eval_jaxpr/all_to_all | solution.py:335
  91.5 19.8 %all-to-all-start = ((f32[128,2,128]{2,1,0:T(2,128)}), f32[128,2,128]{2,1,0:T(2,128)S(1)}, u32[]{:S(2)}, u32[]{:S(2)}) async-start(f32[128,2,128]{2,1,0:T(2,128)} %bitcast.27), calls=%async_computation | async-start | bytes 262144 | tf_op jit(solution)/shard_map/while/body/eval_jaxpr/all_to_all | solution.py:335
  113.5 15.8 %all-to-all-start.1 = ((f32[128,2,128]{2,1,0:T(2,128)}), f32[128,2,128]{2,1,0:T(2,128)S(1)}, u32[]{:S(2)}, u32[]{:S(2)}) async-start(f32[128,2,128]{2,1,0:T(2,128)} %bitcast.29), calls=%async_computation.1 | async-start | bytes 262144 | tf_op jit(solution)/shard_map/while/body/eval_jaxpr/all_to_all | solution.py:335
  132.0 19.8 %all-to-all-start = ((f32[128,2,128]{2,1,0:T(2,128)}), f32[128,2,128]{2,1,0:T(2,128)S(1)}, u32[]{:S(2)}, u32[]{:S(2)}) async-start(f32[128,2,128]{2,1,0:T(2,128)} %bitcast.27), calls=%async_computation | async-start | bytes 262144 | tf_op jit(solution)/shard_map/while/body/eval_jaxpr/all_to_all | solution.py:335
  154.0 15.8 %all-to-all-start.1 = ((f32[128,2,128]{2,1,0:T(2,128)}), f32[128,2,128]{2,1,0:T(2,128)S(1)}, u32[]{:S(2)}, u32[]{:S(2)}) async-start(f32[128,2,128]{2,1,0:T(2,128)} %bitcast.29), calls=%async_computation.1 | async-start | bytes 262144 | tf_op jit(solution)/shard_map/while/body/eval_jaxpr/all_to_all | solution.py:335
  172.5 19.8 %all-to-all-start = ((f32[128,2,128]{2,1,0:T(2,128)}), f32[128,2,128]{2,1,0:T(2,128)S(1)}, u32[]{:S(2)}, u32[]{:S(2)}) async-start(f32[128,2,128]{2,1,0:T(2,128)} %bitcast.27), calls=%async_computation | async-start | bytes 262144 | tf_op jit(solution)/shard_map/while/body/eval_jaxpr/all_to_all | solution.py:335
  194.5 15.8 %all-to-all-start.1 = ((f32[128,2,128]{2,1,0:T(2,128)}), f32[128,2,128]{2,1,0:T(2,128)S(1)}, u32[]{:S(2)}, u32[]{:S(2)}) async-start(f32[128,2,128]{2,1,0:T(2,128)} %bitcast.29), calls=%async_computation.1 | async-start | bytes 262144 | tf_op jit(solution)/shard_map/while/body/eval_jaxpr/all_to_all | solution.py:335
  213.0 19.8 %all-to-all-start = ((f32[128,2,128]{2,1,0:T(2,128)}), f32[128,2,128]{2,1,0:T(2,128)S(1)}, u32[]{:S(2)}, u32[]{:S(2)}) async-start(f32[128,2,128]{2,1,0:T(2,128)} %bitcast.27), calls=%async_computation | async-start | bytes 262144 | tf_op jit(solution)/shard_map/while/body/eval_jaxpr/all_to_all | solution.py:335
  235.0 15.8 %all-to-all-start.1 = ((f32[128,2,128]{2,1,0:T(2,128)}), f32[128,2,128]{2,1,0:T(2,128)S(1)}, u32[]{:S(2)}, u32[]{:S(2)}) async-start(f32[128,2,128]{2,1,0:T(2,128)} %bitcast.29), calls=%async_computation.1 | async-start | bytes 262144 | tf_op jit(solution)/shard_map/while/body/eval_jaxpr/all_to_all | solution.py:335
  253.5 19.8 %all-to-all-start = ((f32[128,2,128]{2,1,0:T(2,128)}), f32[128,2,128]{2,1,0:T(2,128)S(1)}, u32[]{:S(2)}, u32[]{:S(2)}) async-start(f32[128,2,128]{2,1,0:T(2,128)} %bitcast.27), calls=%async_computation | async-start | bytes 262144 | tf_op jit(solution)/shard_map/while/body/eval_jaxpr/all_to_all | solution.py:335
  275.5 15.8 %all-to-all-start.1 = ((f32[128,2,128]{2,1,0:T(2,128)}), f32[128,2,128]{2,1,0:T(2,128)S(1)}, u32[]{:S(2)}, u32[]{:S(2)}) async-start(f32[128,2,128]{2,1,0:T(2,128)} %bitcast.29), calls=%async_computation.1 | async-start | bytes 262144 | tf_op jit(solution)/shard_map/while/body/eval_jaxpr/all_to_all | solution.py:335
  294.0 19.8 %all-to-all-start = ((f32[128,2,128]{2,1,0:T(2,128)}), f32[128,2,128]{2,1,0:T(2,128)S(1)}, u32[]{:S(2)}, u32[]{:S(2)}) async-start(f32[128,2,128]{2,1,0:T(2,128)} %bitcast.27), calls=%async_computation | async-start | bytes 262144 | tf_op jit(solution)/shard_map/while/body/eval_jaxpr/all_to_all | solution.py:335
  316.0 15.8 %all-to-all-start.1 = ((f32[128,2,128]{2,1,0:T(2,128)}), f32[128,2,128]{2,1,0:T(2,128)S(1)}, u32[]{:S(2)}, u32[]{:S(2)}) async-start(f32[128,2,128]{2,1,0:T(2,128)} %bitcast.29), calls=%async_computation.1 | async-start | bytes 262144 | tf_op jit(solution)/shard_map/while/body/eval_jaxpr/all_to_all | solution.py:335
  334.6 19.8 %all-to-all-start = ((f32[128,2,128]{2,1,0:T(2,128)}), f32[128,2,128]{2,1,0:T(2,128)S(1)}, u32[]{:S(2)}, u32[]{:S(2)}) async-start(f32[128,2,128]{2,1,0:T(2,128)} %bitcast.27), calls=%async_computation | async-start | bytes 262144 | tf_op jit(solution)/shard_map/while/body/eval_jaxpr/all_to_all | solution.py:335
  356.6 15.8 %all-to-all-start.1 = ((f32[128,2,128]{2,1,0:T(2,128)}), f32[128,2,128]{2,1,0:T(2,128)S(1)}, u32[]{:S(2)}, u32[]{:S(2)}) async-start(f32[128,2,128]{2,1,0:T(2,128)} %bitcast.29), calls=%async_computation.1 | async-start | bytes 262144 | tf_op jit(solution)/shard_map/while/body/eval_jaxpr/all_to_all | solution.py:335
  375.1 19.8 %all-to-all-start = ((f32[128,2,128]{2,1,0:T(2,128)}), f32[128,2,128]{2,1,0:T(2,128)S(1)}, u32[]{:S(2)}, u32[]{:S(2)}) async-start(f32[128,2,128]{2,1,0:T(2,128)} %bitcast.27), calls=%async_computation | async-start | bytes 262144 | tf_op jit(solution)/shard_map/while/body/eval_jaxpr/all_to_all | solution.py:335
  397.1 15.8 %all-to-all-start.1 = ((f32[128,2,128]{2,1,0:T(2,128)}), f32[128,2,128]{2,1,0:T(2,128)S(1)}, u32[]{:S(2)}, u32[]{:S(2)}) async-start(f32[128,2,128]{2,1,0:T(2,128)} %bitcast.29), calls=%async_computation.1 | async-start | bytes 262144 | tf_op jit(solution)/shard_map/while/body/eval_jaxpr/all_to_all | solution.py:335
  415.6 19.8 %all-to-all-start = ((f32[128,2,128]{2,1,0:T(2,128)}), f32[128,2,128]{2,1,0:T(2,128)S(1)}, u32[]{:S(2)}, u32[]{:S(2)}) async-start(f32[128,2,128]{2,1,0:T(2,128)} %bitcast.27), calls=%async_computation | async-start | bytes 262144 | tf_op jit(solution)/shard_map/while/body/eval_jaxpr/all_to_all | solution.py:335
  437.6 15.8 %all-to-all-start.1 = ((f32[128,2,128]{2,1,0:T(2,128)}), f32[128,2,128]{2,1,0:T(2,128)S(1)}, u32[]{:S(2)}, u32[]{:S(2)}) async-start(f32[128,2,128]{2,1,0:T(2,128)} %bitcast.29), calls=%async_computation.1 | async-start | bytes 262144 | tf_op jit(solution)/shard_map/while/body/eval_jaxpr/all_to_all | solution.py:335
  456.1 19.8 %all-to-all-start = ((f32[128,2,128]{2,1,0:T(2,128)}), f32[128,2,128]{2,1,0:T(2,128)S(1)}, u32[]{:S(2)}, u32[]{:S(2)}) async-start(f32[128,2,128]{2,1,0:T(2,128)} %bitcast.27), calls=%async_computation | async-start | bytes 262144 | tf_op jit(solution)/shard_map/while/body/eval_jaxpr/all_to_all | solution.py:335
  478.1 15.8 %all-to-all-start.1 = ((f32[128,2,128]{2,1,0:T(2,128)}), f32[128,2,128]{2,1,0:T(2,128)S(1)}, u32[]{:S(2)}, u32[]{:S(2)}) async-start(f32[128,2,128]{2,1,0:T(2,128)} %bitcast.29), calls=%async_computation.1 | async-start | bytes 262144 | tf_op jit(solution)/shard_map/while/body/eval_jaxpr/all_to_all | solution.py:335
  496.6 19.8 %all-to-all-start = ((f32[128,2,128]{2,1,0:T(2,128)}), f32[128,2,128]{2,1,0:T(2,128)S(1)}, u32[]{:S(2)}, u32[]{:S(2)}) async-start(f32[128,2,128]{2,1,0:T(2,128)} %bitcast.27), calls=%async_computation | async-start | bytes 262144 | tf_op jit(solution)/shard_map/while/body/eval_jaxpr/all_to_all | solution.py:335
  518.6 15.8 %all-to-all-start.1 = ((f32[128,2,128]{2,1,0:T(2,128)}), f32[128,2,128]{2,1,0:T(2,128)S(1)}, u32[]{:S(2)}, u32[]{:S(2)}) async-start(f32[128,2,128]{2,1,0:T(2,128)} %bitcast.29), calls=%async_computation.1 | async-start | bytes 262144 | tf_op jit(solution)/shard_map/while/body/eval_jaxpr/all_to_all | solution.py:335
  537.1 19.8 %all-to-all-start = ((f32[128,2,128]{2,1,0:T(2,128)}), f32[128,2,128]{2,1,0:T(2,128)S(1)}, u32[]{:S(2)}, u32[]{:S(2)}) async-start(f32[128,2,128]{2,1,0:T(2,128)} %bitcast.27), calls=%async_computation | async-start | bytes 262144 | tf_op jit(solution)/shard_map/while/body/eval_jaxpr/all_to_all | solution.py:335
  559.1 15.8 %all-to-all-start.1 = ((f32[128,2,128]{2,1,0:T(2,128)}), f32[128,2,128]{2,1,0:T(2,128)S(1)}, u32[]{:S(2)}, u32[]{:S(2)}) async-start(f32[128,2,128]{2,1,0:T(2,128)} %bitcast.29), calls=%async_computation.1 | async-start | bytes 262144 | tf_op jit(solution)/shard_map/while/body/eval_jaxpr/all_to_all | solution.py:335
  577.6 19.8 %all-to-all-start = ((f32[128,2,128]{2,1,0:T(2,128)}), f32[128,2,128]{2,1,0:T(2,128)S(1)}, u32[]{:S(2)}, u32[]{:S(2)}) async-start(f32[128,2,128]{2,1,0:T(2,128)} %bitcast.27), calls=%async_computation | async-start | bytes 262144 | tf_op jit(solution)/shard_map/while/body/eval_jaxpr/all_to_all | solution.py:335
  599.6 15.8 %all-to-all-start.1 = ((f32[128,2,128]{2,1,0:T(2,128)}), f32[128,2,128]{2,1,0:T(2,128)S(1)}, u32[]{:S(2)}, u32[]{:S(2)}) async-start(f32[128,2,128]{2,1,0:T(2,128)} %bitcast.29), calls=%async_computation.1 | async-start | bytes 262144 | tf_op jit(solution)/shard_map/while/body/eval_jaxpr/all_to_all | solution.py:335
  619.8 19.4 %all-to-all-start.3 = ((f32[128,1,128]{2,1,0:T(1,128)}), f32[128,1,128]{2,1,0:T(1,128)S(1)}, u32[]{:S(2)}, u32[]{:S(2)}) async-start(f32[128,1,128]{2,1,0:T(1,128)} %broadcast_in_dim.28), calls=%async_computation.3 | async-start | bytes 131072 | tf_op jit(solution)/shard_map/all_to_all | solution.py:335

commit v2 on v1

v2 whole, which is shorter than its diff:
```python
import functools

import jax
import jax.numpy as jnp
from jax import lax
from jax.experimental import pallas as pl
from jax.experimental.pallas import tpu as pltpu
from jax.sharding import PartitionSpec as P

K = 1024
S = 32
AREA = 8
NB = 16
ITEMS = AREA * NB
ROWS = 4
EDGE = NB * ROWS
CAP = 8
N_REGION = 8
N_DEV = 16
WORLD = N_REGION * N_DEV
BUS_DEV = 16
ITERS = 14
RHO = 4.0
SIGMA = 1.0
HALF = AREA // 2
CELLS = 1024.0 * 128.0
BOTH = ("region", "dev")
F32 = jnp.float32
BF16 = jnp.bfloat16


def dot(left, right):
    return jnp.dot(left, right, preferred_element_type=F32)


def split3(x):
    high = x.astype(BF16)
    rest = x - high.astype(F32)
    middle = rest.astype(BF16)
    low = (rest - middle.astype(F32)).astype(BF16)
    return high, middle, low


def pick(x, onehot):
    count = x.shape[0]
    got = dot(jnp.concatenate(split3(x), axis=0), onehot)
    return got[:count] + got[count : 2 * count] + got[2 * count :]


def iota(shape, dim):
    return lax.broadcasted_iota(jnp.int32, shape, dim)


def edge_order(transposed=False):
    old = iota((128, 128), 1 if transposed else 0)
    new = iota((128, 128), 0 if transposed else 1)
    target = jnp.where(old < EDGE, (old & 3) * NB + (old >> 2), old)
    return jnp.where(new == target, 1.0, 0.0).astype(BF16)


def struct(shape, dtype=F32):
    return jax.ShapeDtypeStruct(shape, dtype)


def cost(flops, nbytes):
    return pl.CostEstimate(flops=flops, bytes_accessed=nbytes, transcendentals=0)


SMEM = pl.BlockSpec(memory_space=pltpu.SMEM)
VM = pl.BlockSpec(memory_space=pltpu.VMEM)
ANY = pl.BlockSpec(memory_space=pl.ANY)


def call(kernel, out_shape, limit=16, **kw):
    return pl.pallas_call(
        kernel,
        out_shape=out_shape,
        compiler_params=pltpu.CompilerParams(vmem_limit_bytes=limit * 2**20),
        **kw,
    )


def route_kernel(me_ref, counts_ref, inc_ref, p_ref, pt_ref, tag_ref, live_ref):
    me = me_ref[0]
    lane = iota((ITEMS, ITEMS), 1)
    sub = iota((ITEMS, ITEMS), 0)
    area_of = iota((1, ITEMS), 1) >> 4
    wide = jnp.concatenate([inc_ref[...].astype(F32), jnp.zeros((AREA, 112), F32)], axis=1)
    ids = jnp.zeros((1, ITEMS), F32)
    count = jnp.zeros((1, ITEMS), jnp.int32)
    for a in range(AREA):
        row = wide[a : a + 1, :]
        if a:
            row = pltpu.roll(row, NB * a, 1)
        ids = jnp.where(area_of == a, row, ids)
        count = jnp.where(area_of == a, counts_ref[a], count)
    live = (iota((1, ITEMS), 1) & 15) < count
    live_ref[...] = jnp.where(live, 1.0, 0.0)
    bus = ids.astype(jnp.int32)
    region = bus >> 8
    peer = (bus >> 4) & 15
    key_r = jnp.where(live, jnp.where(region == me, peer, 16 + region), -1).astype(F32)
    key_c = jnp.transpose(jnp.broadcast_to(key_r, (ITEMS, ITEMS)))
    local_c = jnp.transpose(jnp.broadcast_to((bus & 15).astype(F32), (ITEMS, ITEMS)))
    same = (key_c == key_r) & (key_r >= 0.0)
    rank_c = jnp.sum(jnp.where(same & (lane < sub), 1.0, 0.0), axis=1, keepdims=True)
    rank_r = jnp.sum(jnp.where(same & (sub < lane), 1.0, 0.0), axis=0, keepdims=True)

    def place(key, rank):
        far = ITEMS + rank * N_REGION + key - 16.0
        return jnp.where(key < 0.0, -1.0, jnp.where(key < 16.0, rank * N_DEV + key, far))

    place_c = place(key_c, jnp.broadcast_to(rank_c, (ITEMS, ITEMS)))
    place_c = jnp.concatenate([place_c, place_c], axis=1)
    local_c = jnp.concatenate([local_c, local_c], axis=1)
    hit = iota((ITEMS, 256), 1).astype(F32) == place_c
    p_ref[...] = jnp.where(hit, 1.0, 0.0).astype(BF16)
    hit_t = iota((256, ITEMS), 0).astype(F32) == place(key_r, rank_r)
    pt_ref[...] = jnp.where(hit_t, 1.0, 0.0).astype(BF16)
    tag = jnp.sum(jnp.where(hit, local_c + 1.0, 0.0), axis=0, keepdims=True) - 1.0
    tag_ref[0:1, :] = tag[:, :128]
    tag_ref[1:2, :] = tag[:, 128:]


def near_rows(width, dev):
    return pl.ds(width * dev, N_REGION, stride=width * N_DEV)


def far_rows(width, region):
    return pl.ds(width * N_DEV * region + 1, N_DEV, stride=width)


def bus_sums(near, far, near_tags, far_tags):
    group = iota((N_REGION, 128), 1) >> 4
    halves = []
    for half in range(2):
        total = jnp.zeros((N_REGION, 128), F32)
        for low in range(8):
            bus = 8.0 * half + low
            acc = jnp.zeros((N_REGION, 128), F32)
            for dev in range(N_DEV):
                acc = acc + jnp.where(near_tags[dev] == bus, near[dev], 0.0)
            for shift in (16, 32, 64):
                acc = acc + pltpu.roll(acc, shift, 1)
            total = jnp.where(group == low, acc, total)
        rows = []
        for low in range(8):
            bus = 8.0 * half + low
            acc = jnp.zeros((N_DEV, 128), F32)
            for region in range(N_REGION):
                acc = acc + jnp.where(far_tags[region] == bus, far[region], 0.0)
            rows.append(acc)
        turned = jnp.transpose(jnp.concatenate(rows, axis=0))
        for c in range(CAP):
            total = total + turned[8 * c : 8 * c + 8]
        halves.append(total)
    return jnp.concatenate(halves, axis=1)


def owner_kernel(first, last, *refs):
    if first:
        got_ref, tie_ref, out_ref, z_ref, u_ref, rec_ref, tag_ref, inv_ref = refs
        near_tags = [got_ref[pl.ds(4 * d + 2, N_REGION, stride=4 * N_DEV), :] for d in range(N_DEV)]
        far_tags = [
            got_ref[pl.ds(4 * N_DEV * r + 3, N_DEV, stride=4), :] for r in range(N_REGION)
        ]
        one_n = jnp.ones((N_REGION, 128), F32)
        one_f = jnp.ones((N_DEV, 128), F32)
        counts = bus_sums([one_n] * N_DEV, [one_f] * N_REGION, near_tags, far_tags)
        inverse = 1.0 / jnp.maximum(counts, 1.0)
        inv_ref[...] = inverse
        for d in range(N_DEV):
            tag_ref[near_rows(2, d), :] = near_tags[d]
        for r in range(N_REGION):
            tag_ref[far_rows(2, r), :] = far_tags[r]
        rec_ref[...] = jnp.zeros((128, 128), F32)
        step = 0
    else:
        if last:
            step_ref, got_ref, tag_ref, inv_ref, tie_ref, prev_ref, u_in, rec_in, out_ref = refs
        else:
            (step_ref, got_ref, tag_ref, inv_ref, tie_ref, prev_ref, u_in, rec_in,
             out_ref, z_ref, u_ref, rec_ref) = refs
        near_tags = [tag_ref[near_rows(2, d), :] for d in range(N_DEV)]
        far_tags = [tag_ref[far_rows(2, r), :] for r in range(N_REGION)]
        inverse = inv_ref[...]
        step = step_ref[0]
    wide_in = 4 if first else 2
    wide_out = 4 if last else 2
    near = [got_ref[near_rows(wide_in, d), :] for d in range(N_DEV)]
    far = [got_ref[far_rows(wide_in, r), :] for r in range(N_REGION)]
    z = bus_sums(near, far, near_tags, far_tags) * inverse
    change = z if first else z - prev_ref[...]
    change = change * change
    dual = jnp.sum(change[:, :128] + change[:, 128:], axis=0, keepdims=True) * (RHO * RHO / CELLS)
    group = iota((N_REGION, 128), 1) >> 4
    spread = []
    turned = []
    for half in range(2):
        part = z[:, 128 * half : 128 * half + 128]
        for low in range(8):
            one = jnp.where(group == low, part, 0.0)
            for shift in (16, 32, 64):
                one = one + pltpu.roll(one, shift, 1)
            spread.append(one)
        turned.append(jnp.transpose(jnp.concatenate([part] * 16, axis=0)))
    primal = jnp.zeros((N_REGION, 128), F32)
    for dev in range(N_DEV):
        val = jnp.zeros((N_REGION, 128), F32)
        for bus in range(BUS_DEV):
            val = jnp.where(near_tags[dev] == float(bus), spread[bus], val)
        out_ref[near_rows(wide_out, dev), :] = val
        u = near[dev] - val
        gap = u if first else u - u_in[near_rows(2, dev), :]
        primal = primal + gap * gap
        if not last:
            u_ref[near_rows(2, dev), :] = u
    for region in range(N_REGION):
        val = jnp.zeros((N_DEV, 128), F32)
        for bus in range(BUS_DEV):
            low = bus % 8
            one = turned[bus // 8][16 * low : 16 * low + 16]
            val = jnp.where(far_tags[region] == float(bus), one, val)
        out_ref[far_rows(wide_out, region), :] = val
        u = far[region] - val
        gap = u if first else u - u_in[far_rows(2, region), :]
        square = gap * gap
        primal = primal + square[:8] + square[8:]
        if not last:
            u_ref[far_rows(2, region), :] = u
    primal = jnp.sum(primal, axis=0, keepdims=True) * (1.0 / CELLS)
    row = iota((128, 128), 0)
    if last:
        rec = jnp.where(row == step, primal, rec_in[...])
        rec = jnp.where(row == 16 + step, dual, rec)
        sums = jnp.sum(jnp.transpose(rec), axis=0, keepdims=True)
        out_ref[pl.ds(2, WORLD, stride=4), :] = jnp.broadcast_to(sums, (WORLD, 128))
        out_ref[pl.ds(3, WORLD, stride=4), :] = jnp.zeros((WORLD, 128), F32)
    else:
        if not first:
            rec_ref[...] = rec_in[...]
        rec_ref[pl.ds(step, 1), :] = primal
        rec_ref[pl.ds(16 + step, 1), :] = dual
        z_ref[...] = z


def by_lane(rows):
    return jnp.concatenate([rows[S * r : S * r + S] for r in range(ROWS)], axis=1)


def by_row(lanes):
    return jnp.concatenate([lanes[:, ITEMS * r : ITEMS * r + ITEMS] for r in range(ROWS)], axis=0)


def open_kernel(c_ref, p_ref, tag_ref, send_ref, e_ref, blk_ref, u_ref):
    blk = by_row(c_ref[...])
    blk_ref[...] = blk
    u_ref[...] = jnp.zeros_like(blk)
    e_ref[...] = jnp.zeros((S, ROWS * ITEMS), F32)
    send = pick(blk, p_ref[...])
    send_ref[pl.ds(0, WORLD, stride=4), :] = send[:, :128]
    send_ref[pl.ds(1, WORLD, stride=4), :] = send[:, 128:]
    send_ref[pl.ds(2, WORLD, stride=4), :] = jnp.broadcast_to(tag_ref[0:1, :], (WORLD, 128))
    send_ref[pl.ds(3, WORLD, stride=4), :] = jnp.broadcast_to(tag_ref[1:2, :], (WORLD, 128))


def take_means(z_ref, pt_ref, width):
    near = z_ref[pl.ds(0, WORLD, stride=width), :]
    far = z_ref[pl.ds(1, WORLD, stride=width), :]
    return pick(jnp.concatenate([near, far], axis=1), pt_ref[...])


def slot_kernel(
    z_ref, p_ref, pt_ref, live_ref, blk_in, u_in, c_ref, bdh_ref, bdl_ref,
    send_ref, e_ref, blk_ref, u_ref,
):
    z_slot = take_means(z_ref, pt_ref, 2)
    u = u_in[...] + (blk_in[...] - z_slot) * live_ref[...]
    u_ref[...] = u
    e = by_lane(RHO * (z_slot - u))
    e_ref[...] = e
    e_high = e.astype(BF16)
    e_low = (e - e_high.astype(F32)).astype(BF16)
    both = dot(jnp.concatenate([e_high, e_low], axis=0), bdh_ref[...])
    edge = c_ref[...] + both[:S] + both[S:] + dot(e_high, bdl_ref[...])
    blk = by_row(edge)
    blk_ref[...] = blk
    send = pick(blk + u, p_ref[...])
    send_ref[pl.ds(0, WORLD, stride=2), :] = send[:, :128]
    send_ref[pl.ds(1, WORLD, stride=2), :] = send[:, 128:]


def close_kernel(z_ref, pt_ref, live_ref, blk_in, u_in, dual_ref, record_ref):
    z_slot = take_means(z_ref, pt_ref, 4)
    u = u_in[...] + (blk_in[...] - z_slot) * live_ref[...]
    old = iota((128, 128), 0)
    order = jnp.where(iota((128, 128), 1) == (old & 31) * ROWS + (old >> 5), 1.0, 0.0)
    dual_ref[...] = pick(jnp.transpose(u), order.astype(BF16))
    sums = jnp.sum(z_ref[pl.ds(2, WORLD, stride=4), :], axis=0, keepdims=True)
    column = jnp.transpose(jnp.broadcast_to(sums, (128, 128)))
    first = iota((16, 128), 1) == 0
    both = jnp.where(first, column[:16], column[16:32])
    record_ref[...] = both[:ITERS, :2]


def edge_part(right_side, m_edge, diag_edge):
    return dot(right_side.astype(BF16), m_edge) + right_side[:, :128] * diag_edge


def setup_kernel(
    f_ref, p_ref, load_ref, lo_ref, hi_ref,
    m_ref, diag_ref, c_ref, bdh_ref, bdl_ref, load0_ref, load1_ref, lo_out, hi_out, ft, g,
):
    area = pl.program_id(0)
    order = edge_order()
    piv = p_ref[pl.ds(area, 1), :]
    piv_col = jnp.transpose(jnp.broadcast_to(piv, (128, K)))
    step = 256
    count = K // step
    head = dot(f_ref[0, :, :128], order)
    g[:, :128] = (head * piv_col).astype(BF16)
    f_head = head.astype(BF16)
    for q in range(1, K // 128):
        top = q // 2 * step
        part = f_ref[0, top:, 128 * q : 128 * q + 128].astype(F32)
        g[top:, 128 * q : 128 * q + 128] = (part * piv_col[top:]).astype(BF16)
    for i in range(count):
        at = slice(i * step, (i + 1) * step)
        w = (i + 1) * step
        rows = jnp.concatenate([f_head[at], f_ref[0, at, 128:w]], axis=1)
        ft[:w, at] = jnp.transpose(rows)
    eye = iota((step, step), 0) == iota((step, step), 1)
    fix = piv - piv.astype(BF16).astype(F32)
    fix = jnp.concatenate([pick(fix[:, :128], order), fix[:, 128:]], axis=1)
    edge_m = None
    edge_diag = None
    for i in range(count):
        at = slice(i * step, (i + 1) * step)
        w = (i + 1) * step
        column = dot(ft[:w, i * step :], g[i * step :, at])
        block = column[i * step :]
        diag = jnp.sum(jnp.where(eye, block, 0.0), axis=0, keepdims=True) + fix[:, at]
        diag_ref[pl.ds(area, 1), at] = diag
        block = jnp.where(eye, 0.0, block)
        if i == 0:
            edge_diag = diag[:, :128]
            edge_m = jnp.where(eye, diag, block)[:EDGE, :128]
        m_ref[0, at, at] = block.astype(BF16)
        if i:
            above = column[: i * step].astype(BF16)
            m_ref[0, : i * step, at] = above
            m_ref[0, at, : i * step] = jnp.transpose(above)
    mine = (iota((NB, 128), 1) >> 4) == area
    for r in range(ROWS):
        shift = lax.rem(area * NB + (128 - r * NB), 128)
        for r_in in range(ROWS):
            rows = edge_m[NB * r_in : NB * r_in + NB]
            rows = jnp.where(mine, pltpu.roll(rows, shift, 1), 0.0)
            high = rows.astype(BF16)
            at = pl.ds(pl.multiple_of(ITEMS * r_in + NB * area, NB), NB)
            bdh_ref[at, ITEMS * r : ITEMS * r + ITEMS] = high
            bdl_ref[at, ITEMS * r : ITEMS * r + ITEMS] = (rows - high.astype(F32)).astype(BF16)
    load = load_ref[0]
    load = jnp.concatenate([pick(load[:, :128], order), load[:, 128:]], axis=1)
    c = edge_part(load, m_ref[0, :, :128], edge_diag)

    @pl.when(area == 0)
    def _():
        c_ref[...] = jnp.zeros_like(c_ref)
        for source, out in ((lo_ref, lo_out), (hi_ref, hi_out)):
            out[:, :128] = pick(source[:, :128], order)
            out[:, 128:] = source[:, 128:]

    @pl.when(area < HALF)
    def _():
        load0_ref[0] = load

    @pl.when(area >= HALF)
    def _():
        load1_ref[0] = load

    lane_mine = (iota((S, 128), 1) >> 4) == area
    for r in range(ROWS):
        at = slice(ITEMS * r, ITEMS * r + ITEMS)
        moved = pltpu.roll(c, lax.rem(area * NB + (128 - r * NB), 128), 1)
        c_ref[:, at] = jnp.where(lane_mine, moved, c_ref[:, at])


def load_matrices(m_ref, first, buf, sem):
    copies = [pltpu.make_async_copy(m_ref.at[first + q], buf.at[q], sem.at[q]) for q in range(HALF)]
    for copy in copies:
        copy.start()
    return copies


def right_side_of(b_in, e_ref, q, area):
    group = iota((S, 128), 1) >> 4
    part = jnp.zeros((S, 128), F32)
    for r in range(ROWS):
        piece = e_ref[:, ITEMS * r : ITEMS * r + ITEMS]
        shift = (NB * (r - area)) % 128
        if shift:
            piece = pltpu.roll(piece, shift, 1)
        part = jnp.where(group == r, piece, part)
    base = b_in[q]
    return jnp.concatenate([base[:, :128] + part, base[:, 128:]], axis=1)


def area_kernel(first, m_ref, diag_ref, load_ref, lo_ref, hi_ref, e_ref, w_in, b_in, tie_ref, *refs):
    if first:
        c_in, w_ref, b_ref, c_ref, tie_out, buf, sem = refs
    else:
        w_ref, b_ref, c_ref, tie_out, buf, sem = refs
    copies = load_matrices(m_ref, first, buf, sem)
    sides = [right_side_of(b_in, e_ref, q, first + q) for q in range(HALF)]
    news = []
    for q in range(HALF):
        at = slice(first + q, first + q + 1)
        copies[q].wait()
        x = dot(sides[q].astype(BF16), buf[q]) + sides[q] * diag_ref[at, :]
        moved = x + w_in[q]
        y = jnp.clip(moved, lo_ref[at, :], hi_ref[at, :])
        w = moved - y
        w_ref[q] = w
        b = load_ref[q] + SIGMA * (y - w)
        b_ref[q] = b
        news.append(b)
    group = iota((S, 128), 1) >> 4
    edges = [c_in[:, ITEMS * r : ITEMS * r + ITEMS] if first else jnp.zeros((S, 128), F32) for r in range(ROWS)]
    for q in range(HALF):
        area = first + q
        c = edge_part(news[q], buf[q, :, :128], diag_ref[area : area + 1, :128])
        for r in range(ROWS):
            shift = (NB * (area - r)) % 128
            moved = pltpu.roll(c, shift, 1) if shift else c
            edges[r] = jnp.where(group == area, moved, edges[r])
    for r in range(ROWS):
        c_ref[:, ITEMS * r : ITEMS * r + ITEMS] = edges[r]
    tie_out[...] = edges[0][:8]


def last_kernel(first, m_ref, diag_ref, e_ref, b_in, tie_ref, *refs):
    if first:
        _, x_ref, buf, sem, x_buf, x_sem = refs
    else:
        x_ref, tie_out, buf, sem, x_buf, x_sem = refs
    copies = load_matrices(m_ref, first, buf, sem)
    order = edge_order(True)
    for q in range(HALF):
        area = first + q
        side = right_side_of(b_in, e_ref, q, area)
        copies[q].wait()
        x = dot(side.astype(BF16), buf[q]) + side * diag_ref[area : area + 1, :]
        x_buf[q] = jnp.concatenate([pick(x[:, :128], order), x[:, 128:]], axis=1)
    copy = pltpu.make_async_copy(x_buf, x_ref.at[pl.ds(first, HALF)], x_sem)
    copy.start()
    if not first:
        tie_out[...] = jnp.zeros((8, 128), F32)
    copy.wait()


def on_device(loads, factor, pivots, lower, upper, incidence, counts):
    wide = ROWS * ITEMS
    exchange = lambda x: lax.all_to_all(x, BOTH, split_axis=0, concat_axis=0, tiled=True)
    me = lax.axis_index("region").astype(jnp.int32).reshape(1)
    place, place_t, tags, live = call(
        route_kernel,
        (struct((ITEMS, 256), BF16), struct((256, ITEMS), BF16), struct((2, ITEMS)), struct((1, ITEMS))),
        in_specs=[SMEM, SMEM, VM],
    )(me, counts, incidence)

    area_block = lambda rows: pl.BlockSpec((1, rows, K), lambda a: (a, 0, 0))
    whole = lambda *shape: pl.BlockSpec(shape, lambda a: (0,) * len(shape))
    matrix, diag, c_now, bd_high, bd_low, load0, load1, floor_box, ceil_box = call(
        setup_kernel,
        (
            struct((AREA, K, K), BF16),
            struct((AREA, K)),
            struct((S, wide)),
            struct((wide, wide), BF16),
            struct((wide, wide), BF16),
            struct((HALF, S, K)),
            struct((HALF, S, K)),
            struct((AREA, K)),
            struct((AREA, K)),
        ),
        grid=(AREA,),
        in_specs=[area_block(K), whole(AREA, K), area_block(S), whole(AREA, K), whole(AREA, K)],
        out_specs=(
            area_block(K), whole(AREA, K), whole(S, wide), whole(wide, wide), whole(wide, wide),
            pl.BlockSpec((1, S, K), lambda a: (jnp.minimum(a, HALF - 1), 0, 0)),
            pl.BlockSpec((1, S, K), lambda a: (jnp.maximum(a - HALF, 0), 0, 0)),
            whole(AREA, K), whole(AREA, K),
        ),
        scratch_shapes=[pltpu.VMEM((K, K), BF16), pltpu.VMEM((K, K), BF16)],
        cost_estimate=cost(8 * 10**9, 34 * 2**20),
        limit=40,
    )(factor, pivots, loads, lower, upper)

    send, e, blk, u = call(
        open_kernel,
        (struct((512, 128)), struct((S, wide)), struct((128, 128)), struct((128, 128))),
        in_specs=[VM] * 3,
    )(c_now, place, tags)

    part_shape = struct((HALF, S, K))
    matrix_scratch = [pltpu.VMEM((HALF, K, K), BF16), pltpu.SemaphoreType.DMA((HALF,))]

    def run_areas(first, load, e, w, b, tie, c=None):
        return call(
            functools.partial(area_kernel, first),
            (part_shape, part_shape, struct((S, wide)), struct((8, 128))),
            in_specs=[ANY] + [VM] * (9 if first else 8),
            out_specs=(VM,) * 4,
            scratch_shapes=matrix_scratch,
            input_output_aliases={6: 0, 7: 1},
            cost_estimate=cost(4 * 10**8, 10 * 2**20),
            limit=20,
        )(matrix, diag, load, floor_box, ceil_box, e, w, b, tie, *((c,) if first else ()))

    def run_last(first, e, b, tie, x=None):
        x_shape = struct((AREA, S, K))
        return call(
            functools.partial(last_kernel, first),
            x_shape if first else (x_shape, struct((8, 128))),
            in_specs=[ANY, VM, VM, VM, VM] + ([ANY] if first else []),
            out_specs=ANY if first else (ANY, VM),
            scratch_shapes=matrix_scratch + [pltpu.VMEM((HALF, S, K), F32), pltpu.SemaphoreType.DMA],
            input_output_aliases={5: 0} if first else {},
            cost_estimate=cost(4 * 10**8, 10 * 2**20),
            limit=20,
        )(matrix, diag, e, b, tie, *((x,) if first else ()))

    z_shape = struct((N_REGION, 256))
    rows2 = struct((256, 128))
    rec_shape = struct((128, 128))
    small = cost(10**7, 2**20)
    owner_first = call(
        functools.partial(owner_kernel, True, False),
        (rows2, z_shape, rows2, rec_shape, rows2, z_shape),
        in_specs=[VM] * 2,
        cost_estimate=small,
    )
    owner_mid = call(
        functools.partial(owner_kernel, False, False),
        (rows2, z_shape, rows2, rec_shape),
        in_specs=[SMEM] + [VM] * 7,
        input_output_aliases={5: 1, 6: 2, 7: 3},
        cost_estimate=small,
    )
    owner_last = call(
        functools.partial(owner_kernel, False, True),
        struct((512, 128)),
        in_specs=[SMEM] + [VM] * 7,
        cost_estimate=small,
    )
    run_slots = call(
        slot_kernel,
        (rows2, struct((S, wide)), struct((128, 128)), struct((128, 128))),
        in_specs=[VM] * 9,
        input_output_aliases={4: 2, 5: 3},
        cost_estimate=cost(10**8, 3 * 2**20),
    )

    def iterate(step, state):
        send, e, blk, u, z, u_far, rec, w0, b0, w1, b1 = state[:11]
        got = exchange(send)
        w0, b0, c, tie = run_areas(0, load0, e, w0, b0, z)
        if step is None:
            back, z, u_far, rec, tags_at, inverse = owner_first(got, tie)
        else:
            tags_at, inverse = state[11:]
            at = jnp.asarray(step, jnp.int32).reshape(1)
            back, z, u_far, rec = owner_mid(at, got, tags_at, inverse, tie, z, u_far, rec)
        z_back = exchange(back)
        w1, b1, c, _ = run_areas(HALF, load1, e, w1, b1, z, c)
        send, e, blk, u = run_slots(z_back, place, place_t, live, blk, u, c, bd_high, bd_low)
        return (send, e, blk, u, z, u_far, rec, w0, b0, w1, b1, tags_at, inverse)

    zero = jnp.zeros((HALF, S, K), F32)
    state = (send, e, blk, u, jnp.zeros((N_REGION, 256), F32), None, None, zero, load0, zero, load1)
    state = iterate(None, state)
    state = lax.fori_loop(1, ITERS - 1, iterate, state)
    send, e, blk, u, z, u_far, rec, _, b0, _, b1, tags_at, inverse = state
    got = exchange(send)
    x, tie = run_last(0, e, b0, z)
    back = owner_last(
        jnp.full((1,), ITERS - 1, jnp.int32), got, tags_at, inverse, tie, z, u_far, rec
    )
    z_back = exchange(back)
    x = run_last(HALF, e, b1, back, x)
    duals, record = call(
        close_kernel, (struct((128, 128)), struct((ITERS, 2))), in_specs=[VM] * 5
    )(z_back, place_t, live, blk, u)
    return (x, duals.reshape(AREA, NB, 128), record)


def solution(mesh):
    area_split = (
        P(BOTH, None, None),
        P(BOTH, None, None),
        P(BOTH, None),
        P(BOTH, None),
        P(BOTH, None),
        P(BOTH, None),
        P(BOTH),
    )
    return jax.shard_map(
        on_device,
        mesh=mesh,
        in_specs=area_split,
        out_specs=(P(BOTH, None, None), P(BOTH, None, None), P()),
        check_vma=False,
    )
```

time: 644 us -> 536 us (0.83)
  starting transfers between devices: 216 us -> 150 us
  waiting for transfers between devices: 149 us -> 132 us
  Pallas kernels: 257 us -> 243 us
  local copies, waits for them, and re-layouts: 12.7 us -> 5.69 us
    all_to_all x30 -> x28, starting transfers between devices: 216 us -> 150 us  [on_device(): lax.all_to_all(x, BOTH, split_axis=0, concat_axis=0, tiled=True)]
    all_to_all x30 -> x28, waiting for transfers between devices: 149 us -> 132 us  [on_device(): lax.all_to_all(x, BOTH, split_axis=0, concat_axis=0, tiled=True)]
    pallas_call x45 -> x58, Pallas kernels: 256 us -> 242 us  [the longest x26 141 us: run_areas(): call(functools.partial(area_kernel, first), (part_shape, part_shape, stru...]
  transfers between devices with their start and end apart: 30 -> 28, of which waited for: 15 -> 28; matrix products, arithmetic and copies ran while one was open for 1% -> 0% of each run, Pallas kernels for 29% -> 28%
where the time goes in v2:
time: 536 us; the launch traced here: 532 us
  Pallas kernels  243 us (45%)
  starting transfers between devices  150 us (28%)
  waiting for transfers between devices  132 us (25%)
  local copies, waits for them, and re-layouts  5.69 us (1%)
    all_to_all x28, starting transfers between devices, on_device(): lax.all_to_all(x, BOTH, split_axis=0, concat_axis=0, tiled=True)  150 us
    pallas_call x26, Pallas kernels, run_areas(): call(functools.partial(area_kernel, first), (part_shape, part_shape, stru...  141 us
    all_to_all x28, waiting for transfers between devices, on_device(): lax.all_to_all(x, BOTH, split_axis=0, concat_axis=0, tiled=True)  132 us
    pallas_call x13, Pallas kernels, iterate(): run_slots(z_back, place, place_t, live, blk, u, c, bd_high, bd_low)  35.9 us
    pallas_call x12, Pallas kernels, iterate(): owner_mid(at, got, tags_at, inverse, tie, z, u_far, rec)  30.6 us
    pallas_call x1, Pallas kernels, on_device(): call(setup_kernel, (struct((AREA, K, K), BF16), struct((AREA, K)), struct...  18.2 us
  transfers between devices with their start and end apart: 28, of which 28 were waited for; matrix products, arithmetic and copies ran while one was open for 0% of the time, Pallas kernels for 28%

profile of v2, /device:TPU:1, one launch (start us, length us, event | category | flops | bytes accessed | tf_op | source)
XLA Modules:
  0.0 532.0 jit_solution(6554563746523096471)
XLA Ops:
  6.9 18.2 %shard_map.94 = (bf16[8,1024,1024]{2,1,0:T(8,128)(2,1)}, f32[8,1024]{1,0:T(8,128)S(1)}, f32[32,512]{1,0:T(8,128)S(1)}, bf16[512,512]{1,0:T(8,128)(2,1)}, bf16[51...) custom-call(bf16[8,1024,1024]{2,1,0:T(8,128)(2,1)} %f_ref.1, ...), custom_call_target="tpu_custom_call" | custom-call | flops 8000000000 | bytes 35651584 | tf_op jit(solution)/shard_map/pallas_call | solution.py:474
  26.0 11.5 %all-to-all-start.2 = ((f32[128,4,128]{2,1,0:T(4,128)}), f32[128,4,128]{2,1,0:T(4,128)S(1)}, u32[]{:S(2)}, u32[]{:S(2)}) async-start(f32[128,4,128]{2,1,0:T(4,128)} %bitcast.6), calls=%async_computation.2 | async-start | bytes 524288 | tf_op jit(solution)/shard_map/all_to_all | solution.py:464
  42.0 6.7 %all-to-all-done.2 = f32[128,4,128]{2,1,0:T(4,128)S(1)} async-done(((f32[128,4,128]{2,1,0:T(4,128)}), f32[128,4,128]{2,1,0:T(4,128)S(1)}, u32[]{:S(2)}, u32[]{:S(2)}) %all-to-all-start.2) | async-done | bytes 262176 | tf_op jit(solution)/shard_map/all_to_all | solution.py:464
  54.8 5.7 %shard_map.99 = (f32[4,32,1024]{2,1,0:T(8,128)S(1)}, f32[4,32,1024]{2,1,0:T(8,128)S(1)}, f32[32,512]{1,0:T(8,128)S(1)}, f32[8,128]{1,0:T(8,128)}) custom-call(bf16[8,1024,1024]{2,1,0:T(8,128)(2,1)} %get-tuple-element.717.m_ref, f32[8,1024]{1,0:T(8,128)S(1)} %get-tuple-element.718.diag_ref, ...), custom_call_target="tpu_custom_call", output_to_operand_aliasing={{0}: (6, {}), {1}: (7, {})} | custom-call | flops 400000000 | bytes 10485760 | tf_op jit(solution)/shard_map/pallas_call | solution.py:510
  67.6 429.7 %while.33 = (s32[]{:T(128)}, f32[256,128]{1,0:T(8,128)}, f32[32,512]{1,0:T(8,128)S(1)}, f32[128,128]{1,0:T(8,128)}, f32[128,128]{1,0:T(8,128)}, /*index=5*/f32[8...) while((s32[]{:T(128)}, f32[256,128]{1,0:T(8,128)}, ...), condition=%wide.region_1.0_spmd, body=%wide.region_0.0_spmd.sunk | while | flops 910000000 | bytes 25952548 | solution.py:583
  67.6 5.6 %all-to-all-start = ((f32[128,2,128]{2,1,0:T(2,128)}), f32[128,2,128]{2,1,0:T(2,128)S(1)}, u32[]{:S(2)}, u32[]{:S(2)}) async-start(f32[128,2,128]{2,1,0:T(2,128)} %bitcast.31), calls=%async_computation | async-start | bytes 262144 | tf_op jit(solution)/shard_map/while/body/eval_jaxpr/all_to_all | solution.py:464
  73.1 5.2 eval_jaxpr.20
  78.3 4.9 all-to-all-done
  85.8 4.9 all-to-all-start.1
  90.7 5.7 %eval_jaxpr.22 = (f32[4,32,1024]{2,1,0:T(8,128)S(1)}, f32[4,32,1024]{2,1,0:T(8,128)S(1)}, f32[32,512]{1,0:T(8,128)S(1)}, f32[8,128]{1,0:T(8,128)}) custom-call(bf16[8,1024,1024]{2,1,0:T(8,128)(2,1)} %get-tuple-element.769.m_ref, f32[8,1024]{1,0:T(8,128)S(1)} %get-tuple-element.770.diag_ref, ...), custom_call_target="tpu_custom_call", output_to_operand_aliasing={{0}: (6, {}), {1}: (7, {})} | custom-call | flops 400000000 | bytes 10485760 | tf_op jit(solution)/shard_map/while/body/eval_jaxpr/pallas_call | solution.py:510
  103.5 5.5 %all-to-all-start = ((f32[128,2,128]{2,1,0:T(2,128)}), f32[128,2,128]{2,1,0:T(2,128)S(1)}, u32[]{:S(2)}, u32[]{:S(2)}) async-start(f32[128,2,128]{2,1,0:T(2,128)} %bitcast.31), calls=%async_computation | async-start | bytes 262144 | tf_op jit(solution)/shard_map/while/body/eval_jaxpr/all_to_all | solution.py:464
  108.9 5.2 eval_jaxpr.20
  114.1 4.9 all-to-all-done
  121.5 4.9 all-to-all-start.1
  126.4 5.7 %eval_jaxpr.22 = (f32[4,32,1024]{2,1,0:T(8,128)S(1)}, f32[4,32,1024]{2,1,0:T(8,128)S(1)}, f32[32,512]{1,0:T(8,128)S(1)}, f32[8,128]{1,0:T(8,128)}) custom-call(bf16[8,1024,1024]{2,1,0:T(8,128)(2,1)} %get-tuple-element.769.m_ref, f32[8,1024]{1,0:T(8,128)S(1)} %get-tuple-element.770.diag_ref, ...), custom_call_target="tpu_custom_call", output_to_operand_aliasing={{0}: (6, {}), {1}: (7, {})} | custom-call | flops 400000000 | bytes 10485760 | tf_op jit(solution)/shard_map/while/body/eval_jaxpr/pallas_call | solution.py:510
  139.3 5.5 %all-to-all-start = ((f32[128,2,128]{2,1,0:T(2,128)}), f32[128,2,128]{2,1,0:T(2,128)S(1)}, u32[]{:S(2)}, u32[]{:S(2)}) async-start(f32[128,2,128]{2,1,0:T(2,128)} %bitcast.31), calls=%async_computation | async-start | bytes 262144 | tf_op jit(solution)/shard_map/while/body/eval_jaxpr/all_to_all | solution.py:464
  144.7 5.2 eval_jaxpr.20
  149.9 4.9 all-to-all-done
  157.3 4.9 all-to-all-start.1
  162.2 5.7 %eval_jaxpr.22 = (f32[4,32,1024]{2,1,0:T(8,128)S(1)}, f32[4,32,1024]{2,1,0:T(8,128)S(1)}, f32[32,512]{1,0:T(8,128)S(1)}, f32[8,128]{1,0:T(8,128)}) custom-call(bf16[8,1024,1024]{2,1,0:T(8,128)(2,1)} %get-tuple-element.769.m_ref, f32[8,1024]{1,0:T(8,128)S(1)} %get-tuple-element.770.diag_ref, ...), custom_call_target="tpu_custom_call", output_to_operand_aliasing={{0}: (6, {}), {1}: (7, {})} | custom-call | flops 400000000 | bytes 10485760 | tf_op jit(solution)/shard_map/while/body/eval_jaxpr/pallas_call | solution.py:510
  175.1 5.5 %all-to-all-start = ((f32[128,2,128]{2,1,0:T(2,128)}), f32[128,2,128]{2,1,0:T(2,128)S(1)}, u32[]{:S(2)}, u32[]{:S(2)}) async-start(f32[128,2,128]{2,1,0:T(2,128)} %bitcast.31), calls=%async_computation | async-start | bytes 262144 | tf_op jit(solution)/shard_map/while/body/eval_jaxpr/all_to_all | solution.py:464
  180.5 5.2 eval_jaxpr.20
  185.7 4.9 all-to-all-done
  193.1 4.9 all-to-all-start.1
  198.0 5.7 %eval_jaxpr.22 = (f32[4,32,1024]{2,1,0:T(8,128)S(1)}, f32[4,32,1024]{2,1,0:T(8,128)S(1)}, f32[32,512]{1,0:T(8,128)S(1)}, f32[8,128]{1,0:T(8,128)}) custom-call(bf16[8,1024,1024]{2,1,0:T(8,128)(2,1)} %get-tuple-element.769.m_ref, f32[8,1024]{1,0:T(8,128)S(1)} %get-tuple-element.770.diag_ref, ...), custom_call_target="tpu_custom_call", output_to_operand_aliasing={{0}: (6, {}), {1}: (7, {})} | custom-call | flops 400000000 | bytes 10485760 | tf_op jit(solution)/shard_map/while/body/eval_jaxpr/pallas_call | solution.py:510
  210.9 5.5 %all-to-all-start = ((f32[128,2,128]{2,1,0:T(2,128)}), f32[128,2,128]{2,1,0:T(2,128)S(1)}, u32[]{:S(2)}, u32[]{:S(2)}) async-start(f32[128,2,128]{2,1,0:T(2,128)} %bitcast.31), calls=%async_computation | async-start | bytes 262144 | tf_op jit(solution)/shard_map/while/body/eval_jaxpr/all_to_all | solution.py:464
  216.3 5.2 eval_jaxpr.20
  221.5 4.9 all-to-all-done
  228.9 4.9 all-to-all-start.1
  233.8 5.7 %eval_jaxpr.22 = (f32[4,32,1024]{2,1,0:T(8,128)S(1)}, f32[4,32,1024]{2,1,0:T(8,128)S(1)}, f32[32,512]{1,0:T(8,128)S(1)}, f32[8,128]{1,0:T(8,128)}) custom-call(bf16[8,1024,1024]{2,1,0:T(8,128)(2,1)} %get-tuple-element.769.m_ref, f32[8,1024]{1,0:T(8,128)S(1)} %get-tuple-element.770.diag_ref, ...), custom_call_target="tpu_custom_call", output_to_operand_aliasing={{0}: (6, {}), {1}: (7, {})} | custom-call | flops 400000000 | bytes 10485760 | tf_op jit(solution)/shard_map/while/body/eval_jaxpr/pallas_call | solution.py:510
  246.7 5.5 %all-to-all-start = ((f32[128,2,128]{2,1,0:T(2,128)}), f32[128,2,128]{2,1,0:T(2,128)S(1)}, u32[]{:S(2)}, u32[]{:S(2)}) async-start(f32[128,2,128]{2,1,0:T(2,128)} %bitcast.31), calls=%async_computation | async-start | bytes 262144 | tf_op jit(solution)/shard_map/while/body/eval_jaxpr/all_to_all | solution.py:464
  252.1 5.2 eval_jaxpr.20
  257.3 4.9 all-to-all-done
  264.7 4.9 all-to-all-start.1
  269.6 5.7 %eval_jaxpr.22 = (f32[4,32,1024]{2,1,0:T(8,128)S(1)}, f32[4,32,1024]{2,1,0:T(8,128)S(1)}, f32[32,512]{1,0:T(8,128)S(1)}, f32[8,128]{1,0:T(8,128)}) custom-call(bf16[8,1024,1024]{2,1,0:T(8,128)(2,1)} %get-tuple-element.769.m_ref, f32[8,1024]{1,0:T(8,128)S(1)} %get-tuple-element.770.diag_ref, ...), custom_call_target="tpu_custom_call", output_to_operand_aliasing={{0}: (6, {}), {1}: (7, {})} | custom-call | flops 400000000 | bytes 10485760 | tf_op jit(solution)/shard_map/while/body/eval_jaxpr/pallas_call | solution.py:510
  282.5 5.5 %all-to-all-start = ((f32[128,2,128]{2,1,0:T(2,128)}), f32[128,2,128]{2,1,0:T(2,128)S(1)}, u32[]{:S(2)}, u32[]{:S(2)}) async-start(f32[128,2,128]{2,1,0:T(2,128)} %bitcast.31), calls=%async_computation | async-start | bytes 262144 | tf_op jit(solution)/shard_map/while/body/eval_jaxpr/all_to_all | solution.py:464
  287.9 5.2 eval_jaxpr.20
  293.1 4.9 all-to-all-done
  300.5 4.9 all-to-all-start.1
  305.4 5.7 %eval_jaxpr.22 = (f32[4,32,1024]{2,1,0:T(8,128)S(1)}, f32[4,32,1024]{2,1,0:T(8,128)S(1)}, f32[32,512]{1,0:T(8,128)S(1)}, f32[8,128]{1,0:T(8,128)}) custom-call(bf16[8,1024,1024]{2,1,0:T(8,128)(2,1)} %get-tuple-element.769.m_ref, f32[8,1024]{1,0:T(8,128)S(1)} %get-tuple-element.770.diag_ref, ...), custom_call_target="tpu_custom_call", output_to_operand_aliasing={{0}: (6, {}), {1}: (7, {})} | custom-call | flops 400000000 | bytes 10485760 | tf_op jit(solution)/shard_map/while/body/eval_jaxpr/pallas_call | solution.py:510
  318.3 5.5 %all-to-all-start = ((f32[128,2,128]{2,1,0:T(2,128)}), f32[128,2,128]{2,1,0:T(2,128)S(1)}, u32[]{:S(2)}, u32[]{:S(2)}) async-start(f32[128,2,128]{2,1,0:T(2,128)} %bitcast.31), calls=%async_computation | async-start | bytes 262144 | tf_op jit(solution)/shard_map/while/body/eval_jaxpr/all_to_all | solution.py:464
  323.7 5.2 eval_jaxpr.20
  336.3 4.9 all-to-all-start.1
  341.2 5.7 %eval_jaxpr.22 = (f32[4,32,1024]{2,1,0:T(8,128)S(1)}, f32[4,32,1024]{2,1,0:T(8,128)S(1)}, f32[32,512]{1,0:T(8,128)S(1)}, f32[8,128]{1,0:T(8,128)}) custom-call(bf16[8,1024,1024]{2,1,0:T(8,128)(2,1)} %get-tuple-element.769.m_ref, f32[8,1024]{1,0:T(8,128)S(1)} %get-tuple-element.770.diag_ref, ...), custom_call_target="tpu_custom_call", output_to_operand_aliasing={{0}: (6, {}), {1}: (7, {})} | custom-call | flops 400000000 | bytes 10485760 | tf_op jit(solution)/shard_map/while/body/eval_jaxpr/pallas_call | solution.py:510
  354.1 5.5 %all-to-all-start = ((f32[128,2,128]{2,1,0:T(2,128)}), f32[128,2,128]{2,1,0:T(2,128)S(1)}, u32[]{:S(2)}, u32[]{:S(2)}) async-start(f32[128,2,128]{2,1,0:T(2,128)} %bitcast.31), calls=%async_computation | async-start | bytes 262144 | tf_op jit(solution)/shard_map/while/body/eval_jaxpr/all_to_all | solution.py:464
  359.5 5.2 eval_jaxpr.20
  372.1 4.9 all-to-all-start.1
  377.0 5.7 %eval_jaxpr.22 = (f32[4,32,1024]{2,1,0:T(8,128)S(1)}, f32[4,32,1024]{2,1,0:T(8,128)S(1)}, f32[32,512]{1,0:T(8,128)S(1)}, f32[8,128]{1,0:T(8,128)}) custom-call(bf16[8,1024,1024]{2,1,0:T(8,128)(2,1)} %get-tuple-element.769.m_ref, f32[8,1024]{1,0:T(8,128)S(1)} %get-tuple-element.770.diag_ref, ...), custom_call_target="tpu_custom_call", output_to_operand_aliasing={{0}: (6, {}), {1}: (7, {})} | custom-call | flops 400000000 | bytes 10485760 | tf_op jit(solution)/shard_map/while/body/eval_jaxpr/pallas_call | solution.py:510
  389.9 5.5 %all-to-all-start = ((f32[128,2,128]{2,1,0:T(2,128)}), f32[128,2,128]{2,1,0:T(2,128)S(1)}, u32[]{:S(2)}, u32[]{:S(2)}) async-start(f32[128,2,128]{2,1,0:T(2,128)} %bitcast.31), calls=%async_computation | async-start | bytes 262144 | tf_op jit(solution)/shard_map/while/body/eval_jaxpr/all_to_all | solution.py:464
  395.3 5.2 eval_jaxpr.20
  407.9 4.9 all-to-all-start.1
  412.8 5.7 %eval_jaxpr.22 = (f32[4,32,1024]{2,1,0:T(8,128)S(1)}, f32[4,32,1024]{2,1,0:T(8,128)S(1)}, f32[32,512]{1,0:T(8,128)S(1)}, f32[8,128]{1,0:T(8,128)}) custom-call(bf16[8,1024,1024]{2,1,0:T(8,128)(2,1)} %get-tuple-element.769.m_ref, f32[8,1024]{1,0:T(8,128)S(1)} %get-tuple-element.770.diag_ref, ...), custom_call_target="tpu_custom_call", output_to_operand_aliasing={{0}: (6, {}), {1}: (7, {})} | custom-call | flops 400000000 | bytes 10485760 | tf_op jit(solution)/shard_map/while/body/eval_jaxpr/pallas_call | solution.py:510
  425.7 5.5 %all-to-all-start = ((f32[128,2,128]{2,1,0:T(2,128)}), f32[128,2,128]{2,1,0:T(2,128)S(1)}, u32[]{:S(2)}, u32[]{:S(2)}) async-start(f32[128,2,128]{2,1,0:T(2,128)} %bitcast.31), calls=%async_computation | async-start | bytes 262144 | tf_op jit(solution)/shard_map/while/body/eval_jaxpr/all_to_all | solution.py:464
  431.1 5.2 eval_jaxpr.20
  443.7 4.9 all-to-all-start.1
  448.6 5.7 %eval_jaxpr.22 = (f32[4,32,1024]{2,1,0:T(8,128)S(1)}, f32[4,32,1024]{2,1,0:T(8,128)S(1)}, f32[32,512]{1,0:T(8,128)S(1)}, f32[8,128]{1,0:T(8,128)}) custom-call(bf16[8,1024,1024]{2,1,0:T(8,128)(2,1)} %get-tuple-element.769.m_ref, f32[8,1024]{1,0:T(8,128)S(1)} %get-tuple-element.770.diag_ref, ...), custom_call_target="tpu_custom_call", output_to_operand_aliasing={{0}: (6, {}), {1}: (7, {})} | custom-call | flops 400000000 | bytes 10485760 | tf_op jit(solution)/shard_map/while/body/eval_jaxpr/pallas_call | solution.py:510
  461.5 5.5 %all-to-all-start = ((f32[128,2,128]{2,1,0:T(2,128)}), f32[128,2,128]{2,1,0:T(2,128)S(1)}, u32[]{:S(2)}, u32[]{:S(2)}) async-start(f32[128,2,128]{2,1,0:T(2,128)} %bitcast.31), calls=%async_computation | async-start | bytes 262144 | tf_op jit(solution)/shard_map/while/body/eval_jaxpr/all_to_all | solution.py:464
  466.9 5.2 eval_jaxpr.20
  479.5 4.9 all-to-all-start.1
  484.4 5.7 %eval_jaxpr.22 = (f32[4,32,1024]{2,1,0:T(8,128)S(1)}, f32[4,32,1024]{2,1,0:T(8,128)S(1)}, f32[32,512]{1,0:T(8,128)S(1)}, f32[8,128]{1,0:T(8,128)}) custom-call(bf16[8,1024,1024]{2,1,0:T(8,128)(2,1)} %get-tuple-element.769.m_ref, f32[8,1024]{1,0:T(8,128)S(1)} %get-tuple-element.770.diag_ref, ...), custom_call_target="tpu_custom_call", output_to_operand_aliasing={{0}: (6, {}), {1}: (7, {})} | custom-call | flops 400000000 | bytes 10485760 | tf_op jit(solution)/shard_map/while/body/eval_jaxpr/pallas_call | solution.py:510
  497.3 5.5 %all-to-all-start.4 = ((f32[128,2,128]{2,1,0:T(2,128)}), f32[128,2,128]{2,1,0:T(2,128)S(1)}, u32[]{:S(2)}, u32[]{:S(2)}) async-start(f32[128,2,128]{2,1,0:T(2,128)} %bitcast.32), calls=%async_computation.4 | async-start | bytes 262144 | tf_op jit(solution)/shard_map/all_to_all | solution.py:464
  507.6 5.2 all-to-all-done.4
  519.1 5.8 %shard_map.103 = f32[8,32,1024]{2,1,0:T(8,128)} custom-call(bf16[8,1024,1024]{2,1,0:T(8,128)(2,1)} %get-tuple-element.789, f32[8,1024]{1,0:T(8,128)S(1)} %get-tuple-element.790, f32[32,512]{1,0:T(8,128)S(1)} %get-tuple-element.458.e_ref, f32[4,32,1024]{2,1,0:T(8,128)S(1)} %get-tuple-element.459.b_in, ...), custom_call_target="tpu_custom_call", output_to_operand_aliasing={{}: (5, {})} | custom-call | flops 400000000 | bytes 10485760 | tf_op jit(solution)/shard_map/pallas_call | solution.py:523
  524.9 5.3 %all-to-all-done.5 = f32[128,4,128]{2,1,0:T(4,128)S(1)} async-done(((f32[128,4,128]{2,1,0:T(4,128)}), f32[128,4,128]{2,1,0:T(4,128)S(1)}, u32[]{:S(2)}, u32[]{:S(2)}) %all-to-all-start.5) | async-done | bytes 262176 | tf_op jit(solution)/shard_map/all_to_all | solution.py:464
  (88 shorter events, 177.7 us)
Async XLA Ops:
  0.6 0.7 copy-start
  1.3 0.7 copy-start.1
  3.4 1.2 copy-start.2
  4.6 0.8 copy-start.3
  5.3 0.8 copy-start.4
  6.1 0.8 copy-start.5
  6.9 35.1 %copy-start.9 = (bf16[128,256]{1,0:T(8,128)(2,1)}, bf16[128,256]{1,0:T(8,128)(2,1)S(1)}, u32[]{:S(2)}) copy-start(bf16[128,256]{1,0:T(8,128)(2,1)S(1)} %get-tuple-element.725.p_ref) | copy-start | bytes 196612
  25.1 29.7 %copy-start.6 = (f32[8,1024]{1,0:T(8,128)}, f32[8,1024]{1,0:T(8,128)S(1)}, u32[]{:S(2)}) copy-start(f32[8,1024]{1,0:T(8,128)S(1)} %get-tuple-element.721.hi_ref) | copy-start | bytes 98308
  26.0 22.7 %all-to-all-start.2 = ((f32[128,4,128]{2,1,0:T(4,128)}), f32[128,4,128]{2,1,0:T(4,128)S(1)}, u32[]{:S(2)}, u32[]{:S(2)}) async-start(f32[128,4,128]{2,1,0:T(4,128)} %bitcast.6), calls=%async_computation.2 | async-start | bytes 524288 | tf_op jit(solution)/shard_map/all_to_all | solution.py:464
  50.4 14.4 %all-to-all-start.3 = ((f32[128,2,128]{2,1,0:T(2,128)}), f32[128,2,128]{2,1,0:T(2,128)S(1)}, u32[]{:S(2)}, u32[]{:S(2)}) async-start(f32[128,2,128]{2,1,0:T(2,128)} %bitcast.8), calls=%async_computation.3 | async-start | bytes 262144 | tf_op jit(solution)/shard_map/all_to_all | solution.py:464
  67.6 15.6 %all-to-all-start = ((f32[128,2,128]{2,1,0:T(2,128)}), f32[128,2,128]{2,1,0:T(2,128)S(1)}, u32[]{:S(2)}, u32[]{:S(2)}) async-start(f32[128,2,128]{2,1,0:T(2,128)} %bitcast.31), calls=%async_computation | async-start | bytes 262144 | tf_op jit(solution)/shard_map/while/body/eval_jaxpr/all_to_all | solution.py:464
  85.8 15.0 %all-to-all-start.1 = ((f32[128,2,128]{2,1,0:T(2,128)}), f32[128,2,128]{2,1,0:T(2,128)S(1)}, u32[]{:S(2)}, u32[]{:S(2)}) async-start(f32[128,2,128]{2,1,0:T(2,128)} %bitcast.23), calls=%async_computation.1 | async-start | bytes 262144 | tf_op jit(solution)/shard_map/while/body/eval_jaxpr/all_to_all | solution.py:464
  103.5 15.5 %all-to-all-start = ((f32[128,2,128]{2,1,0:T(2,128)}), f32[128,2,128]{2,1,0:T(2,128)S(1)}, u32[]{:S(2)}, u32[]{:S(2)}) async-start(f32[128,2,128]{2,1,0:T(2,128)} %bitcast.31), calls=%async_computation | async-start | bytes 262144 | tf_op jit(solution)/shard_map/while/body/eval_jaxpr/all_to_all | solution.py:464
  121.5 15.0 %all-to-all-start.1 = ((f32[128,2,128]{2,1,0:T(2,128)}), f32[128,2,128]{2,1,0:T(2,128)S(1)}, u32[]{:S(2)}, u32[]{:S(2)}) async-start(f32[128,2,128]{2,1,0:T(2,128)} %bitcast.23), calls=%async_computation.1 | async-start | bytes 262144 | tf_op jit(solution)/shard_map/while/body/eval_jaxpr/all_to_all | solution.py:464
  139.3 15.5 %all-to-all-start = ((f32[128,2,128]{2,1,0:T(2,128)}), f32[128,2,128]{2,1,0:T(2,128)S(1)}, u32[]{:S(2)}, u32[]{:S(2)}) async-start(f32[128,2,128]{2,1,0:T(2,128)} %bitcast.31), calls=%async_computation | async-start | bytes 262144 | tf_op jit(solution)/shard_map/while/body/eval_jaxpr/all_to_all | solution.py:464
  157.3 15.0 %all-to-all-start.1 = ((f32[128,2,128]{2,1,0:T(2,128)}), f32[128,2,128]{2,1,0:T(2,128)S(1)}, u32[]{:S(2)}, u32[]{:S(2)}) async-start(f32[128,2,128]{2,1,0:T(2,128)} %bitcast.23), calls=%async_computation.1 | async-start | bytes 262144 | tf_op jit(solution)/shard_map/while/body/eval_jaxpr/all_to_all | solution.py:464
  175.1 15.5 %all-to-all-start = ((f32[128,2,128]{2,1,0:T(2,128)}), f32[128,2,128]{2,1,0:T(2,128)S(1)}, u32[]{:S(2)}, u32[]{:S(2)}) async-start(f32[128,2,128]{2,1,0:T(2,128)} %bitcast.31), calls=%async_computation | async-start | bytes 262144 | tf_op jit(solution)/shard_map/while/body/eval_jaxpr/all_to_all | solution.py:464
  193.1 15.0 %all-to-all-start.1 = ((f32[128,2,128]{2,1,0:T(2,128)}), f32[128,2,128]{2,1,0:T(2,128)S(1)}, u32[]{:S(2)}, u32[]{:S(2)}) async-start(f32[128,2,128]{2,1,0:T(2,128)} %bitcast.23), calls=%async_computation.1 | async-start | bytes 262144 | tf_op jit(solution)/shard_map/while/body/eval_jaxpr/all_to_all | solution.py:464
  210.9 15.5 %all-to-all-start = ((f32[128,2,128]{2,1,0:T(2,128)}), f32[128,2,128]{2,1,0:T(2,128)S(1)}, u32[]{:S(2)}, u32[]{:S(2)}) async-start(f32[128,2,128]{2,1,0:T(2,128)} %bitcast.31), calls=%async_computation | async-start | bytes 262144 | tf_op jit(solution)/shard_map/while/body/eval_jaxpr/all_to_all | solution.py:464
  228.9 15.0 %all-to-all-start.1 = ((f32[128,2,128]{2,1,0:T(2,128)}), f32[128,2,128]{2,1,0:T(2,128)S(1)}, u32[]{:S(2)}, u32[]{:S(2)}) async-start(f32[128,2,128]{2,1,0:T(2,128)} %bitcast.23), calls=%async_computation.1 | async-start | bytes 262144 | tf_op jit(solution)/shard_map/while/body/eval_jaxpr/all_to_all | solution.py:464
  246.7 15.5 %all-to-all-start = ((f32[128,2,128]{2,1,0:T(2,128)}), f32[128,2,128]{2,1,0:T(2,128)S(1)}, u32[]{:S(2)}, u32[]{:S(2)}) async-start(f32[128,2,128]{2,1,0:T(2,128)} %bitcast.31), calls=%async_computation | async-start | bytes 262144 | tf_op jit(solution)/shard_map/while/body/eval_jaxpr/all_to_all | solution.py:464
  264.7 15.0 %all-to-all-start.1 = ((f32[128,2,128]{2,1,0:T(2,128)}), f32[128,2,128]{2,1,0:T(2,128)S(1)}, u32[]{:S(2)}, u32[]{:S(2)}) async-start(f32[128,2,128]{2,1,0:T(2,128)} %bitcast.23), calls=%async_computation.1 | async-start | bytes 262144 | tf_op jit(solution)/shard_map/while/body/eval_jaxpr/all_to_all | solution.py:464
  282.5 15.5 %all-to-all-start = ((f32[128,2,128]{2,1,0:T(2,128)}), f32[128,2,128]{2,1,0:T(2,128)S(1)}, u32[]{:S(2)}, u32[]{:S(2)}) async-start(f32[128,2,128]{2,1,0:T(2,128)} %bitcast.31), calls=%async_computation | async-start | bytes 262144 | tf_op jit(solution)/shard_map/while/body/eval_jaxpr/all_to_all | solution.py:464
  300.5 15.0 %all-to-all-start.1 = ((f32[128,2,128]{2,1,0:T(2,128)}), f32[128,2,128]{2,1,0:T(2,128)S(1)}, u32[]{:S(2)}, u32[]{:S(2)}) async-start(f32[128,2,128]{2,1,0:T(2,128)} %bitcast.23), calls=%async_computation.1 | async-start | bytes 262144 | tf_op jit(solution)/shard_map/while/body/eval_jaxpr/all_to_all | solution.py:464
  318.3 15.5 %all-to-all-start = ((f32[128,2,128]{2,1,0:T(2,128)}), f32[128,2,128]{2,1,0:T(2,128)S(1)}, u32[]{:S(2)}, u32[]{:S(2)}) async-start(f32[128,2,128]{2,1,0:T(2,128)} %bitcast.31), calls=%async_computation | async-start | bytes 262144 | tf_op jit(solution)/shard_map/while/body/eval_jaxpr/all_to_all | solution.py:464
  336.3 15.0 %all-to-all-start.1 = ((f32[128,2,128]{2,1,0:T(2,128)}), f32[128,2,128]{2,1,0:T(2,128)S(1)}, u32[]{:S(2)}, u32[]{:S(2)}) async-start(f32[128,2,128]{2,1,0:T(2,128)} %bitcast.23), calls=%async_computation.1 | async-start | bytes 262144 | tf_op jit(solution)/shard_map/while/body/eval_jaxpr/all_to_all | solution.py:464
  354.1 15.5 %all-to-all-start = ((f32[128,2,128]{2,1,0:T(2,128)}), f32[128,2,128]{2,1,0:T(2,128)S(1)}, u32[]{:S(2)}, u32[]{:S(2)}) async-start(f32[128,2,128]{2,1,0:T(2,128)} %bitcast.31), calls=%async_computation | async-start | bytes 262144 | tf_op jit(solution)/shard_map/while/body/eval_jaxpr/all_to_all | solution.py:464
  372.1 15.0 %all-to-all-start.1 = ((f32[128,2,128]{2,1,0:T(2,128)}), f32[128,2,128]{2,1,0:T(2,128)S(1)}, u32[]{:S(2)}, u32[]{:S(2)}) async-start(f32[128,2,128]{2,1,0:T(2,128)} %bitcast.23), calls=%async_computation.1 | async-start | bytes 262144 | tf_op jit(solution)/shard_map/while/body/eval_jaxpr/all_to_all | solution.py:464
  389.9 15.5 %all-to-all-start = ((f32[128,2,128]{2,1,0:T(2,128)}), f32[128,2,128]{2,1,0:T(2,128)S(1)}, u32[]{:S(2)}, u32[]{:S(2)}) async-start(f32[128,2,128]{2,1,0:T(2,128)} %bitcast.31), calls=%async_computation | async-start | bytes 262144 | tf_op jit(solution)/shard_map/while/body/eval_jaxpr/all_to_all | solution.py:464
  407.9 15.0 %all-to-all-start.1 = ((f32[128,2,128]{2,1,0:T(2,128)}), f32[128,2,128]{2,1,0:T(2,128)S(1)}, u32[]{:S(2)}, u32[]{:S(2)}) async-start(f32[128,2,128]{2,1,0:T(2,128)} %bitcast.23), calls=%async_computation.1 | async-start | bytes 262144 | tf_op jit(solution)/shard_map/while/body/eval_jaxpr/all_to_all | solution.py:464
  425.7 15.5 %all-to-all-start = ((f32[128,2,128]{2,1,0:T(2,128)}), f32[128,2,128]{2,1,0:T(2,128)S(1)}, u32[]{:S(2)}, u32[]{:S(2)}) async-start(f32[128,2,128]{2,1,0:T(2,128)} %bitcast.31), calls=%async_computation | async-start | bytes 262144 | tf_op jit(solution)/shard_map/while/body/eval_jaxpr/all_to_all | solution.py:464
  443.7 15.0 %all-to-all-start.1 = ((f32[128,2,128]{2,1,0:T(2,128)}), f32[128,2,128]{2,1,0:T(2,128)S(1)}, u32[]{:S(2)}, u32[]{:S(2)}) async-start(f32[128,2,128]{2,1,0:T(2,128)} %bitcast.23), calls=%async_computation.1 | async-start | bytes 262144 | tf_op jit(solution)/shard_map/while/body/eval_jaxpr/all_to_all | solution.py:464
  461.5 15.5 %all-to-all-start = ((f32[128,2,128]{2,1,0:T(2,128)}), f32[128,2,128]{2,1,0:T(2,128)S(1)}, u32[]{:S(2)}, u32[]{:S(2)}) async-start(f32[128,2,128]{2,1,0:T(2,128)} %bitcast.31), calls=%async_computation | async-start | bytes 262144 | tf_op jit(solution)/shard_map/while/body/eval_jaxpr/all_to_all | solution.py:464
  479.5 15.0 %all-to-all-start.1 = ((f32[128,2,128]{2,1,0:T(2,128)}), f32[128,2,128]{2,1,0:T(2,128)S(1)}, u32[]{:S(2)}, u32[]{:S(2)}) async-start(f32[128,2,128]{2,1,0:T(2,128)} %bitcast.23), calls=%async_computation.1 | async-start | bytes 262144 | tf_op jit(solution)/shard_map/while/body/eval_jaxpr/all_to_all | solution.py:464
  497.3 15.6 %copy-start.7 = (f32[256,128]{1,0:T(8,128)S(1)}, f32[256,128]{1,0:T(8,128)}, u32[]{:S(2)}) copy-start(f32[256,128]{1,0:T(8,128)} %get-tuple-element.791) | copy-start | bytes 393220
  497.3 15.6 %copy-start.8 = (f32[256,128]{1,0:T(8,128)S(1)}, f32[256,128]{1,0:T(8,128)}, u32[]{:S(2)}) copy-start(f32[256,128]{1,0:T(8,128)} %get-tuple-element.464.refs_6_) | copy-start | bytes 393220
  497.3 15.6 %copy-start.13 = (f32[128,128]{1,0:T(8,128)S(1)}, f32[128,128]{1,0:T(8,128)}, u32[]{:S(2)}) copy-start(f32[128,128]{1,0:T(8,128)} %get-tuple-element.465.refs_7_) | copy-start | bytes 196612
  497.3 15.5 %all-to-all-start.4 = ((f32[128,2,128]{2,1,0:T(2,128)}), f32[128,2,128]{2,1,0:T(2,128)S(1)}, u32[]{:S(2)}, u32[]{:S(2)}) async-start(f32[128,2,128]{2,1,0:T(2,128)} %bitcast.32), calls=%async_computation.4 | async-start | bytes 262144 | tf_op jit(solution)/shard_map/all_to_all | solution.py:464
  502.7 27.5 %copy-start.10 = (bf16[256,128]{1,0:T(8,128)(2,1)S(1)}, bf16[256,128]{1,0:T(8,128)(2,1)}, u32[]{:S(2)}) copy-start(bf16[256,128]{1,0:T(8,128)(2,1)} %get-tuple-element.796) | copy-start | bytes 196612
  502.8 27.5 %copy-start.11 = (f32[128,128]{1,0:T(8,128)S(1)}, f32[128,128]{1,0:T(8,128)}, u32[]{:S(2)}) copy-start(f32[128,128]{1,0:T(8,128)} %get-tuple-element.467.blk_in) | copy-start | bytes 196612
  502.8 27.5 %copy-start.12 = (f32[128,128]{1,0:T(8,128)S(1)}, f32[128,128]{1,0:T(8,128)}, u32[]{:S(2)}) copy-start(f32[128,128]{1,0:T(8,128)} %get-tuple-element.468.u_in) | copy-start | bytes 196612
  502.8 27.5 %copy-start.14 = (f32[1,128]{1,0:T(1,128)S(1)}, f32[1,128]{1,0:T(1,128)}, u32[]{:S(2)}) copy-start(f32[1,128]{1,0:T(1,128)} %get-tuple-element.798) | copy-start | bytes 1540
  514.4 15.8 %all-to-all-start.5 = ((f32[128,4,128]{2,1,0:T(4,128)}), f32[128,4,128]{2,1,0:T(4,128)S(1)}, u32[]{:S(2)}, u32[]{:S(2)}) async-start(f32[128,4,128]{2,1,0:T(4,128)} %bitcast.12), calls=%async_computation.5 | async-start | bytes 524288 | tf_op jit(solution)/shard_map/all_to_all | solution.py:464

commit v3 on v2

--- a/solution.py
+++ b/solution.py
@@ -68,7 +68,7 @@
 
 SMEM = pl.BlockSpec(memory_space=pltpu.SMEM)
 VM = pl.BlockSpec(memory_space=pltpu.VMEM)
-ANY = pl.BlockSpec(memory_space=pl.ANY)
+HBM = pl.BlockSpec(memory_space=pltpu.HBM)
 
 
 def call(kernel, out_shape, limit=16, **kw):
@@ -173,7 +173,7 @@
             tag_ref[near_rows(2, d), :] = near_tags[d]
         for r in range(N_REGION):
             tag_ref[far_rows(2, r), :] = far_tags[r]
-        rec_ref[...] = jnp.zeros((128, 128), F32)
+        rec_ref[...] = jnp.zeros((32, 128), F32)
         step = 0
     else:
         if last:
@@ -229,10 +229,11 @@
         if not last:
             u_ref[far_rows(2, region), :] = u
     primal = jnp.sum(primal, axis=0, keepdims=True) * (1.0 / CELLS)
-    row = iota((128, 128), 0)
+    row = iota((32, 128), 0)
     if last:
         rec = jnp.where(row == step, primal, rec_in[...])
         rec = jnp.where(row == 16 + step, dual, rec)
+        rec = jnp.concatenate([rec, jnp.zeros((96, 128), F32)], axis=0)
         sums = jnp.sum(jnp.transpose(rec), axis=0, keepdims=True)
         out_ref[pl.ds(2, WORLD, stride=4), :] = jnp.broadcast_to(sums, (WORLD, 128))
         out_ref[pl.ds(3, WORLD, stride=4), :] = jnp.zeros((WORLD, 128), F32)
@@ -252,12 +253,11 @@
     return jnp.concatenate([lanes[:, ITEMS * r : ITEMS * r + ITEMS] for r in range(ROWS)], axis=0)
 
 
-def open_kernel(c_ref, p_ref, tag_ref, send_ref, e_ref, blk_ref, u_ref):
-    blk = by_row(c_ref[...])
-    blk_ref[...] = blk
-    u_ref[...] = jnp.zeros_like(blk)
+def open_kernel(c_ref, p_ref, tag_ref, send_ref, e_ref, val_ref):
+    val = by_row(c_ref[...])
+    val_ref[...] = val
     e_ref[...] = jnp.zeros((S, ROWS * ITEMS), F32)
-    send = pick(blk, p_ref[...])
+    send = pick(val, p_ref[...])
     send_ref[pl.ds(0, WORLD, stride=4), :] = send[:, :128]
     send_ref[pl.ds(1, WORLD, stride=4), :] = send[:, 128:]
     send_ref[pl.ds(2, WORLD, stride=4), :] = jnp.broadcast_to(tag_ref[0:1, :], (WORLD, 128))
@@ -271,36 +271,32 @@
 
 
 def slot_kernel(
-    z_ref, p_ref, pt_ref, live_ref, blk_in, u_in, c_ref, bdh_ref, bdl_ref,
-    send_ref, e_ref, blk_ref, u_ref,
+    z_ref, p_ref, pt_ref, live_ref, val_in, c_ref, bd_ref, bdiag_ref, send_ref, e_ref, val_ref
 ):
     z_slot = take_means(z_ref, pt_ref, 2)
-    u = u_in[...] + (blk_in[...] - z_slot) * live_ref[...]
-    u_ref[...] = u
+    u = val_in[...] * live_ref[...] - z_slot
     e = by_lane(RHO * (z_slot - u))
     e_ref[...] = e
     e_high = e.astype(BF16)
     e_low = (e - e_high.astype(F32)).astype(BF16)
-    both = dot(jnp.concatenate([e_high, e_low], axis=0), bdh_ref[...])
-    edge = c_ref[...] + both[:S] + both[S:] + dot(e_high, bdl_ref[...])
-    blk = by_row(edge)
-    blk_ref[...] = blk
-    send = pick(blk + u, p_ref[...])
+    both = dot(jnp.concatenate([e_high, e_low], axis=0), bd_ref[...])
+    edge = c_ref[...] + e * bdiag_ref[...] + both[:S] + both[S:]
+    val = by_row(edge) + u
+    val_ref[...] = val
+    send = pick(val, p_ref[...])
     send_ref[pl.ds(0, WORLD, stride=2), :] = send[:, :128]
     send_ref[pl.ds(1, WORLD, stride=2), :] = send[:, 128:]
 
 
-def close_kernel(z_ref, pt_ref, live_ref, blk_in, u_in, dual_ref, record_ref):
+def close_kernel(z_ref, pt_ref, live_ref, val_in, dual_ref, record_ref):
     z_slot = take_means(z_ref, pt_ref, 4)
-    u = u_in[...] + (blk_in[...] - z_slot) * live_ref[...]
+    u = val_in[...] * live_ref[...] - z_slot
     old = iota((128, 128), 0)
     order = jnp.where(iota((128, 128), 1) == (old & 31) * ROWS + (old >> 5), 1.0, 0.0)
     dual_ref[...] = pick(jnp.transpose(u), order.astype(BF16))
     sums = jnp.sum(z_ref[pl.ds(2, WORLD, stride=4), :], axis=0, keepdims=True)
-    column = jnp.transpose(jnp.broadcast_to(sums, (128, 128)))
-    first = iota((16, 128), 1) == 0
-    both = jnp.where(first, column[:16], column[16:32])
-    record_ref[...] = both[:ITERS, :2]
+    both = jnp.concatenate([sums, pltpu.roll(sums, 112, 1)], axis=0)
+    record_ref[...] = both[:, :ITERS]
 
 
 def edge_part(right_side, m_edge, diag_edge):
@@ -308,11 +304,26 @@
 
 
 def setup_kernel(
-    f_ref, p_ref, load_ref, lo_ref, hi_ref,
-    m_ref, diag_ref, c_ref, bdh_ref, bdl_ref, load0_ref, load1_ref, lo_out, hi_out, ft, g,
+    f_ref, p_hbm, load_hbm, lo_hbm, hi_hbm,
+    m_ref, diag_ref, c_ref, bd_ref, bdiag_ref, load_out, lo_out, hi_out,
+    ft, g, p_ref, loads, lo_ref, hi_ref, sem,
 ):
     area = pl.program_id(0)
     order = edge_order()
+    fetch = [
+        pltpu.make_async_copy(source, target, sem.at[n])
+        for n, (source, target) in enumerate(
+            ((p_hbm, p_ref), (load_hbm, loads), (lo_hbm, lo_ref), (hi_hbm, hi_ref))
+        )
+    ]
+
+    @pl.when(area == 0)
+    def _():
+        for copy in fetch:
+            copy.start()
+        for copy in fetch:
+            copy.wait()
+
     piv = p_ref[pl.ds(area, 1), :]
     piv_col = jnp.transpose(jnp.broadcast_to(piv, (128, K)))
     step = 256
@@ -344,7 +355,7 @@
         block = jnp.where(eye, 0.0, block)
         if i == 0:
             edge_diag = diag[:, :128]
-            edge_m = jnp.where(eye, diag, block)[:EDGE, :128]
+            edge_m = block[:EDGE, :128]
         m_ref[0, at, at] = block.astype(BF16)
         if i:
             above = column[: i * step].astype(BF16)
@@ -356,44 +367,52 @@
         for r_in in range(ROWS):
             rows = edge_m[NB * r_in : NB * r_in + NB]
             rows = jnp.where(mine, pltpu.roll(rows, shift, 1), 0.0)
-            high = rows.astype(BF16)
             at = pl.ds(pl.multiple_of(ITEMS * r_in + NB * area, NB), NB)
-            bdh_ref[at, ITEMS * r : ITEMS * r + ITEMS] = high
-            bdl_ref[at, ITEMS * r : ITEMS * r + ITEMS] = (rows - high.astype(F32)).astype(BF16)
-    load = load_ref[0]
+            bd_ref[at, ITEMS * r : ITEMS * r + ITEMS] = rows.astype(BF16)
+    load = loads[area]
     load = jnp.concatenate([pick(load[:, :128], order), load[:, 128:]], axis=1)
+    load_out[0] = load
     c = edge_part(load, m_ref[0, :, :128], edge_diag)
 
     @pl.when(area == 0)
     def _():
         c_ref[...] = jnp.zeros_like(c_ref)
+        bdiag_ref[...] = jnp.zeros_like(bdiag_ref)
         for source, out in ((lo_ref, lo_out), (hi_ref, hi_out)):
             out[:, :128] = pick(source[:, :128], order)
             out[:, 128:] = source[:, 128:]
-
-    @pl.when(area < HALF)
-    def _():
-        load0_ref[0] = load
-
-    @pl.when(area >= HALF)
-    def _():
-        load1_ref[0] = load
 
     lane_mine = (iota((S, 128), 1) >> 4) == area
     for r in range(ROWS):
         at = slice(ITEMS * r, ITEMS * r + ITEMS)
         moved = pltpu.roll(c, lax.rem(area * NB + (128 - r * NB), 128), 1)
         c_ref[:, at] = jnp.where(lane_mine, moved, c_ref[:, at])
-
-
-def load_matrices(m_ref, first, buf, sem):
-    copies = [pltpu.make_async_copy(m_ref.at[first + q], buf.at[q], sem.at[q]) for q in range(HALF)]
-    for copy in copies:
-        copy.start()
+        moved = pltpu.roll(edge_diag, lax.rem(area * NB + (128 - r * NB), 128), 1)
+        bdiag_ref[:, at] = jnp.where(lane_mine[:1], moved, bdiag_ref[:, at])
+
+
+def fetch_areas(first, m_ref, buf, sem):
+    half = K // 2
+    copies = [
+        [
+            pltpu.make_async_copy(
+                m_ref.at[first + q, pl.ds(half * n, half)],
+                buf.at[q, pl.ds(half * n, half)],
+                sem.at[q, n],
+            )
+            for n in range(2)
+        ]
+        for q in range(HALF)
+    ]
+    for group in copies:
+        for copy in group:
+            copy.start()
     return copies
 
 
-def right_side_of(b_in, e_ref, q, area):
+def product(first, q, copies, buf, load_ref, diag_ref, lo_ref, hi_ref, e_ref, moved_in):
+    area = first + q
+    at = slice(area, area + 1)
     group = iota((S, 128), 1) >> 4
     part = jnp.zeros((S, 128), F32)
     for r in range(ROWS):
@@ -402,61 +421,74 @@
         if shift:
             piece = pltpu.roll(piece, shift, 1)
         part = jnp.where(group == r, piece, part)
-    base = b_in[q]
-    return jnp.concatenate([base[:, :128] + part, base[:, 128:]], axis=1)
-
-
-def area_kernel(first, m_ref, diag_ref, load_ref, lo_ref, hi_ref, e_ref, w_in, b_in, tie_ref, *refs):
+    moved = moved_in[q]
+    y = jnp.clip(moved, lo_ref[at, :], hi_ref[at, :])
+    w = moved - y
+    base = load_ref[area] + SIGMA * (y - w)
+    side = jnp.concatenate([base[:, :128] + part, base[:, 128:]], axis=1)
+    rounded = side.astype(BF16)
+    half = K // 2
+    copies[q][0].wait()
+    x = side * diag_ref[at, :] + dot(rounded[:, :half], buf[q, :half])
+    copies[q][1].wait()
+    return x + dot(rounded[:, half:], buf[q, half:]), w
+
+
+def area_kernel(
+    first, m_ref, load_ref, diag_ref, lo_ref, hi_ref, e_ref, moved_in, tie_ref, *refs
+):
     if first:
-        c_in, w_ref, b_ref, c_ref, tie_out, buf, sem = refs
+        c_in, moved_ref, c_ref, buf, sem = refs
     else:
-        w_ref, b_ref, c_ref, tie_out, buf, sem = refs
-    copies = load_matrices(m_ref, first, buf, sem)
-    sides = [right_side_of(b_in, e_ref, q, first + q) for q in range(HALF)]
+        moved_ref, c_ref, tie_out, buf, sem = refs
+    copies = fetch_areas(first, m_ref, buf, sem)
+    group = iota((S, 128), 1) >> 4
+    edges = [
+        c_in[:, ITEMS * r : ITEMS * r + ITEMS] if first else jnp.zeros((S, 128), F32)
+        for r in range(ROWS)
+    ]
     news = []
-    for q in range(HALF):
-        at = slice(first + q, first + q + 1)
-        copies[q].wait()
-        x = dot(sides[q].astype(BF16), buf[q]) + sides[q] * diag_ref[at, :]
-        moved = x + w_in[q]
-        y = jnp.clip(moved, lo_ref[at, :], hi_ref[at, :])
-        w = moved - y
-        w_ref[q] = w
-        b = load_ref[q] + SIGMA * (y - w)
-        b_ref[q] = b
-        news.append(b)
-    group = iota((S, 128), 1) >> 4
-    edges = [c_in[:, ITEMS * r : ITEMS * r + ITEMS] if first else jnp.zeros((S, 128), F32) for r in range(ROWS)]
-    for q in range(HALF):
-        area = first + q
-        c = edge_part(news[q], buf[q, :, :128], diag_ref[area : area + 1, :128])
-        for r in range(ROWS):
-            shift = (NB * (area - r)) % 128
-            moved = pltpu.roll(c, shift, 1) if shift else c
-            edges[r] = jnp.where(group == area, moved, edges[r])
+    for q in range(HALF + 1):
+        if q < HALF:
+            at = slice(first + q, first + q + 1)
+            x, w = product(first, q, copies, buf, load_ref, diag_ref, lo_ref, hi_ref, e_ref, moved_in)
+            moved = x + w
+            moved_ref[q] = moved
+            y = jnp.clip(moved, lo_ref[at, :], hi_ref[at, :])
+            news.append(load_ref[first + q] + SIGMA * (y - (moved - y)))
+        if q > 0:
+            area = first + q - 1
+            diag = diag_ref[area : area + 1, :128]
+            c = edge_part(news[q - 1], buf[q - 1, :, :128], diag)
+            for r in range(ROWS):
+                shift = (NB * (area - r)) % 128
+                turned = pltpu.roll(c, shift, 1) if shift else c
+                edges[r] = jnp.where(group == area, turned, edges[r])
     for r in range(ROWS):
         c_ref[:, ITEMS * r : ITEMS * r + ITEMS] = edges[r]
-    tie_out[...] = edges[0][:8]
-
-
-def last_kernel(first, m_ref, diag_ref, e_ref, b_in, tie_ref, *refs):
+    if not first:
+        tie_out[...] = edges[0][:8]
+
+
+def last_kernel(
+    first, m_ref, load_ref, diag_ref, lo_ref, hi_ref, e_ref, moved_in, tie_ref, *refs
+):
     if first:
         _, x_ref, buf, sem, x_buf, x_sem = refs
     else:
         x_ref, tie_out, buf, sem, x_buf, x_sem = refs
-    copies = load_matrices(m_ref, first, buf, sem)
+    copies = fetch_areas(first, m_ref, buf, sem)
     order = edge_order(True)
+    writes = []
     for q in range(HALF):
-        area = first + q
-        side = right_side_of(b_in, e_ref, q, area)
-        copies[q].wait()
-        x = dot(side.astype(BF16), buf[q]) + side * diag_ref[area : area + 1, :]
+        x, _ = product(first, q, copies, buf, load_ref, diag_ref, lo_ref, hi_ref, e_ref, moved_in)
         x_buf[q] = jnp.concatenate([pick(x[:, :128], order), x[:, 128:]], axis=1)
-    copy = pltpu.make_async_copy(x_buf, x_ref.at[pl.ds(first, HALF)], x_sem)
-    copy.start()
+        writes.append(pltpu.make_async_copy(x_buf.at[q], x_ref.at[first + q], x_sem.at[q]))
+        writes[-1].start()
     if not first:
         tie_out[...] = jnp.zeros((8, 128), F32)
-    copy.wait()
+    for copy in writes:
+        copy.wait()
 
 
 def on_device(loads, factor, pivots, lower, upper, incidence, counts):
@@ -471,69 +503,78 @@
 
     area_block = lambda rows: pl.BlockSpec((1, rows, K), lambda a: (a, 0, 0))
     whole = lambda *shape: pl.BlockSpec(shape, lambda a: (0,) * len(shape))
-    matrix, diag, c_now, bd_high, bd_low, load0, load1, floor_box, ceil_box = call(
+    matrix, diag, c_now, bd, bd_diag, load, floor_box, ceil_box = call(
         setup_kernel,
         (
             struct((AREA, K, K), BF16),
             struct((AREA, K)),
             struct((S, wide)),
             struct((wide, wide), BF16),
-            struct((wide, wide), BF16),
-            struct((HALF, S, K)),
-            struct((HALF, S, K)),
+            struct((1, wide)),
+            struct((AREA, S, K)),
             struct((AREA, K)),
             struct((AREA, K)),
         ),
         grid=(AREA,),
-        in_specs=[area_block(K), whole(AREA, K), area_block(S), whole(AREA, K), whole(AREA, K)],
+        in_specs=[area_block(K), HBM, HBM, HBM, HBM],
         out_specs=(
-            area_block(K), whole(AREA, K), whole(S, wide), whole(wide, wide), whole(wide, wide),
-            pl.BlockSpec((1, S, K), lambda a: (jnp.minimum(a, HALF - 1), 0, 0)),
-            pl.BlockSpec((1, S, K), lambda a: (jnp.maximum(a - HALF, 0), 0, 0)),
-            whole(AREA, K), whole(AREA, K),
+            area_block(K), whole(AREA, K), whole(S, wide), whole(wide, wide), whole(1, wide),
+            area_block(S), whole(AREA, K), whole(AREA, K),
         ),
-        scratch_shapes=[pltpu.VMEM((K, K), BF16), pltpu.VMEM((K, K), BF16)],
+        scratch_shapes=[
+            pltpu.VMEM((K, K), BF16),
+            pltpu.VMEM((K, K), BF16),
+            pltpu.VMEM((AREA, K), F32),
+            pltpu.VMEM((AREA, S, K), F32),
+            pltpu.VMEM((AREA, K), F32),
+            pltpu.VMEM((AREA, K), F32),
+            pltpu.SemaphoreType.DMA((4,)),
+        ],
         cost_estimate=cost(8 * 10**9, 34 * 2**20),
-        limit=40,
+        limit=60,
     )(factor, pivots, loads, lower, upper)
 
-    send, e, blk, u = call(
+    send, e, val = call(
         open_kernel,
-        (struct((512, 128)), struct((S, wide)), struct((128, 128)), struct((128, 128))),
+        (struct((512, 128)), struct((S, wide)), struct((128, 128))),
         in_specs=[VM] * 3,
     )(c_now, place, tags)
 
     part_shape = struct((HALF, S, K))
-    matrix_scratch = [pltpu.VMEM((HALF, K, K), BF16), pltpu.SemaphoreType.DMA((HALF,))]
-
-    def run_areas(first, load, e, w, b, tie, c=None):
+    scratch = [
+        pltpu.VMEM((HALF, K, K), BF16),
+        pltpu.SemaphoreType.DMA((HALF, 2)),
+    ]
+
+    def run_areas(first, e, moved, tie, c=None):
         return call(
             functools.partial(area_kernel, first),
-            (part_shape, part_shape, struct((S, wide)), struct((8, 128))),
-            in_specs=[ANY] + [VM] * (9 if first else 8),
-            out_specs=(VM,) * 4,
-            scratch_shapes=matrix_scratch,
-            input_output_aliases={6: 0, 7: 1},
+            (part_shape, struct((S, wide))) + (() if first else (struct((8, 128)),)),
+            in_specs=[HBM] + [VM] * (8 if first else 7),
+            out_specs=(VM,) * (2 if first else 3),
+            scratch_shapes=scratch,
+            input_output_aliases={6: 0},
             cost_estimate=cost(4 * 10**8, 10 * 2**20),
             limit=20,
-        )(matrix, diag, load, floor_box, ceil_box, e, w, b, tie, *((c,) if first else ()))
-
-    def run_last(first, e, b, tie, x=None):
+        )(matrix, load, diag, floor_box, ceil_box, e, moved, tie, *((c,) if first else ()))
+
+    def run_last(first, e, moved, tie, x=None):
         x_shape = struct((AREA, S, K))
         return call(
             functools.partial(last_kernel, first),
             x_shape if first else (x_shape, struct((8, 128))),
-            in_specs=[ANY, VM, VM, VM, VM] + ([ANY] if first else []),
-            out_specs=ANY if first else (ANY, VM),
-            scratch_shapes=matrix_scratch + [pltpu.VMEM((HALF, S, K), F32), pltpu.SemaphoreType.DMA],
-            input_output_aliases={5: 0} if first else {},
+            in_specs=[HBM] + [VM] * 7 + ([HBM] if first else []),
+            out_specs=HBM if first else (HBM, VM),
+            scratch_shapes=scratch
+            + [pltpu.VMEM((HALF, S, K), F32), pltpu.SemaphoreType.DMA((HALF,))],
+            input_output_aliases={8: 0} if first else {},
             cost_estimate=cost(4 * 10**8, 10 * 2**20),
             limit=20,
-        )(matrix, diag, e, b, tie, *((x,) if first else ()))
+        )(matrix, load, diag, floor_box, ceil_box, e, moved, tie, *((x,) if first else ()))
 
     z_shape = struct((N_REGION, 256))
     rows2 = struct((256, 128))
-    rec_shape = struct((128, 128))
+    rec_shape = struct((32, 128))
     small = cost(10**7, 2**20)
     owner_first = call(
         functools.partial(owner_kernel, True, False),
@@ -556,43 +597,43 @@
     )
     run_slots = call(
         slot_kernel,
-        (rows2, struct((S, wide)), struct((128, 128)), struct((128, 128))),
-        in_specs=[VM] * 9,
-        input_output_aliases={4: 2, 5: 3},
+        (rows2, struct((S, wide)), struct((128, 128))),
+        in_specs=[VM] * 8,
+        input_output_aliases={4: 2},
         cost_estimate=cost(10**8, 3 * 2**20),
     )
 
     def iterate(step, state):
-        send, e, blk, u, z, u_far, rec, w0, b0, w1, b1 = state[:11]
+        send, e, val, z, u_far, rec, moved0, moved1 = state[:8]
         got = exchange(send)
-        w0, b0, c, tie = run_areas(0, load0, e, w0, b0, z)
+        moved0, c, tie = run_areas(0, e, moved0, z)
         if step is None:
             back, z, u_far, rec, tags_at, inverse = owner_first(got, tie)
         else:
-            tags_at, inverse = state[11:]
+            tags_at, inverse = state[8:]
             at = jnp.asarray(step, jnp.int32).reshape(1)
             back, z, u_far, rec = owner_mid(at, got, tags_at, inverse, tie, z, u_far, rec)
         z_back = exchange(back)
-        w1, b1, c, _ = run_areas(HALF, load1, e, w1, b1, z, c)
-        send, e, blk, u = run_slots(z_back, place, place_t, live, blk, u, c, bd_high, bd_low)
-        return (send, e, blk, u, z, u_far, rec, w0, b0, w1, b1, tags_at, inverse)
+        moved1, c = run_areas(HALF, e, moved1, z, c)
+        send, e, val = run_slots(z_back, place, place_t, live, val, c, bd, bd_diag)
+        return (send, e, val, z, u_far, rec, moved0, moved1, tags_at, inverse)
 
     zero = jnp.zeros((HALF, S, K), F32)
-    state = (send, e, blk, u, jnp.zeros((N_REGION, 256), F32), None, None, zero, load0, zero, load1)
+    state = (send, e, val, jnp.zeros((N_REGION, 256), F32), None, None, zero, zero)
     state = iterate(None, state)
     state = lax.fori_loop(1, ITERS - 1, iterate, state)
-    send, e, blk, u, z, u_far, rec, _, b0, _, b1, tags_at, inverse = state
+    send, e, val, z, u_far, rec, moved0, moved1, tags_at, inverse = state
     got = exchange(send)
-    x, tie = run_last(0, e, b0, z)
+    x, tie = run_last(0, e, moved0, z)
     back = owner_last(
         jnp.full((1,), ITERS - 1, jnp.int32), got, tags_at, inverse, tie, z, u_far, rec
     )
     z_back = exchange(back)
-    x = run_last(HALF, e, b1, back, x)
+    x = run_last(HALF, e, moved1, back, x)
     duals, record = call(
-        close_kernel, (struct((128, 128)), struct((ITERS, 2))), in_specs=[VM] * 5
-    )(z_back, place_t, live, blk, u)
-    return (x, duals.reshape(AREA, NB, 128), record)
+        close_kernel, (struct((128, 128)), struct((2, ITERS))), in_specs=[VM] * 4
+    )(z_back, place_t, live, val)
+    return (x, duals.reshape(AREA, NB, 128), record.T)
 
 
 def solution(mesh):

time: 536 us -> 473 us (0.88)
  Pallas kernels: 243 us -> 176 us
  waiting for transfers between devices: 132 us -> 168 us
  starting transfers between devices: 150 us -> 123 us
    pallas_call x40, Pallas kernels: 178 us -> 124 us  [the longest x26 106 us: run_areas(): call(functools.partial(area_kernel, first), (part_shape, struct((S, wide)...]
    all_to_all x28, waiting for transfers between devices: 132 us -> 168 us  [on_device(): lax.all_to_all(x, BOTH, split_axis=0, concat_axis=0, tiled=True)]
    all_to_all x28, starting transfers between devices: 150 us -> 123 us  [on_device(): lax.all_to_all(x, BOTH, split_axis=0, concat_axis=0, tiled=True)]
    pallas_call x12, Pallas kernels: 30.6 us -> 17.9 us  [iterate(): owner_mid(at, got, tags_at, inverse, tie, z, u_far, rec)]
  transfers between devices with their start and end apart: 28 -> 28, of which waited for: 28 -> 28; matrix products, arithmetic and copies ran while one was open for 0% -> 0% of each run, Pallas kernels for 28% -> 25%
where the time goes in v3:
time: 473 us; the launch traced here: 471 us
  Pallas kernels  176 us (37%)
  waiting for transfers between devices  168 us (36%)
  starting transfers between devices  123 us (26%)
    all_to_all x28, waiting for transfers between devices, on_device(): lax.all_to_all(x, BOTH, split_axis=0, concat_axis=0, tiled=True)  168 us
    all_to_all x28, starting transfers between devices, on_device(): lax.all_to_all(x, BOTH, split_axis=0, concat_axis=0, tiled=True)  123 us
    pallas_call x26, Pallas kernels, run_areas(): call(functools.partial(area_kernel, first), (part_shape, struct((S, wide)...  106 us
    pallas_call x1, Pallas kernels, on_device(): call(setup_kernel, (struct((AREA, K, K), BF16), struct((AREA, K)), struct...  19.2 us
    pallas_call x12, Pallas kernels, iterate(): owner_mid(at, got, tags_at, inverse, tie, z, u_far, rec)  17.9 us
    pallas_call x13, Pallas kernels, iterate(): send, e, val = run_slots(z_back, place, place_t, live, val, c, bd, bd_diag)  17 us
    pallas_call x2, Pallas kernels, run_last(): call(functools.partial(last_kernel, first), x_shape if first else (x_shap...  10.1 us
  transfers between devices with their start and end apart: 28, of which 28 were waited for; matrix products, arithmetic and copies ran while one was open for 0% of the time, Pallas kernels for 25%

profile of v3, /device:TPU:1, one launch (start us, length us, event | category | flops | bytes accessed | tf_op | source)
XLA Modules:
  0.0 471.1 jit_solution(13040814656273001367)
XLA Ops:
  2.8 19.2 %shard_map.94 = (bf16[8,1024,1024]{2,1,0:T(8,128)(2,1)}, f32[8,1024]{1,0:T(8,128)S(1)}, f32[32,512]{1,0:T(8,128)}, bf16[512,512]{1,0:T(8,128)(2,1)S(1)}, f32[1,5...) custom-call(bf16[8,1024,1024]{2,1,0:T(8,128)(2,1)} %f_ref.1, ...), custom_call_target="tpu_custom_call" | custom-call | flops 8000000000 | bytes 35651584 | tf_op jit(solution)/shard_map/pallas_call | solution.py:506
  23.8 11.5 %all-to-all-start.2 = ((f32[128,4,128]{2,1,0:T(4,128)}), f32[128,4,128]{2,1,0:T(4,128)S(1)}, u32[]{:S(2)}, u32[]{:S(2)}) async-start(f32[128,4,128]{2,1,0:T(4,128)} %bitcast.6), calls=%async_computation.2 | async-start | bytes 524288 | tf_op jit(solution)/shard_map/all_to_all | solution.py:496
  35.4 4.1 shard_map.97
  39.5 7.0 %all-to-all-done.2 = f32[128,4,128]{2,1,0:T(4,128)S(1)} async-done(((f32[128,4,128]{2,1,0:T(4,128)}), f32[128,4,128]{2,1,0:T(4,128)S(1)}, u32[]{:S(2)}, u32[]{:S(2)}) %all-to-all-start.2) | async-done | bytes 262176 | tf_op jit(solution)/shard_map/all_to_all | solution.py:496
  48.2 4.3 all-to-all-start.3
  56.6 6.0 %all-to-all-done.3 = f32[128,2,128]{2,1,0:T(2,128)S(1)} async-done(((f32[128,2,128]{2,1,0:T(2,128)}), f32[128,2,128]{2,1,0:T(2,128)S(1)}, u32[]{:S(2)}, u32[]{:S(2)}) %all-to-all-start.3) | async-done | bytes 131104 | tf_op jit(solution)/shard_map/all_to_all | solution.py:496
  63.9 374.8 %while.27 = (s32[]{:T(128)}, f32[256,128]{1,0:T(8,128)}, f32[32,512]{1,0:T(8,128)S(1)}, f32[128,128]{1,0:T(8,128)S(1)}, f32[8,256]{1,0:T(8,128)S(1)}, /*index=5*...) while((s32[]{:T(128)}, f32[256,128]{1,0:T(8,128)}, ...), condition=%wide.region_1.0_spmd, body=%wide.region_0.0_spmd.sunk | while | flops 910000000 | bytes 25952516 | solution.py:624
  63.9 4.1 all-to-all-start
  72.1 6.0 %all-to-all-done = f32[128,2,128]{2,1,0:T(2,128)S(1)} async-done(((f32[128,2,128]{2,1,0:T(2,128)}), f32[128,2,128]{2,1,0:T(2,128)S(1)}, u32[]{:S(2)}, u32[]{:S(2)}) %all-to-all-start) | async-done | bytes 131104 | tf_op jit(solution)/shard_map/while/body/eval_jaxpr/all_to_all | solution.py:496
  79.6 4.1 all-to-all-start.1
  83.7 4.1 eval_jaxpr.22
  87.8 6.0 %all-to-all-done.1 = f32[128,2,128]{2,1,0:T(2,128)S(1)} async-done(((f32[128,2,128]{2,1,0:T(2,128)}), f32[128,2,128]{2,1,0:T(2,128)S(1)}, u32[]{:S(2)}, u32[]{:S(2)}) %all-to-all-start.1) | async-done | bytes 131104 | tf_op jit(solution)/shard_map/while/body/eval_jaxpr/all_to_all | solution.py:496
  95.1 4.1 all-to-all-start
  103.3 6.0 %all-to-all-done = f32[128,2,128]{2,1,0:T(2,128)S(1)} async-done(((f32[128,2,128]{2,1,0:T(2,128)}), f32[128,2,128]{2,1,0:T(2,128)S(1)}, u32[]{:S(2)}, u32[]{:S(2)}) %all-to-all-start) | async-done | bytes 131104 | tf_op jit(solution)/shard_map/while/body/eval_jaxpr/all_to_all | solution.py:496
  110.8 4.1 all-to-all-start.1
  119.0 6.0 %all-to-all-done.1 = f32[128,2,128]{2,1,0:T(2,128)S(1)} async-done(((f32[128,2,128]{2,1,0:T(2,128)}), f32[128,2,128]{2,1,0:T(2,128)S(1)}, u32[]{:S(2)}, u32[]{:S(2)}) %all-to-all-start.1) | async-done | bytes 131104 | tf_op jit(solution)/shard_map/while/body/eval_jaxpr/all_to_all | solution.py:496
  126.4 4.1 all-to-all-start
  134.6 6.0 %all-to-all-done = f32[128,2,128]{2,1,0:T(2,128)S(1)} async-done(((f32[128,2,128]{2,1,0:T(2,128)}), f32[128,2,128]{2,1,0:T(2,128)S(1)}, u32[]{:S(2)}, u32[]{:S(2)}) %all-to-all-start) | async-done | bytes 131104 | tf_op jit(solution)/shard_map/while/body/eval_jaxpr/all_to_all | solution.py:496
  142.1 4.1 all-to-all-start.1
  150.3 6.0 %all-to-all-done.1 = f32[128,2,128]{2,1,0:T(2,128)S(1)} async-done(((f32[128,2,128]{2,1,0:T(2,128)}), f32[128,2,128]{2,1,0:T(2,128)S(1)}, u32[]{:S(2)}, u32[]{:S(2)}) %all-to-all-start.1) | async-done | bytes 131104 | tf_op jit(solution)/shard_map/while/body/eval_jaxpr/all_to_all | solution.py:496
  157.6 4.1 all-to-all-start
  161.7 4.1 eval_jaxpr.20
  165.8 6.0 %all-to-all-done = f32[128,2,128]{2,1,0:T(2,128)S(1)} async-done(((f32[128,2,128]{2,1,0:T(2,128)}), f32[128,2,128]{2,1,0:T(2,128)S(1)}, u32[]{:S(2)}, u32[]{:S(2)}) %all-to-all-start) | async-done | bytes 131104 | tf_op jit(solution)/shard_map/while/body/eval_jaxpr/all_to_all | solution.py:496
  173.3 4.1 all-to-all-start.1
  181.5 6.0 %all-to-all-done.1 = f32[128,2,128]{2,1,0:T(2,128)S(1)} async-done(((f32[128,2,128]{2,1,0:T(2,128)}), f32[128,2,128]{2,1,0:T(2,128)S(1)}, u32[]{:S(2)}, u32[]{:S(2)}) %all-to-all-start.1) | async-done | bytes 131104 | tf_op jit(solution)/shard_map/while/body/eval_jaxpr/all_to_all | solution.py:496
  188.8 4.1 all-to-all-start
  197.0 6.0 %all-to-all-done = f32[128,2,128]{2,1,0:T(2,128)S(1)} async-done(((f32[128,2,128]{2,1,0:T(2,128)}), f32[128,2,128]{2,1,0:T(2,128)S(1)}, u32[]{:S(2)}, u32[]{:S(2)}) %all-to-all-start) | async-done | bytes 131104 | tf_op jit(solution)/shard_map/while/body/eval_jaxpr/all_to_all | solution.py:496
  204.5 4.1 all-to-all-start.1
  212.7 6.0 %all-to-all-done.1 = f32[128,2,128]{2,1,0:T(2,128)S(1)} async-done(((f32[128,2,128]{2,1,0:T(2,128)}), f32[128,2,128]{2,1,0:T(2,128)S(1)}, u32[]{:S(2)}, u32[]{:S(2)}) %all-to-all-start.1) | async-done | bytes 131104 | tf_op jit(solution)/shard_map/while/body/eval_jaxpr/all_to_all | solution.py:496
  220.1 4.1 all-to-all-start
  228.3 6.0 %all-to-all-done = f32[128,2,128]{2,1,0:T(2,128)S(1)} async-done(((f32[128,2,128]{2,1,0:T(2,128)}), f32[128,2,128]{2,1,0:T(2,128)S(1)}, u32[]{:S(2)}, u32[]{:S(2)}) %all-to-all-start) | async-done | bytes 131104 | tf_op jit(solution)/shard_map/while/body/eval_jaxpr/all_to_all | solution.py:496
  235.8 4.1 all-to-all-start.1
  244.0 6.0 %all-to-all-done.1 = f32[128,2,128]{2,1,0:T(2,128)S(1)} async-done(((f32[128,2,128]{2,1,0:T(2,128)}), f32[128,2,128]{2,1,0:T(2,128)S(1)}, u32[]{:S(2)}, u32[]{:S(2)}) %all-to-all-start.1) | async-done | bytes 131104 | tf_op jit(solution)/shard_map/while/body/eval_jaxpr/all_to_all | solution.py:496
  251.3 4.1 all-to-all-start
  255.4 4.1 eval_jaxpr.20
  259.5 6.0 %all-to-all-done = f32[128,2,128]{2,1,0:T(2,128)S(1)} async-done(((f32[128,2,128]{2,1,0:T(2,128)}), f32[128,2,128]{2,1,0:T(2,128)S(1)}, u32[]{:S(2)}, u32[]{:S(2)}) %all-to-all-start) | async-done | bytes 131104 | tf_op jit(solution)/shard_map/while/body/eval_jaxpr/all_to_all | solution.py:496
  267.0 4.1 all-to-all-start.1
  275.2 6.0 %all-to-all-done.1 = f32[128,2,128]{2,1,0:T(2,128)S(1)} async-done(((f32[128,2,128]{2,1,0:T(2,128)}), f32[128,2,128]{2,1,0:T(2,128)S(1)}, u32[]{:S(2)}, u32[]{:S(2)}) %all-to-all-start.1) | async-done | bytes 131104 | tf_op jit(solution)/shard_map/while/body/eval_jaxpr/all_to_all | solution.py:496
  282.5 4.1 all-to-all-start
  290.7 6.0 %all-to-all-done = f32[128,2,128]{2,1,0:T(2,128)S(1)} async-done(((f32[128,2,128]{2,1,0:T(2,128)}), f32[128,2,128]{2,1,0:T(2,128)S(1)}, u32[]{:S(2)}, u32[]{:S(2)}) %all-to-all-start) | async-done | bytes 131104 | tf_op jit(solution)/shard_map/while/body/eval_jaxpr/all_to_all | solution.py:496
  298.2 4.1 all-to-all-start.1
  306.4 6.0 %all-to-all-done.1 = f32[128,2,128]{2,1,0:T(2,128)S(1)} async-done(((f32[128,2,128]{2,1,0:T(2,128)}), f32[128,2,128]{2,1,0:T(2,128)S(1)}, u32[]{:S(2)}, u32[]{:S(2)}) %all-to-all-start.1) | async-done | bytes 131104 | tf_op jit(solution)/shard_map/while/body/eval_jaxpr/all_to_all | solution.py:496
  313.8 4.1 all-to-all-start
  322.0 6.0 %all-to-all-done = f32[128,2,128]{2,1,0:T(2,128)S(1)} async-done(((f32[128,2,128]{2,1,0:T(2,128)}), f32[128,2,128]{2,1,0:T(2,128)S(1)}, u32[]{:S(2)}, u32[]{:S(2)}) %all-to-all-start) | async-done | bytes 131104 | tf_op jit(solution)/shard_map/while/body/eval_jaxpr/all_to_all | solution.py:496
  329.5 4.1 all-to-all-start.1
  337.7 6.0 %all-to-all-done.1 = f32[128,2,128]{2,1,0:T(2,128)S(1)} async-done(((f32[128,2,128]{2,1,0:T(2,128)}), f32[128,2,128]{2,1,0:T(2,128)S(1)}, u32[]{:S(2)}, u32[]{:S(2)}) %all-to-all-start.1) | async-done | bytes 131104 | tf_op jit(solution)/shard_map/while/body/eval_jaxpr/all_to_all | solution.py:496
  345.0 4.1 all-to-all-start
  353.2 6.0 %all-to-all-done = f32[128,2,128]{2,1,0:T(2,128)S(1)} async-done(((f32[128,2,128]{2,1,0:T(2,128)}), f32[128,2,128]{2,1,0:T(2,128)S(1)}, u32[]{:S(2)}, u32[]{:S(2)}) %all-to-all-start) | async-done | bytes 131104 | tf_op jit(solution)/shard_map/while/body/eval_jaxpr/all_to_all | solution.py:496
  360.7 4.1 all-to-all-start.1
  368.9 6.0 %all-to-all-done.1 = f32[128,2,128]{2,1,0:T(2,128)S(1)} async-done(((f32[128,2,128]{2,1,0:T(2,128)}), f32[128,2,128]{2,1,0:T(2,128)S(1)}, u32[]{:S(2)}, u32[]{:S(2)}) %all-to-all-start.1) | async-done | bytes 131104 | tf_op jit(solution)/shard_map/while/body/eval_jaxpr/all_to_all | solution.py:496
  376.2 4.1 all-to-all-start
  384.4 6.0 %all-to-all-done = f32[128,2,128]{2,1,0:T(2,128)S(1)} async-done(((f32[128,2,128]{2,1,0:T(2,128)}), f32[128,2,128]{2,1,0:T(2,128)S(1)}, u32[]{:S(2)}, u32[]{:S(2)}) %all-to-all-start) | async-done | bytes 131104 | tf_op jit(solution)/shard_map/while/body/eval_jaxpr/all_to_all | solution.py:496
  391.9 4.1 all-to-all-start.1
  400.1 6.0 %all-to-all-done.1 = f32[128,2,128]{2,1,0:T(2,128)S(1)} async-done(((f32[128,2,128]{2,1,0:T(2,128)}), f32[128,2,128]{2,1,0:T(2,128)S(1)}, u32[]{:S(2)}, u32[]{:S(2)}) %all-to-all-start.1) | async-done | bytes 131104 | tf_op jit(solution)/shard_map/while/body/eval_jaxpr/all_to_all | solution.py:496
  407.5 4.1 all-to-all-start
  415.7 6.0 %all-to-all-done = f32[128,2,128]{2,1,0:T(2,128)S(1)} async-done(((f32[128,2,128]{2,1,0:T(2,128)}), f32[128,2,128]{2,1,0:T(2,128)S(1)}, u32[]{:S(2)}, u32[]{:S(2)}) %all-to-all-start) | async-done | bytes 131104 | tf_op jit(solution)/shard_map/while/body/eval_jaxpr/all_to_all | solution.py:496
  423.2 4.1 all-to-all-start.1
  431.4 6.0 %all-to-all-done.1 = f32[128,2,128]{2,1,0:T(2,128)S(1)} async-done(((f32[128,2,128]{2,1,0:T(2,128)}), f32[128,2,128]{2,1,0:T(2,128)S(1)}, u32[]{:S(2)}, u32[]{:S(2)}) %all-to-all-start.1) | async-done | bytes 131104 | tf_op jit(solution)/shard_map/while/body/eval_jaxpr/all_to_all | solution.py:496
  438.7 4.1 all-to-all-start.4
  442.8 4.5 shard_map.101
  447.4 5.5 %all-to-all-done.4 = f32[128,2,128]{2,1,0:T(2,128)S(1)} async-done(((f32[128,2,128]{2,1,0:T(2,128)}), f32[128,2,128]{2,1,0:T(2,128)S(1)}, u32[]{:S(2)}, u32[]{:S(2)}) %all-to-all-start.4) | async-done | bytes 131104 | tf_op jit(solution)/shard_map/all_to_all | solution.py:496
  454.5 4.3 all-to-all-start.5
  458.8 5.5 %shard_map.103 = f32[8,32,1024]{2,1,0:T(8,128)} custom-call(bf16[8,1024,1024]{2,1,0:T(8,128)(2,1)} %get-tuple-element.666, f32[8,32,1024]{2,1,0:T(8,128)S(1)} %get-tuple-element.667, f32[8,1024]{1,0:T(8,128)S(1)} %get-tuple-element.668, f32[8,1024]{1,0:T(8,128)S(1)} %get-tuple-element.669, ...), custom_call_target="tpu_custom_call", output_to_operand_aliasing={{}: (8, {})} | custom-call | flops 400000000 | bytes 10485760 | tf_op jit(solution)/shard_map/pallas_call | solution.py:563
  464.4 5.6 %all-to-all-done.5 = f32[128,4,128]{2,1,0:T(4,128)S(1)} async-done(((f32[128,4,128]{2,1,0:T(4,128)}), f32[128,4,128]{2,1,0:T(4,128)S(1)}, u32[]{:S(2)}, u32[]{:S(2)}) %all-to-all-start.5) | async-done | bytes 262176 | tf_op jit(solution)/shard_map/all_to_all | solution.py:496
  (61 shorter events, 132.9 us)
Async XLA Ops:
  0.6 0.7 copy-start.1
  1.3 0.7 copy-start.2
  22.1 0.8 copy-start
  23.8 22.7 %all-to-all-start.2 = ((f32[128,4,128]{2,1,0:T(4,128)}), f32[128,4,128]{2,1,0:T(4,128)S(1)}, u32[]{:S(2)}, u32[]{:S(2)}) async-start(f32[128,4,128]{2,1,0:T(4,128)} %bitcast.6), calls=%async_computation.2 | async-start | bytes 524288 | tf_op jit(solution)/shard_map/all_to_all | solution.py:496
  48.2 14.4 %all-to-all-start.3 = ((f32[128,2,128]{2,1,0:T(2,128)}), f32[128,2,128]{2,1,0:T(2,128)S(1)}, u32[]{:S(2)}, u32[]{:S(2)}) async-start(f32[128,2,128]{2,1,0:T(2,128)} %bitcast.8), calls=%async_computation.3 | async-start | bytes 262144 | tf_op jit(solution)/shard_map/all_to_all | solution.py:496
  63.9 14.2 %all-to-all-start = ((f32[128,2,128]{2,1,0:T(2,128)}), f32[128,2,128]{2,1,0:T(2,128)S(1)}, u32[]{:S(2)}, u32[]{:S(2)}) async-start(f32[128,2,128]{2,1,0:T(2,128)} %bitcast.22), calls=%async_computation | async-start | bytes 262144 | tf_op jit(solution)/shard_map/while/body/eval_jaxpr/all_to_all | solution.py:496
  79.6 14.2 %all-to-all-start.1 = ((f32[128,2,128]{2,1,0:T(2,128)}), f32[128,2,128]{2,1,0:T(2,128)S(1)}, u32[]{:S(2)}, u32[]{:S(2)}) async-start(f32[128,2,128]{2,1,0:T(2,128)} %bitcast.24), calls=%async_computation.1 | async-start | bytes 262144 | tf_op jit(solution)/shard_map/while/body/eval_jaxpr/all_to_all | solution.py:496
  95.1 14.2 %all-to-all-start = ((f32[128,2,128]{2,1,0:T(2,128)}), f32[128,2,128]{2,1,0:T(2,128)S(1)}, u32[]{:S(2)}, u32[]{:S(2)}) async-start(f32[128,2,128]{2,1,0:T(2,128)} %bitcast.22), calls=%async_computation | async-start | bytes 262144 | tf_op jit(solution)/shard_map/while/body/eval_jaxpr/all_to_all | solution.py:496
  110.8 14.2 %all-to-all-start.1 = ((f32[128,2,128]{2,1,0:T(2,128)}), f32[128,2,128]{2,1,0:T(2,128)S(1)}, u32[]{:S(2)}, u32[]{:S(2)}) async-start(f32[128,2,128]{2,1,0:T(2,128)} %bitcast.24), calls=%async_computation.1 | async-start | bytes 262144 | tf_op jit(solution)/shard_map/while/body/eval_jaxpr/all_to_all | solution.py:496
  126.4 14.2 %all-to-all-start = ((f32[128,2,128]{2,1,0:T(2,128)}), f32[128,2,128]{2,1,0:T(2,128)S(1)}, u32[]{:S(2)}, u32[]{:S(2)}) async-start(f32[128,2,128]{2,1,0:T(2,128)} %bitcast.22), calls=%async_computation | async-start | bytes 262144 | tf_op jit(solution)/shard_map/while/body/eval_jaxpr/all_to_all | solution.py:496
  142.1 14.2 %all-to-all-start.1 = ((f32[128,2,128]{2,1,0:T(2,128)}), f32[128,2,128]{2,1,0:T(2,128)S(1)}, u32[]{:S(2)}, u32[]{:S(2)}) async-start(f32[128,2,128]{2,1,0:T(2,128)} %bitcast.24), calls=%async_computation.1 | async-start | bytes 262144 | tf_op jit(solution)/shard_map/while/body/eval_jaxpr/all_to_all | solution.py:496
  157.6 14.2 %all-to-all-start = ((f32[128,2,128]{2,1,0:T(2,128)}), f32[128,2,128]{2,1,0:T(2,128)S(1)}, u32[]{:S(2)}, u32[]{:S(2)}) async-start(f32[128,2,128]{2,1,0:T(2,128)} %bitcast.22), calls=%async_computation | async-start | bytes 262144 | tf_op jit(solution)/shard_map/while/body/eval_jaxpr/all_to_all | solution.py:496
  173.3 14.2 %all-to-all-start.1 = ((f32[128,2,128]{2,1,0:T(2,128)}), f32[128,2,128]{2,1,0:T(2,128)S(1)}, u32[]{:S(2)}, u32[]{:S(2)}) async-start(f32[128,2,128]{2,1,0:T(2,128)} %bitcast.24), calls=%async_computation.1 | async-start | bytes 262144 | tf_op jit(solution)/shard_map/while/body/eval_jaxpr/all_to_all | solution.py:496
  188.8 14.2 %all-to-all-start = ((f32[128,2,128]{2,1,0:T(2,128)}), f32[128,2,128]{2,1,0:T(2,128)S(1)}, u32[]{:S(2)}, u32[]{:S(2)}) async-start(f32[128,2,128]{2,1,0:T(2,128)} %bitcast.22), calls=%async_computation | async-start | bytes 262144 | tf_op jit(solution)/shard_map/while/body/eval_jaxpr/all_to_all | solution.py:496
  204.5 14.2 %all-to-all-start.1 = ((f32[128,2,128]{2,1,0:T(2,128)}), f32[128,2,128]{2,1,0:T(2,128)S(1)}, u32[]{:S(2)}, u32[]{:S(2)}) async-start(f32[128,2,128]{2,1,0:T(2,128)} %bitcast.24), calls=%async_computation.1 | async-start | bytes 262144 | tf_op jit(solution)/shard_map/while/body/eval_jaxpr/all_to_all | solution.py:496
  220.1 14.2 %all-to-all-start = ((f32[128,2,128]{2,1,0:T(2,128)}), f32[128,2,128]{2,1,0:T(2,128)S(1)}, u32[]{:S(2)}, u32[]{:S(2)}) async-start(f32[128,2,128]{2,1,0:T(2,128)} %bitcast.22), calls=%async_computation | async-start | bytes 262144 | tf_op jit(solution)/shard_map/while/body/eval_jaxpr/all_to_all | solution.py:496
  235.8 14.2 %all-to-all-start.1 = ((f32[128,2,128]{2,1,0:T(2,128)}), f32[128,2,128]{2,1,0:T(2,128)S(1)}, u32[]{:S(2)}, u32[]{:S(2)}) async-start(f32[128,2,128]{2,1,0:T(2,128)} %bitcast.24), calls=%async_computation.1 | async-start | bytes 262144 | tf_op jit(solution)/shard_map/while/body/eval_jaxpr/all_to_all | solution.py:496
  251.3 14.2 %all-to-all-start = ((f32[128,2,128]{2,1,0:T(2,128)}), f32[128,2,128]{2,1,0:T(2,128)S(1)}, u32[]{:S(2)}, u32[]{:S(2)}) async-start(f32[128,2,128]{2,1,0:T(2,128)} %bitcast.22), calls=%async_computation | async-start | bytes 262144 | tf_op jit(solution)/shard_map/while/body/eval_jaxpr/all_to_all | solution.py:496
  267.0 14.2 %all-to-all-start.1 = ((f32[128,2,128]{2,1,0:T(2,128)}), f32[128,2,128]{2,1,0:T(2,128)S(1)}, u32[]{:S(2)}, u32[]{:S(2)}) async-start(f32[128,2,128]{2,1,0:T(2,128)} %bitcast.24), calls=%async_computation.1 | async-start | bytes 262144 | tf_op jit(solution)/shard_map/while/body/eval_jaxpr/all_to_all | solution.py:496
  282.5 14.2 %all-to-all-start = ((f32[128,2,128]{2,1,0:T(2,128)}), f32[128,2,128]{2,1,0:T(2,128)S(1)}, u32[]{:S(2)}, u32[]{:S(2)}) async-start(f32[128,2,128]{2,1,0:T(2,128)} %bitcast.22), calls=%async_computation | async-start | bytes 262144 | tf_op jit(solution)/shard_map/while/body/eval_jaxpr/all_to_all | solution.py:496
  298.2 14.2 %all-to-all-start.1 = ((f32[128,2,128]{2,1,0:T(2,128)}), f32[128,2,128]{2,1,0:T(2,128)S(1)}, u32[]{:S(2)}, u32[]{:S(2)}) async-start(f32[128,2,128]{2,1,0:T(2,128)} %bitcast.24), calls=%async_computation.1 | async-start | bytes 262144 | tf_op jit(solution)/shard_map/while/body/eval_jaxpr/all_to_all | solution.py:496
  313.8 14.2 %all-to-all-start = ((f32[128,2,128]{2,1,0:T(2,128)}), f32[128,2,128]{2,1,0:T(2,128)S(1)}, u32[]{:S(2)}, u32[]{:S(2)}) async-start(f32[128,2,128]{2,1,0:T(2,128)} %bitcast.22), calls=%async_computation | async-start | bytes 262144 | tf_op jit(solution)/shard_map/while/body/eval_jaxpr/all_to_all | solution.py:496
  329.5 14.2 %all-to-all-start.1 = ((f32[128,2,128]{2,1,0:T(2,128)}), f32[128,2,128]{2,1,0:T(2,128)S(1)}, u32[]{:S(2)}, u32[]{:S(2)}) async-start(f32[128,2,128]{2,1,0:T(2,128)} %bitcast.24), calls=%async_computation.1 | async-start | bytes 262144 | tf_op jit(solution)/shard_map/while/body/eval_jaxpr/all_to_all | solution.py:496
  345.0 14.2 %all-to-all-start = ((f32[128,2,128]{2,1,0:T(2,128)}), f32[128,2,128]{2,1,0:T(2,128)S(1)}, u32[]{:S(2)}, u32[]{:S(2)}) async-start(f32[128,2,128]{2,1,0:T(2,128)} %bitcast.22), calls=%async_computation | async-start | bytes 262144 | tf_op jit(solution)/shard_map/while/body/eval_jaxpr/all_to_all | solution.py:496
  360.7 14.2 %all-to-all-start.1 = ((f32[128,2,128]{2,1,0:T(2,128)}), f32[128,2,128]{2,1,0:T(2,128)S(1)}, u32[]{:S(2)}, u32[]{:S(2)}) async-start(f32[128,2,128]{2,1,0:T(2,128)} %bitcast.24), calls=%async_computation.1 | async-start | bytes 262144 | tf_op jit(solution)/shard_map/while/body/eval_jaxpr/all_to_all | solution.py:496
  376.2 14.2 %all-to-all-start = ((f32[128,2,128]{2,1,0:T(2,128)}), f32[128,2,128]{2,1,0:T(2,128)S(1)}, u32[]{:S(2)}, u32[]{:S(2)}) async-start(f32[128,2,128]{2,1,0:T(2,128)} %bitcast.22), calls=%async_computation | async-start | bytes 262144 | tf_op jit(solution)/shard_map/while/body/eval_jaxpr/all_to_all | solution.py:496
  391.9 14.2 %all-to-all-start.1 = ((f32[128,2,128]{2,1,0:T(2,128)}), f32[128,2,128]{2,1,0:T(2,128)S(1)}, u32[]{:S(2)}, u32[]{:S(2)}) async-start(f32[128,2,128]{2,1,0:T(2,128)} %bitcast.24), calls=%async_computation.1 | async-start | bytes 262144 | tf_op jit(solution)/shard_map/while/body/eval_jaxpr/all_to_all | solution.py:496
  407.5 14.2 %all-to-all-start = ((f32[128,2,128]{2,1,0:T(2,128)}), f32[128,2,128]{2,1,0:T(2,128)S(1)}, u32[]{:S(2)}, u32[]{:S(2)}) async-start(f32[128,2,128]{2,1,0:T(2,128)} %bitcast.22), calls=%async_computation | async-start | bytes 262144 | tf_op jit(solution)/shard_map/while/body/eval_jaxpr/all_to_all | solution.py:496
  423.2 14.2 %all-to-all-start.1 = ((f32[128,2,128]{2,1,0:T(2,128)}), f32[128,2,128]{2,1,0:T(2,128)S(1)}, u32[]{:S(2)}, u32[]{:S(2)}) async-start(f32[128,2,128]{2,1,0:T(2,128)} %bitcast.24), calls=%async_computation.1 | async-start | bytes 262144 | tf_op jit(solution)/shard_map/while/body/eval_jaxpr/all_to_all | solution.py:496
  438.7 14.2 %all-to-all-start.4 = ((f32[128,2,128]{2,1,0:T(2,128)}), f32[128,2,128]{2,1,0:T(2,128)S(1)}, u32[]{:S(2)}, u32[]{:S(2)}) async-start(f32[128,2,128]{2,1,0:T(2,128)} %bitcast.10), calls=%async_computation.4 | async-start | bytes 262144 | tf_op jit(solution)/shard_map/all_to_all | solution.py:496
  454.5 15.4 %all-to-all-start.5 = ((f32[128,4,128]{2,1,0:T(4,128)}), f32[128,4,128]{2,1,0:T(4,128)S(1)}, u32[]{:S(2)}, u32[]{:S(2)}) async-start(f32[128,4,128]{2,1,0:T(4,128)} %bitcast.12), calls=%async_computation.5 | async-start | bytes 524288 | tf_op jit(solution)/shard_map/all_to_all | solution.py:496

commit v4 on v3

--- a/solution.py
+++ b/solution.py
@@ -80,7 +80,7 @@
     )
 
 
-def route_kernel(me_ref, counts_ref, inc_ref, p_ref, pt_ref, tag_ref, live_ref):
+def route(me_ref, counts_ref, inc_ref, p_ref, pt_ref, tag_ref, live_ref):
     me = me_ref[0]
     lane = iota((ITEMS, ITEMS), 1)
     sub = iota((ITEMS, ITEMS), 0)
@@ -128,6 +128,14 @@
 
 def far_rows(width, region):
     return pl.ds(width * N_DEV * region + 1, N_DEV, stride=width)
+
+
+def near_tile(dev):
+    return pl.ds(N_REGION * dev, N_REGION)
+
+
+def far_tile(region):
+    return pl.ds(WORLD + N_DEV * region, N_DEV)
 
 
 def bus_sums(near, far, near_tags, far_tags):
@@ -170,9 +178,9 @@
         inverse = 1.0 / jnp.maximum(counts, 1.0)
         inv_ref[...] = inverse
         for d in range(N_DEV):
-            tag_ref[near_rows(2, d), :] = near_tags[d]
+            tag_ref[near_tile(d), :] = near_tags[d]
         for r in range(N_REGION):
-            tag_ref[far_rows(2, r), :] = far_tags[r]
+            tag_ref[far_tile(r), :] = far_tags[r]
         rec_ref[...] = jnp.zeros((32, 128), F32)
         step = 0
     else:
@@ -181,8 +189,8 @@
         else:
             (step_ref, got_ref, tag_ref, inv_ref, tie_ref, prev_ref, u_in, rec_in,
              out_ref, z_ref, u_ref, rec_ref) = refs
-        near_tags = [tag_ref[near_rows(2, d), :] for d in range(N_DEV)]
-        far_tags = [tag_ref[far_rows(2, r), :] for r in range(N_REGION)]
+        near_tags = [tag_ref[near_tile(d), :] for d in range(N_DEV)]
+        far_tags = [tag_ref[far_tile(r), :] for r in range(N_REGION)]
         inverse = inv_ref[...]
         step = step_ref[0]
     wide_in = 4 if first else 2
@@ -211,10 +219,10 @@
             val = jnp.where(near_tags[dev] == float(bus), spread[bus], val)
         out_ref[near_rows(wide_out, dev), :] = val
         u = near[dev] - val
-        gap = u if first else u - u_in[near_rows(2, dev), :]
+        gap = u if first else u - u_in[near_tile(dev), :]
         primal = primal + gap * gap
         if not last:
-            u_ref[near_rows(2, dev), :] = u
+            u_ref[near_tile(dev), :] = u
     for region in range(N_REGION):
         val = jnp.zeros((N_DEV, 128), F32)
         for bus in range(BUS_DEV):
@@ -223,11 +231,11 @@
             val = jnp.where(far_tags[region] == float(bus), one, val)
         out_ref[far_rows(wide_out, region), :] = val
         u = far[region] - val
-        gap = u if first else u - u_in[far_rows(2, region), :]
+        gap = u if first else u - u_in[far_tile(region), :]
         square = gap * gap
         primal = primal + square[:8] + square[8:]
         if not last:
-            u_ref[far_rows(2, region), :] = u
+            u_ref[far_tile(region), :] = u
     primal = jnp.sum(primal, axis=0, keepdims=True) * (1.0 / CELLS)
     row = iota((32, 128), 0)
     if last:
@@ -253,7 +261,7 @@
     return jnp.concatenate([lanes[:, ITEMS * r : ITEMS * r + ITEMS] for r in range(ROWS)], axis=0)
 
 
-def open_kernel(c_ref, p_ref, tag_ref, send_ref, e_ref, val_ref):
+def open_exchange(c_ref, p_ref, tag_ref, send_ref, e_ref, val_ref):
     val = by_row(c_ref[...])
     val_ref[...] = val
     e_ref[...] = jnp.zeros((S, ROWS * ITEMS), F32)
@@ -304,41 +312,40 @@
 
 
 def setup_kernel(
-    f_ref, p_hbm, load_hbm, lo_hbm, hi_hbm,
-    m_ref, diag_ref, c_ref, bd_ref, bdiag_ref, load_out, lo_out, hi_out,
-    ft, g, p_ref, loads, lo_ref, hi_ref, sem,
+    me_ref, counts_ref, f0_ref, f1_ref, f2_ref, f3_ref, p_hbm, load_hbm, lo_hbm, hi_hbm, inc_hbm,
+    m_ref, diag_ref, bd_ref, bdiag_ref, load_out, lo_out, hi_out,
+    place_ref, place_t_ref, live_ref, send_ref, e_ref, val_ref,
+    ft, g, p_ref, loads, lo_ref, hi_ref, inc_ref, tag_ref, c_ref, sem,
 ):
     area = pl.program_id(0)
     order = edge_order()
+    pairs = ((p_hbm, p_ref), (load_hbm, loads), (lo_hbm, lo_ref), (hi_hbm, hi_ref), (inc_hbm, inc_ref))
     fetch = [
         pltpu.make_async_copy(source, target, sem.at[n])
-        for n, (source, target) in enumerate(
-            ((p_hbm, p_ref), (load_hbm, loads), (lo_hbm, lo_ref), (hi_hbm, hi_ref))
-        )
+        for n, (source, target) in enumerate(pairs)
     ]
 
     @pl.when(area == 0)
     def _():
         for copy in fetch:
             copy.start()
-        for copy in fetch:
-            copy.wait()
+        fetch[0].wait()
 
     piv = p_ref[pl.ds(area, 1), :]
     piv_col = jnp.transpose(jnp.broadcast_to(piv, (128, K)))
     step = 256
     count = K // step
-    head = dot(f_ref[0, :, :128], order)
+    stripes = (f0_ref, f1_ref, f2_ref, f3_ref)
+    head = jnp.concatenate([dot(f[0, :, :128], order) for f in stripes], axis=0)
     g[:, :128] = (head * piv_col).astype(BF16)
     f_head = head.astype(BF16)
-    for q in range(1, K // 128):
-        top = q // 2 * step
-        part = f_ref[0, top:, 128 * q : 128 * q + 128].astype(F32)
-        g[top:, 128 * q : 128 * q + 128] = (part * piv_col[top:]).astype(BF16)
     for i in range(count):
         at = slice(i * step, (i + 1) * step)
         w = (i + 1) * step
-        rows = jnp.concatenate([f_head[at], f_ref[0, at, 128:w]], axis=1)
+        for q in range(1, w // 128):
+            part = stripes[i][0, :, 128 * q : 128 * q + 128].astype(F32)
+            g[at, 128 * q : 128 * q + 128] = (part * piv_col[at]).astype(BF16)
+        rows = jnp.concatenate([f_head[at], stripes[i][0, :, 128:]], axis=1)
         ft[:w, at] = jnp.transpose(rows)
     eye = iota((step, step), 0) == iota((step, step), 1)
     fix = piv - piv.astype(BF16).astype(F32)
@@ -369,6 +376,13 @@
             rows = jnp.where(mine, pltpu.roll(rows, shift, 1), 0.0)
             at = pl.ds(pl.multiple_of(ITEMS * r_in + NB * area, NB), NB)
             bd_ref[at, ITEMS * r : ITEMS * r + ITEMS] = rows.astype(BF16)
+
+    @pl.when(area == 0)
+    def _():
+        for copy in fetch[1:]:
+            copy.wait()
+        route(me_ref, counts_ref, inc_ref, place_ref, place_t_ref, tag_ref, live_ref)
+
     load = loads[area]
     load = jnp.concatenate([pick(load[:, :128], order), load[:, 128:]], axis=1)
     load_out[0] = load
@@ -389,6 +403,10 @@
         c_ref[:, at] = jnp.where(lane_mine, moved, c_ref[:, at])
         moved = pltpu.roll(edge_diag, lax.rem(area * NB + (128 - r * NB), 128), 1)
         bdiag_ref[:, at] = jnp.where(lane_mine[:1], moved, bdiag_ref[:, at])
+
+    @pl.when(area == AREA - 1)
+    def _():
+        open_exchange(c_ref, place_ref, tag_ref, send_ref, e_ref, val_ref)
 
 
 def fetch_areas(first, m_ref, buf, sem):
@@ -495,32 +513,30 @@
     wide = ROWS * ITEMS
     exchange = lambda x: lax.all_to_all(x, BOTH, split_axis=0, concat_axis=0, tiled=True)
     me = lax.axis_index("region").astype(jnp.int32).reshape(1)
-    place, place_t, tags, live = call(
-        route_kernel,
-        (struct((ITEMS, 256), BF16), struct((256, ITEMS), BF16), struct((2, ITEMS)), struct((1, ITEMS))),
-        in_specs=[SMEM, SMEM, VM],
-    )(me, counts, incidence)
-
     area_block = lambda rows: pl.BlockSpec((1, rows, K), lambda a: (a, 0, 0))
     whole = lambda *shape: pl.BlockSpec(shape, lambda a: (0,) * len(shape))
-    matrix, diag, c_now, bd, bd_diag, load, floor_box, ceil_box = call(
+    stripe = lambda i: pl.BlockSpec((1, K // 4, (i + 1) * K // 4), lambda a: (a, i, 0))
+    outs = (
+        (struct((AREA, K, K), BF16), area_block(K)),
+        (struct((AREA, K)), whole(AREA, K)),
+        (struct((wide, wide), BF16), whole(wide, wide)),
+        (struct((1, wide)), whole(1, wide)),
+        (struct((AREA, S, K)), area_block(S)),
+        (struct((AREA, K)), whole(AREA, K)),
+        (struct((AREA, K)), whole(AREA, K)),
+        (struct((ITEMS, 256), BF16), whole(ITEMS, 256)),
+        (struct((256, ITEMS), BF16), whole(256, ITEMS)),
+        (struct((1, ITEMS)), whole(1, ITEMS)),
+        (struct((512, 128)), whole(512, 128)),
+        (struct((S, wide)), whole(S, wide)),
+        (struct((128, 128)), whole(128, 128)),
+    )
+    (matrix, diag, bd, bd_diag, load, floor_box, ceil_box, place, place_t, live, send, e, val) = call(
         setup_kernel,
-        (
-            struct((AREA, K, K), BF16),
-            struct((AREA, K)),
-            struct((S, wide)),
-            struct((wide, wide), BF16),
-            struct((1, wide)),
-            struct((AREA, S, K)),
-            struct((AREA, K)),
-            struct((AREA, K)),
-        ),
+        tuple(shape for shape, _ in outs),
         grid=(AREA,),
-        in_specs=[area_block(K), HBM, HBM, HBM, HBM],
-        out_specs=(
-            area_block(K), whole(AREA, K), whole(S, wide), whole(wide, wide), whole(1, wide),
-            area_block(S), whole(AREA, K), whole(AREA, K),
-        ),
+        in_specs=[SMEM, SMEM] + [stripe(i) for i in range(4)] + [HBM] * 5,
+        out_specs=tuple(spec for _, spec in outs),
         scratch_shapes=[
             pltpu.VMEM((K, K), BF16),
             pltpu.VMEM((K, K), BF16),
@@ -528,17 +544,14 @@
             pltpu.VMEM((AREA, S, K), F32),
             pltpu.VMEM((AREA, K), F32),
             pltpu.VMEM((AREA, K), F32),
-            pltpu.SemaphoreType.DMA((4,)),
+            pltpu.VMEM((AREA, NB), jnp.int32),
+            pltpu.VMEM((2, ITEMS), F32),
+            pltpu.VMEM((S, wide), F32),
+            pltpu.SemaphoreType.DMA((5,)),
         ],
         cost_estimate=cost(8 * 10**9, 34 * 2**20),
         limit=60,
-    )(factor, pivots, loads, lower, upper)
-
-    send, e, val = call(
-        open_kernel,
-        (struct((512, 128)), struct((S, wide)), struct((128, 128))),
-        in_specs=[VM] * 3,
-    )(c_now, place, tags)
+    )(me, counts, *[factor] * 4, pivots, loads, lower, upper, incidence)
 
     part_shape = struct((HALF, S, K))
     scratch = [

time: 473 us -> 467 us (0.987)
    pallas_call x3 -> x1, Pallas kernels: 21 us -> 18.8 us  [on_device(): call(setup_kernel, tuple((shape for shape, _ in outs)), grid=(AREA,), in_...]
where the time goes in v4:
time: 467 us; the launch traced here: 465 us
  Pallas kernels  173 us (37%)
  waiting for transfers between devices  167 us (36%)
  starting transfers between devices  123 us (26%)
    all_to_all x28, waiting for transfers between devices, on_device(): lax.all_to_all(x, BOTH, split_axis=0, concat_axis=0, tiled=True)  167 us
    all_to_all x28, starting transfers between devices, on_device(): lax.all_to_all(x, BOTH, split_axis=0, concat_axis=0, tiled=True)  123 us
    pallas_call x26, Pallas kernels, run_areas(): call(functools.partial(area_kernel, first), (part_shape, struct((S, wide)...  106 us
    pallas_call x1, Pallas kernels, on_device(): call(setup_kernel, tuple((shape for shape, _ in outs)), grid=(AREA,), in_...  18.8 us
    pallas_call x12, Pallas kernels, iterate(): owner_mid(at, got, tags_at, inverse, tie, z, u_far, rec)  17 us
    pallas_call x13, Pallas kernels, iterate(): send, e, val = run_slots(z_back, place, place_t, live, val, c, bd, bd_diag)  16.8 us
    pallas_call x2, Pallas kernels, run_last(): call(functools.partial(last_kernel, first), x_shape if first else (x_shap...  10.1 us
  transfers between devices with their start and end apart: 28, of which 28 were waited for; matrix products, arithmetic and copies ran while one was open for 0% of the time, Pallas kernels for 25%

profile of v4, /device:TPU:1, one launch (start us, length us, event | category | flops | bytes accessed | tf_op | source)
XLA Modules:
  0.0 465.4 jit_solution(306250434889093252)
XLA Ops:
  0.6 18.8 %shard_map.94 = (bf16[8,1024,1024]{2,1,0:T(8,128)(2,1)}, f32[8,1024]{1,0:T(8,128)S(1)}, bf16[512,512]{1,0:T(8,128)(2,1)S(1)}, f32[1,512]{1,0:T(1,128)S(1)}, f32[...) custom-call(s32[1]{0:T(128)} %bitcast.5.me_ref, ...), custom_call_target="tpu_custom_call" | custom-call | flops 8000000000 | bytes 35651584 | tf_op jit(solution)/shard_map/pallas_call | solution.py:534
  19.5 11.5 %all-to-all-start.2 = ((f32[128,4,128]{2,1,0:T(4,128)}), f32[128,4,128]{2,1,0:T(4,128)S(1)}, u32[]{:S(2)}, u32[]{:S(2)}) async-start(f32[128,4,128]{2,1,0:T(4,128)} %bitcast.32), calls=%async_computation.2 | async-start | bytes 524288 | tf_op jit(solution)/shard_map/all_to_all | solution.py:514
  36.0 6.2 %all-to-all-done.2 = f32[128,4,128]{2,1,0:T(4,128)S(1)} async-done(((f32[128,4,128]{2,1,0:T(4,128)}), f32[128,4,128]{2,1,0:T(4,128)S(1)}, u32[]{:S(2)}, u32[]{:S(2)}) %all-to-all-start.2) | async-done | bytes 262176 | tf_op jit(solution)/shard_map/all_to_all | solution.py:514
  43.8 4.3 all-to-all-start.3
  52.2 6.0 %all-to-all-done.3 = f32[128,2,128]{2,1,0:T(2,128)S(1)} async-done(((f32[128,2,128]{2,1,0:T(2,128)}), f32[128,2,128]{2,1,0:T(2,128)S(1)}, u32[]{:S(2)}, u32[]{:S(2)}) %all-to-all-start.3) | async-done | bytes 131104 | tf_op jit(solution)/shard_map/all_to_all | solution.py:514
  59.5 373.6 %while.27 = (s32[]{:T(128)}, f32[256,128]{1,0:T(8,128)}, f32[32,512]{1,0:T(8,128)S(1)}, f32[128,128]{1,0:T(8,128)S(1)}, f32[8,256]{1,0:T(8,128)S(1)}, /*index=5*...) while((s32[]{:T(128)}, f32[256,128]{1,0:T(8,128)}, ...), condition=%wide.region_1.0_spmd, body=%wide.region_0.0_spmd.sunk | while | flops 910000000 | bytes 25952516 | solution.py:637
  59.5 4.1 all-to-all-start
  67.7 6.0 %all-to-all-done = f32[128,2,128]{2,1,0:T(2,128)S(1)} async-done(((f32[128,2,128]{2,1,0:T(2,128)}), f32[128,2,128]{2,1,0:T(2,128)S(1)}, u32[]{:S(2)}, u32[]{:S(2)}) %all-to-all-start) | async-done | bytes 131104 | tf_op jit(solution)/shard_map/while/body/eval_jaxpr/all_to_all | solution.py:514
  75.1 4.1 all-to-all-start.1
  83.3 6.0 %all-to-all-done.1 = f32[128,2,128]{2,1,0:T(2,128)S(1)} async-done(((f32[128,2,128]{2,1,0:T(2,128)}), f32[128,2,128]{2,1,0:T(2,128)S(1)}, u32[]{:S(2)}, u32[]{:S(2)}) %all-to-all-start.1) | async-done | bytes 131104 | tf_op jit(solution)/shard_map/while/body/eval_jaxpr/all_to_all | solution.py:514
  90.6 4.1 all-to-all-start
  98.8 6.0 %all-to-all-done = f32[128,2,128]{2,1,0:T(2,128)S(1)} async-done(((f32[128,2,128]{2,1,0:T(2,128)}), f32[128,2,128]{2,1,0:T(2,128)S(1)}, u32[]{:S(2)}, u32[]{:S(2)}) %all-to-all-start) | async-done | bytes 131104 | tf_op jit(solution)/shard_map/while/body/eval_jaxpr/all_to_all | solution.py:514
  106.2 4.1 all-to-all-start.1
  114.4 6.0 %all-to-all-done.1 = f32[128,2,128]{2,1,0:T(2,128)S(1)} async-done(((f32[128,2,128]{2,1,0:T(2,128)}), f32[128,2,128]{2,1,0:T(2,128)S(1)}, u32[]{:S(2)}, u32[]{:S(2)}) %all-to-all-start.1) | async-done | bytes 131104 | tf_op jit(solution)/shard_map/while/body/eval_jaxpr/all_to_all | solution.py:514
  121.7 4.1 all-to-all-start
  130.0 6.0 %all-to-all-done = f32[128,2,128]{2,1,0:T(2,128)S(1)} async-done(((f32[128,2,128]{2,1,0:T(2,128)}), f32[128,2,128]{2,1,0:T(2,128)S(1)}, u32[]{:S(2)}, u32[]{:S(2)}) %all-to-all-start) | async-done | bytes 131104 | tf_op jit(solution)/shard_map/while/body/eval_jaxpr/all_to_all | solution.py:514
  137.4 4.1 all-to-all-start.1
  145.6 6.0 %all-to-all-done.1 = f32[128,2,128]{2,1,0:T(2,128)S(1)} async-done(((f32[128,2,128]{2,1,0:T(2,128)}), f32[128,2,128]{2,1,0:T(2,128)S(1)}, u32[]{:S(2)}, u32[]{:S(2)}) %all-to-all-start.1) | async-done | bytes 131104 | tf_op jit(solution)/shard_map/while/body/eval_jaxpr/all_to_all | solution.py:514
  152.9 4.1 all-to-all-start
  161.1 6.0 %all-to-all-done = f32[128,2,128]{2,1,0:T(2,128)S(1)} async-done(((f32[128,2,128]{2,1,0:T(2,128)}), f32[128,2,128]{2,1,0:T(2,128)S(1)}, u32[]{:S(2)}, u32[]{:S(2)}) %all-to-all-start) | async-done | bytes 131104 | tf_op jit(solution)/shard_map/while/body/eval_jaxpr/all_to_all | solution.py:514
  168.5 4.1 all-to-all-start.1
  172.6 4.1 eval_jaxpr.22
  176.7 6.0 %all-to-all-done.1 = f32[128,2,128]{2,1,0:T(2,128)S(1)} async-done(((f32[128,2,128]{2,1,0:T(2,128)}), f32[128,2,128]{2,1,0:T(2,128)S(1)}, u32[]{:S(2)}, u32[]{:S(2)}) %all-to-all-start.1) | async-done | bytes 131104 | tf_op jit(solution)/shard_map/while/body/eval_jaxpr/all_to_all | solution.py:514
  184.0 4.1 all-to-all-start
  192.2 6.0 %all-to-all-done = f32[128,2,128]{2,1,0:T(2,128)S(1)} async-done(((f32[128,2,128]{2,1,0:T(2,128)}), f32[128,2,128]{2,1,0:T(2,128)S(1)}, u32[]{:S(2)}, u32[]{:S(2)}) %all-to-all-start) | async-done | bytes 131104 | tf_op jit(solution)/shard_map/while/body/eval_jaxpr/all_to_all | solution.py:514
  199.6 4.1 all-to-all-start.1
  203.8 4.1 eval_jaxpr.22
  207.8 6.0 %all-to-all-done.1 = f32[128,2,128]{2,1,0:T(2,128)S(1)} async-done(((f32[128,2,128]{2,1,0:T(2,128)}), f32[128,2,128]{2,1,0:T(2,128)S(1)}, u32[]{:S(2)}, u32[]{:S(2)}) %all-to-all-start.1) | async-done | bytes 131104 | tf_op jit(solution)/shard_map/while/body/eval_jaxpr/all_to_all | solution.py:514
  215.1 4.1 all-to-all-start
  223.3 6.0 %all-to-all-done = f32[128,2,128]{2,1,0:T(2,128)S(1)} async-done(((f32[128,2,128]{2,1,0:T(2,128)}), f32[128,2,128]{2,1,0:T(2,128)S(1)}, u32[]{:S(2)}, u32[]{:S(2)}) %all-to-all-start) | async-done | bytes 131104 | tf_op jit(solution)/shard_map/while/body/eval_jaxpr/all_to_all | solution.py:514
  230.8 4.1 all-to-all-start.1
  239.0 6.0 %all-to-all-done.1 = f32[128,2,128]{2,1,0:T(2,128)S(1)} async-done(((f32[128,2,128]{2,1,0:T(2,128)}), f32[128,2,128]{2,1,0:T(2,128)S(1)}, u32[]{:S(2)}, u32[]{:S(2)}) %all-to-all-start.1) | async-done | bytes 131104 | tf_op jit(solution)/shard_map/while/body/eval_jaxpr/all_to_all | solution.py:514
  246.3 4.1 all-to-all-start
  254.5 6.0 %all-to-all-done = f32[128,2,128]{2,1,0:T(2,128)S(1)} async-done(((f32[128,2,128]{2,1,0:T(2,128)}), f32[128,2,128]{2,1,0:T(2,128)S(1)}, u32[]{:S(2)}, u32[]{:S(2)}) %all-to-all-start) | async-done | bytes 131104 | tf_op jit(solution)/shard_map/while/body/eval_jaxpr/all_to_all | solution.py:514
  261.9 4.1 all-to-all-start.1
  270.1 6.0 %all-to-all-done.1 = f32[128,2,128]{2,1,0:T(2,128)S(1)} async-done(((f32[128,2,128]{2,1,0:T(2,128)}), f32[128,2,128]{2,1,0:T(2,128)S(1)}, u32[]{:S(2)}, u32[]{:S(2)}) %all-to-all-start.1) | async-done | bytes 131104 | tf_op jit(solution)/shard_map/while/body/eval_jaxpr/all_to_all | solution.py:514
  277.4 4.1 all-to-all-start
  285.6 6.0 %all-to-all-done = f32[128,2,128]{2,1,0:T(2,128)S(1)} async-done(((f32[128,2,128]{2,1,0:T(2,128)}), f32[128,2,128]{2,1,0:T(2,128)S(1)}, u32[]{:S(2)}, u32[]{:S(2)}) %all-to-all-start) | async-done | bytes 131104 | tf_op jit(solution)/shard_map/while/body/eval_jaxpr/all_to_all | solution.py:514
  293.0 4.1 all-to-all-start.1
  297.1 4.1 eval_jaxpr.22
  301.2 6.0 %all-to-all-done.1 = f32[128,2,128]{2,1,0:T(2,128)S(1)} async-done(((f32[128,2,128]{2,1,0:T(2,128)}), f32[128,2,128]{2,1,0:T(2,128)S(1)}, u32[]{:S(2)}, u32[]{:S(2)}) %all-to-all-start.1) | async-done | bytes 131104 | tf_op jit(solution)/shard_map/while/body/eval_jaxpr/all_to_all | solution.py:514
  308.5 4.1 all-to-all-start
  316.7 6.0 %all-to-all-done = f32[128,2,128]{2,1,0:T(2,128)S(1)} async-done(((f32[128,2,128]{2,1,0:T(2,128)}), f32[128,2,128]{2,1,0:T(2,128)S(1)}, u32[]{:S(2)}, u32[]{:S(2)}) %all-to-all-start) | async-done | bytes 131104 | tf_op jit(solution)/shard_map/while/body/eval_jaxpr/all_to_all | solution.py:514
  324.2 4.1 all-to-all-start.1
  332.4 6.0 %all-to-all-done.1 = f32[128,2,128]{2,1,0:T(2,128)S(1)} async-done(((f32[128,2,128]{2,1,0:T(2,128)}), f32[128,2,128]{2,1,0:T(2,128)S(1)}, u32[]{:S(2)}, u32[]{:S(2)}) %all-to-all-start.1) | async-done | bytes 131104 | tf_op jit(solution)/shard_map/while/body/eval_jaxpr/all_to_all | solution.py:514
  339.7 4.1 all-to-all-start
  347.9 6.0 %all-to-all-done = f32[128,2,128]{2,1,0:T(2,128)S(1)} async-done(((f32[128,2,128]{2,1,0:T(2,128)}), f32[128,2,128]{2,1,0:T(2,128)S(1)}, u32[]{:S(2)}, u32[]{:S(2)}) %all-to-all-start) | async-done | bytes 131104 | tf_op jit(solution)/shard_map/while/body/eval_jaxpr/all_to_all | solution.py:514
  355.3 4.1 all-to-all-start.1
  359.4 4.1 eval_jaxpr.22
  363.5 6.0 %all-to-all-done.1 = f32[128,2,128]{2,1,0:T(2,128)S(1)} async-done(((f32[128,2,128]{2,1,0:T(2,128)}), f32[128,2,128]{2,1,0:T(2,128)S(1)}, u32[]{:S(2)}, u32[]{:S(2)}) %all-to-all-start.1) | async-done | bytes 131104 | tf_op jit(solution)/shard_map/while/body/eval_jaxpr/all_to_all | solution.py:514
  370.8 4.1 all-to-all-start
  379.0 6.0 %all-to-all-done = f32[128,2,128]{2,1,0:T(2,128)S(1)} async-done(((f32[128,2,128]{2,1,0:T(2,128)}), f32[128,2,128]{2,1,0:T(2,128)S(1)}, u32[]{:S(2)}, u32[]{:S(2)}) %all-to-all-start) | async-done | bytes 131104 | tf_op jit(solution)/shard_map/while/body/eval_jaxpr/all_to_all | solution.py:514
  386.4 4.1 all-to-all-start.1
  394.6 6.0 %all-to-all-done.1 = f32[128,2,128]{2,1,0:T(2,128)S(1)} async-done(((f32[128,2,128]{2,1,0:T(2,128)}), f32[128,2,128]{2,1,0:T(2,128)S(1)}, u32[]{:S(2)}, u32[]{:S(2)}) %all-to-all-start.1) | async-done | bytes 131104 | tf_op jit(solution)/shard_map/while/body/eval_jaxpr/all_to_all | solution.py:514
  401.9 4.1 all-to-all-start
  410.1 6.0 %all-to-all-done = f32[128,2,128]{2,1,0:T(2,128)S(1)} async-done(((f32[128,2,128]{2,1,0:T(2,128)}), f32[128,2,128]{2,1,0:T(2,128)S(1)}, u32[]{:S(2)}, u32[]{:S(2)}) %all-to-all-start) | async-done | bytes 131104 | tf_op jit(solution)/shard_map/while/body/eval_jaxpr/all_to_all | solution.py:514
  417.5 4.1 all-to-all-start.1
  425.7 6.0 %all-to-all-done.1 = f32[128,2,128]{2,1,0:T(2,128)S(1)} async-done(((f32[128,2,128]{2,1,0:T(2,128)}), f32[128,2,128]{2,1,0:T(2,128)S(1)}, u32[]{:S(2)}, u32[]{:S(2)}) %all-to-all-start.1) | async-done | bytes 131104 | tf_op jit(solution)/shard_map/while/body/eval_jaxpr/all_to_all | solution.py:514
  433.1 4.1 all-to-all-start.4
  437.2 4.5 shard_map.99
  441.7 5.5 %all-to-all-done.4 = f32[128,2,128]{2,1,0:T(2,128)S(1)} async-done(((f32[128,2,128]{2,1,0:T(2,128)}), f32[128,2,128]{2,1,0:T(2,128)S(1)}, u32[]{:S(2)}, u32[]{:S(2)}) %all-to-all-start.4) | async-done | bytes 131104 | tf_op jit(solution)/shard_map/all_to_all | solution.py:514
  448.9 4.3 all-to-all-start.5
  453.1 5.5 %shard_map.101 = f32[8,32,1024]{2,1,0:T(8,128)} custom-call(bf16[8,1024,1024]{2,1,0:T(8,128)(2,1)} %get-tuple-element.662, f32[8,32,1024]{2,1,0:T(8,128)S(1)} %get-tuple-element.663, f32[8,1024]{1,0:T(8,128)S(1)} %get-tuple-element.664, f32[8,1024]{1,0:T(8,128)S(1)} %get-tuple-element.665, ...), custom_call_target="tpu_custom_call", output_to_operand_aliasing={{}: (8, {})} | custom-call | flops 400000000 | bytes 10485760 | tf_op jit(solution)/shard_map/pallas_call | solution.py:576
  458.7 5.6 %all-to-all-done.5 = f32[128,4,128]{2,1,0:T(4,128)S(1)} async-done(((f32[128,4,128]{2,1,0:T(4,128)}), f32[128,4,128]{2,1,0:T(4,128)S(1)}, u32[]{:S(2)}, u32[]{:S(2)}) %all-to-all-start.5) | async-done | bytes 262176 | tf_op jit(solution)/shard_map/all_to_all | solution.py:514
  (57 shorter events, 128.6 us)
Async XLA Ops:
  19.5 28.6 %copy-start.1 = (f32[32,512]{1,0:T(8,128)S(1)}, f32[32,512]{1,0:T(8,128)}, u32[]{:S(2)}) copy-start(f32[32,512]{1,0:T(8,128)} %get-tuple-element.364.e_ref) | copy-start | bytes 196612
  19.5 22.7 %all-to-all-start.2 = ((f32[128,4,128]{2,1,0:T(4,128)}), f32[128,4,128]{2,1,0:T(4,128)S(1)}, u32[]{:S(2)}, u32[]{:S(2)}) async-start(f32[128,4,128]{2,1,0:T(4,128)} %bitcast.32), calls=%async_computation.2 | async-start | bytes 524288 | tf_op jit(solution)/shard_map/all_to_all | solution.py:514
  31.1 0.8 copy-start
  43.8 14.4 %all-to-all-start.3 = ((f32[128,2,128]{2,1,0:T(2,128)}), f32[128,2,128]{2,1,0:T(2,128)S(1)}, u32[]{:S(2)}, u32[]{:S(2)}) async-start(f32[128,2,128]{2,1,0:T(2,128)} %bitcast.8), calls=%async_computation.3 | async-start | bytes 262144 | tf_op jit(solution)/shard_map/all_to_all | solution.py:514
  59.5 14.2 %all-to-all-start = ((f32[128,2,128]{2,1,0:T(2,128)}), f32[128,2,128]{2,1,0:T(2,128)S(1)}, u32[]{:S(2)}, u32[]{:S(2)}) async-start(f32[128,2,128]{2,1,0:T(2,128)} %bitcast.22), calls=%async_computation | async-start | bytes 262144 | tf_op jit(solution)/shard_map/while/body/eval_jaxpr/all_to_all | solution.py:514
  75.1 14.2 %all-to-all-start.1 = ((f32[128,2,128]{2,1,0:T(2,128)}), f32[128,2,128]{2,1,0:T(2,128)S(1)}, u32[]{:S(2)}, u32[]{:S(2)}) async-start(f32[128,2,128]{2,1,0:T(2,128)} %bitcast.24), calls=%async_computation.1 | async-start | bytes 262144 | tf_op jit(solution)/shard_map/while/body/eval_jaxpr/all_to_all | solution.py:514
  90.6 14.2 %all-to-all-start = ((f32[128,2,128]{2,1,0:T(2,128)}), f32[128,2,128]{2,1,0:T(2,128)S(1)}, u32[]{:S(2)}, u32[]{:S(2)}) async-start(f32[128,2,128]{2,1,0:T(2,128)} %bitcast.22), calls=%async_computation | async-start | bytes 262144 | tf_op jit(solution)/shard_map/while/body/eval_jaxpr/all_to_all | solution.py:514
  106.2 14.2 %all-to-all-start.1 = ((f32[128,2,128]{2,1,0:T(2,128)}), f32[128,2,128]{2,1,0:T(2,128)S(1)}, u32[]{:S(2)}, u32[]{:S(2)}) async-start(f32[128,2,128]{2,1,0:T(2,128)} %bitcast.24), calls=%async_computation.1 | async-start | bytes 262144 | tf_op jit(solution)/shard_map/while/body/eval_jaxpr/all_to_all | solution.py:514
  121.7 14.2 %all-to-all-start = ((f32[128,2,128]{2,1,0:T(2,128)}), f32[128,2,128]{2,1,0:T(2,128)S(1)}, u32[]{:S(2)}, u32[]{:S(2)}) async-start(f32[128,2,128]{2,1,0:T(2,128)} %bitcast.22), calls=%async_computation | async-start | bytes 262144 | tf_op jit(solution)/shard_map/while/body/eval_jaxpr/all_to_all | solution.py:514
  137.4 14.2 %all-to-all-start.1 = ((f32[128,2,128]{2,1,0:T(2,128)}), f32[128,2,128]{2,1,0:T(2,128)S(1)}, u32[]{:S(2)}, u32[]{:S(2)}) async-start(f32[128,2,128]{2,1,0:T(2,128)} %bitcast.24), calls=%async_computation.1 | async-start | bytes 262144 | tf_op jit(solution)/shard_map/while/body/eval_jaxpr/all_to_all | solution.py:514
  152.9 14.2 %all-to-all-start = ((f32[128,2,128]{2,1,0:T(2,128)}), f32[128,2,128]{2,1,0:T(2,128)S(1)}, u32[]{:S(2)}, u32[]{:S(2)}) async-start(f32[128,2,128]{2,1,0:T(2,128)} %bitcast.22), calls=%async_computation | async-start | bytes 262144 | tf_op jit(solution)/shard_map/while/body/eval_jaxpr/all_to_all | solution.py:514
  168.5 14.2 %all-to-all-start.1 = ((f32[128,2,128]{2,1,0:T(2,128)}), f32[128,2,128]{2,1,0:T(2,128)S(1)}, u32[]{:S(2)}, u32[]{:S(2)}) async-start(f32[128,2,128]{2,1,0:T(2,128)} %bitcast.24), calls=%async_computation.1 | async-start | bytes 262144 | tf_op jit(solution)/shard_map/while/body/eval_jaxpr/all_to_all | solution.py:514
  184.0 14.2 %all-to-all-start = ((f32[128,2,128]{2,1,0:T(2,128)}), f32[128,2,128]{2,1,0:T(2,128)S(1)}, u32[]{:S(2)}, u32[]{:S(2)}) async-start(f32[128,2,128]{2,1,0:T(2,128)} %bitcast.22), calls=%async_computation | async-start | bytes 262144 | tf_op jit(solution)/shard_map/while/body/eval_jaxpr/all_to_all | solution.py:514
  199.6 14.2 %all-to-all-start.1 = ((f32[128,2,128]{2,1,0:T(2,128)}), f32[128,2,128]{2,1,0:T(2,128)S(1)}, u32[]{:S(2)}, u32[]{:S(2)}) async-start(f32[128,2,128]{2,1,0:T(2,128)} %bitcast.24), calls=%async_computation.1 | async-start | bytes 262144 | tf_op jit(solution)/shard_map/while/body/eval_jaxpr/all_to_all | solution.py:514
  215.1 14.2 %all-to-all-start = ((f32[128,2,128]{2,1,0:T(2,128)}), f32[128,2,128]{2,1,0:T(2,128)S(1)}, u32[]{:S(2)}, u32[]{:S(2)}) async-start(f32[128,2,128]{2,1,0:T(2,128)} %bitcast.22), calls=%async_computation | async-start | bytes 262144 | tf_op jit(solution)/shard_map/while/body/eval_jaxpr/all_to_all | solution.py:514
  230.8 14.2 %all-to-all-start.1 = ((f32[128,2,128]{2,1,0:T(2,128)}), f32[128,2,128]{2,1,0:T(2,128)S(1)}, u32[]{:S(2)}, u32[]{:S(2)}) async-start(f32[128,2,128]{2,1,0:T(2,128)} %bitcast.24), calls=%async_computation.1 | async-start | bytes 262144 | tf_op jit(solution)/shard_map/while/body/eval_jaxpr/all_to_all | solution.py:514
  246.3 14.2 %all-to-all-start = ((f32[128,2,128]{2,1,0:T(2,128)}), f32[128,2,128]{2,1,0:T(2,128)S(1)}, u32[]{:S(2)}, u32[]{:S(2)}) async-start(f32[128,2,128]{2,1,0:T(2,128)} %bitcast.22), calls=%async_computation | async-start | bytes 262144 | tf_op jit(solution)/shard_map/while/body/eval_jaxpr/all_to_all | solution.py:514
  261.9 14.2 %all-to-all-start.1 = ((f32[128,2,128]{2,1,0:T(2,128)}), f32[128,2,128]{2,1,0:T(2,128)S(1)}, u32[]{:S(2)}, u32[]{:S(2)}) async-start(f32[128,2,128]{2,1,0:T(2,128)} %bitcast.24), calls=%async_computation.1 | async-start | bytes 262144 | tf_op jit(solution)/shard_map/while/body/eval_jaxpr/all_to_all | solution.py:514
  277.4 14.2 %all-to-all-start = ((f32[128,2,128]{2,1,0:T(2,128)}), f32[128,2,128]{2,1,0:T(2,128)S(1)}, u32[]{:S(2)}, u32[]{:S(2)}) async-start(f32[128,2,128]{2,1,0:T(2,128)} %bitcast.22), calls=%async_computation | async-start | bytes 262144 | tf_op jit(solution)/shard_map/while/body/eval_jaxpr/all_to_all | solution.py:514
  293.0 14.2 %all-to-all-start.1 = ((f32[128,2,128]{2,1,0:T(2,128)}), f32[128,2,128]{2,1,0:T(2,128)S(1)}, u32[]{:S(2)}, u32[]{:S(2)}) async-start(f32[128,2,128]{2,1,0:T(2,128)} %bitcast.24), calls=%async_computation.1 | async-start | bytes 262144 | tf_op jit(solution)/shard_map/while/body/eval_jaxpr/all_to_all | solution.py:514
  308.5 14.2 %all-to-all-start = ((f32[128,2,128]{2,1,0:T(2,128)}), f32[128,2,128]{2,1,0:T(2,128)S(1)}, u32[]{:S(2)}, u32[]{:S(2)}) async-start(f32[128,2,128]{2,1,0:T(2,128)} %bitcast.22), calls=%async_computation | async-start | bytes 262144 | tf_op jit(solution)/shard_map/while/body/eval_jaxpr/all_to_all | solution.py:514
  324.2 14.2 %all-to-all-start.1 = ((f32[128,2,128]{2,1,0:T(2,128)}), f32[128,2,128]{2,1,0:T(2,128)S(1)}, u32[]{:S(2)}, u32[]{:S(2)}) async-start(f32[128,2,128]{2,1,0:T(2,128)} %bitcast.24), calls=%async_computation.1 | async-start | bytes 262144 | tf_op jit(solution)/shard_map/while/body/eval_jaxpr/all_to_all | solution.py:514
  339.7 14.2 %all-to-all-start = ((f32[128,2,128]{2,1,0:T(2,128)}), f32[128,2,128]{2,1,0:T(2,128)S(1)}, u32[]{:S(2)}, u32[]{:S(2)}) async-start(f32[128,2,128]{2,1,0:T(2,128)} %bitcast.22), calls=%async_computation | async-start | bytes 262144 | tf_op jit(solution)/shard_map/while/body/eval_jaxpr/all_to_all | solution.py:514
  355.3 14.2 %all-to-all-start.1 = ((f32[128,2,128]{2,1,0:T(2,128)}), f32[128,2,128]{2,1,0:T(2,128)S(1)}, u32[]{:S(2)}, u32[]{:S(2)}) async-start(f32[128,2,128]{2,1,0:T(2,128)} %bitcast.24), calls=%async_computation.1 | async-start | bytes 262144 | tf_op jit(solution)/shard_map/while/body/eval_jaxpr/all_to_all | solution.py:514
  370.8 14.2 %all-to-all-start = ((f32[128,2,128]{2,1,0:T(2,128)}), f32[128,2,128]{2,1,0:T(2,128)S(1)}, u32[]{:S(2)}, u32[]{:S(2)}) async-start(f32[128,2,128]{2,1,0:T(2,128)} %bitcast.22), calls=%async_computation | async-start | bytes 262144 | tf_op jit(solution)/shard_map/while/body/eval_jaxpr/all_to_all | solution.py:514
  386.4 14.2 %all-to-all-start.1 = ((f32[128,2,128]{2,1,0:T(2,128)}), f32[128,2,128]{2,1,0:T(2,128)S(1)}, u32[]{:S(2)}, u32[]{:S(2)}) async-start(f32[128,2,128]{2,1,0:T(2,128)} %bitcast.24), calls=%async_computation.1 | async-start | bytes 262144 | tf_op jit(solution)/shard_map/while/body/eval_jaxpr/all_to_all | solution.py:514
  401.9 14.2 %all-to-all-start = ((f32[128,2,128]{2,1,0:T(2,128)}), f32[128,2,128]{2,1,0:T(2,128)S(1)}, u32[]{:S(2)}, u32[]{:S(2)}) async-start(f32[128,2,128]{2,1,0:T(2,128)} %bitcast.22), calls=%async_computation | async-start | bytes 262144 | tf_op jit(solution)/shard_map/while/body/eval_jaxpr/all_to_all | solution.py:514
  417.5 14.2 %all-to-all-start.1 = ((f32[128,2,128]{2,1,0:T(2,128)}), f32[128,2,128]{2,1,0:T(2,128)S(1)}, u32[]{:S(2)}, u32[]{:S(2)}) async-start(f32[128,2,128]{2,1,0:T(2,128)} %bitcast.24), calls=%async_computation.1 | async-start | bytes 262144 | tf_op jit(solution)/shard_map/while/body/eval_jaxpr/all_to_all | solution.py:514
  433.1 14.2 %all-to-all-start.4 = ((f32[128,2,128]{2,1,0:T(2,128)}), f32[128,2,128]{2,1,0:T(2,128)S(1)}, u32[]{:S(2)}, u32[]{:S(2)}) async-start(f32[128,2,128]{2,1,0:T(2,128)} %bitcast.10), calls=%async_computation.4 | async-start | bytes 262144 | tf_op jit(solution)/shard_map/all_to_all | solution.py:514
  448.9 15.4 %all-to-all-start.5 = ((f32[128,4,128]{2,1,0:T(4,128)}), f32[128,4,128]{2,1,0:T(4,128)S(1)}, u32[]{:S(2)}, u32[]{:S(2)}) async-start(f32[128,4,128]{2,1,0:T(4,128)} %bitcast.12), calls=%async_computation.5 | async-start | bytes 524288 | tf_op jit(solution)/shard_map/all_to_all | solution.py:514

commit v5 on v4

--- a/solution.py
+++ b/solution.py
@@ -311,41 +311,20 @@
     return dot(right_side.astype(BF16), m_edge) + right_side[:, :128] * diag_edge
 
 
-def setup_kernel(
-    me_ref, counts_ref, f0_ref, f1_ref, f2_ref, f3_ref, p_hbm, load_hbm, lo_hbm, hi_hbm, inc_hbm,
-    m_ref, diag_ref, bd_ref, bdiag_ref, load_out, lo_out, hi_out,
-    place_ref, place_t_ref, live_ref, send_ref, e_ref, val_ref,
-    ft, g, p_ref, loads, lo_ref, hi_ref, inc_ref, tag_ref, c_ref, sem,
-):
-    area = pl.program_id(0)
-    order = edge_order()
-    pairs = ((p_hbm, p_ref), (load_hbm, loads), (lo_hbm, lo_ref), (hi_hbm, hi_ref), (inc_hbm, inc_ref))
-    fetch = [
-        pltpu.make_async_copy(source, target, sem.at[n])
-        for n, (source, target) in enumerate(pairs)
-    ]
-
-    @pl.when(area == 0)
-    def _():
-        for copy in fetch:
-            copy.start()
-        fetch[0].wait()
-
-    piv = p_ref[pl.ds(area, 1), :]
+def setup_area(area, sub, stripes, piv, load, order, m_ref, diag_ref, bd_ref, ft, g):
     piv_col = jnp.transpose(jnp.broadcast_to(piv, (128, K)))
     step = 256
     count = K // step
-    stripes = (f0_ref, f1_ref, f2_ref, f3_ref)
-    head = jnp.concatenate([dot(f[0, :, :128], order) for f in stripes], axis=0)
+    head = jnp.concatenate([dot(f[sub, :, :128], order) for f in stripes], axis=0)
     g[:, :128] = (head * piv_col).astype(BF16)
     f_head = head.astype(BF16)
     for i in range(count):
         at = slice(i * step, (i + 1) * step)
         w = (i + 1) * step
         for q in range(1, w // 128):
-            part = stripes[i][0, :, 128 * q : 128 * q + 128].astype(F32)
+            part = stripes[i][sub, :, 128 * q : 128 * q + 128].astype(F32)
             g[at, 128 * q : 128 * q + 128] = (part * piv_col[at]).astype(BF16)
-        rows = jnp.concatenate([f_head[at], stripes[i][0, :, 128:]], axis=1)
+        rows = jnp.concatenate([f_head[at], stripes[i][sub, :, 128:]], axis=1)
         ft[:w, at] = jnp.transpose(rows)
     eye = iota((step, step), 0) == iota((step, step), 1)
     fix = piv - piv.astype(BF16).astype(F32)
@@ -363,11 +342,11 @@
         if i == 0:
             edge_diag = diag[:, :128]
             edge_m = block[:EDGE, :128]
-        m_ref[0, at, at] = block.astype(BF16)
+        m_ref[sub, at, at] = block.astype(BF16)
         if i:
             above = column[: i * step].astype(BF16)
-            m_ref[0, : i * step, at] = above
-            m_ref[0, at, : i * step] = jnp.transpose(above)
+            m_ref[sub, : i * step, at] = above
+            m_ref[sub, at, : i * step] = jnp.transpose(above)
     mine = (iota((NB, 128), 1) >> 4) == area
     for r in range(ROWS):
         shift = lax.rem(area * NB + (128 - r * NB), 128)
@@ -376,35 +355,60 @@
             rows = jnp.where(mine, pltpu.roll(rows, shift, 1), 0.0)
             at = pl.ds(pl.multiple_of(ITEMS * r_in + NB * area, NB), NB)
             bd_ref[at, ITEMS * r : ITEMS * r + ITEMS] = rows.astype(BF16)
-
-    @pl.when(area == 0)
+    return edge_diag, edge_part(load, m_ref[sub, :, :128], edge_diag)
+
+
+def setup_kernel(
+    me_ref, counts_ref, f0_ref, f1_ref, f2_ref, f3_ref, p_hbm, load_hbm, lo_hbm, hi_hbm, inc_hbm,
+    m_ref, diag_ref, bd_ref, bdiag_ref, load_out, lo_out, hi_out,
+    place_ref, place_t_ref, live_ref, send_ref, e_ref, val_ref,
+    ft0, g0, ft1, g1, p_ref, loads, lo_ref, hi_ref, inc_ref, tag_ref, c_ref, sem,
+):
+    pair = pl.program_id(0)
+    order = edge_order()
+
+    @pl.when(pair == 0)
     def _():
-        for copy in fetch[1:]:
+        pairs = (
+            (p_hbm, p_ref), (load_hbm, loads), (lo_hbm, lo_ref), (hi_hbm, hi_ref), (inc_hbm, inc_ref),
+        )
+        fetch = [
+            pltpu.make_async_copy(source, target, sem.at[n])
+            for n, (source, target) in enumerate(pairs)
+        ]
+        for copy in fetch:
+            copy.start()
+        for copy in fetch:
             copy.wait()
         route(me_ref, counts_ref, inc_ref, place_ref, place_t_ref, tag_ref, live_ref)
-
-    load = loads[area]
-    load = jnp.concatenate([pick(load[:, :128], order), load[:, 128:]], axis=1)
-    load_out[0] = load
-    c = edge_part(load, m_ref[0, :, :128], edge_diag)
-
-    @pl.when(area == 0)
-    def _():
         c_ref[...] = jnp.zeros_like(c_ref)
         bdiag_ref[...] = jnp.zeros_like(bdiag_ref)
         for source, out in ((lo_ref, lo_out), (hi_ref, hi_out)):
             out[:, :128] = pick(source[:, :128], order)
             out[:, 128:] = source[:, 128:]
 
-    lane_mine = (iota((S, 128), 1) >> 4) == area
-    for r in range(ROWS):
-        at = slice(ITEMS * r, ITEMS * r + ITEMS)
-        moved = pltpu.roll(c, lax.rem(area * NB + (128 - r * NB), 128), 1)
-        c_ref[:, at] = jnp.where(lane_mine, moved, c_ref[:, at])
-        moved = pltpu.roll(edge_diag, lax.rem(area * NB + (128 - r * NB), 128), 1)
-        bdiag_ref[:, at] = jnp.where(lane_mine[:1], moved, bdiag_ref[:, at])
-
-    @pl.when(area == AREA - 1)
+    stripes = (f0_ref, f1_ref, f2_ref, f3_ref)
+    found = []
+    for sub, (ft, g) in enumerate(((ft0, g0), (ft1, g1))):
+        area = 2 * pair + sub
+        piv = p_ref[pl.ds(area, 1), :]
+        load = loads[area]
+        load = jnp.concatenate([pick(load[:, :128], order), load[:, 128:]], axis=1)
+        load_out[sub] = load
+        found.append(
+            setup_area(area, sub, stripes, piv, load, order, m_ref, diag_ref, bd_ref, ft, g)
+        )
+    for sub, (edge_diag, c) in enumerate(found):
+        area = 2 * pair + sub
+        lane_mine = (iota((S, 128), 1) >> 4) == area
+        for r in range(ROWS):
+            at = slice(ITEMS * r, ITEMS * r + ITEMS)
+            shift = lax.rem(area * NB + (128 - r * NB), 128)
+            c_ref[:, at] = jnp.where(lane_mine, pltpu.roll(c, shift, 1), c_ref[:, at])
+            moved = pltpu.roll(edge_diag, shift, 1)
+            bdiag_ref[:, at] = jnp.where(lane_mine[:1], moved, bdiag_ref[:, at])
+
+    @pl.when(pair == AREA // 2 - 1)
     def _():
         open_exchange(c_ref, place_ref, tag_ref, send_ref, e_ref, val_ref)
 
@@ -513,9 +517,9 @@
     wide = ROWS * ITEMS
     exchange = lambda x: lax.all_to_all(x, BOTH, split_axis=0, concat_axis=0, tiled=True)
     me = lax.axis_index("region").astype(jnp.int32).reshape(1)
-    area_block = lambda rows: pl.BlockSpec((1, rows, K), lambda a: (a, 0, 0))
+    area_block = lambda rows: pl.BlockSpec((2, rows, K), lambda a: (a, 0, 0))
     whole = lambda *shape: pl.BlockSpec(shape, lambda a: (0,) * len(shape))
-    stripe = lambda i: pl.BlockSpec((1, K // 4, (i + 1) * K // 4), lambda a: (a, i, 0))
+    stripe = lambda i: pl.BlockSpec((2, K // 4, (i + 1) * K // 4), lambda a: (a, i, 0))
     outs = (
         (struct((AREA, K, K), BF16), area_block(K)),
         (struct((AREA, K)), whole(AREA, K)),
@@ -534,10 +538,12 @@
     (matrix, diag, bd, bd_diag, load, floor_box, ceil_box, place, place_t, live, send, e, val) = call(
         setup_kernel,
         tuple(shape for shape, _ in outs),
-        grid=(AREA,),
+        grid=(AREA // 2,),
         in_specs=[SMEM, SMEM] + [stripe(i) for i in range(4)] + [HBM] * 5,
         out_specs=tuple(spec for _, spec in outs),
         scratch_shapes=[
+            pltpu.VMEM((K, K), BF16),
+            pltpu.VMEM((K, K), BF16),
             pltpu.VMEM((K, K), BF16),
             pltpu.VMEM((K, K), BF16),
             pltpu.VMEM((AREA, K), F32),

time: 467 us -> 465 us (level)
  no operation moved by 1% of the time
where the time goes in v5:
time: 465 us; the launch traced here: 464 us
  Pallas kernels  171 us (37%)
  waiting for transfers between devices  167 us (36%)
  starting transfers between devices  123 us (26%)
    all_to_all x28, waiting for transfers between devices, on_device(): lax.all_to_all(x, BOTH, split_axis=0, concat_axis=0, tiled=True)  167 us
    all_to_all x28, starting transfers between devices, on_device(): lax.all_to_all(x, BOTH, split_axis=0, concat_axis=0, tiled=True)  123 us
    pallas_call x26, Pallas kernels, run_areas(): call(functools.partial(area_kernel, first), (part_shape, struct((S, wide)...  106 us
    pallas_call x1, Pallas kernels, on_device(): call(setup_kernel, tuple((shape for shape, _ in outs)), grid=(AREA // 2,)...  17 us
    pallas_call x12, Pallas kernels, iterate(): owner_mid(at, got, tags_at, inverse, tie, z, u_far, rec)  17 us
    pallas_call x13, Pallas kernels, iterate(): send, e, val = run_slots(z_back, place, place_t, live, val, c, bd, bd_diag)  16.8 us
    pallas_call x2, Pallas kernels, run_last(): call(functools.partial(last_kernel, first), x_shape if first else (x_shap...  10.1 us
  transfers between devices with their start and end apart: 28, of which 28 were waited for; matrix products, arithmetic and copies ran while one was open for 0% of the time, Pallas kernels for 25%

profile of v5, /device:TPU:1, one launch (start us, length us, event | category | flops | bytes accessed | tf_op | source)
XLA Modules:
  0.0 463.5 jit_solution(7121653364938728795)
XLA Ops:
  0.6 17.0 %shard_map.94 = (bf16[8,1024,1024]{2,1,0:T(8,128)(2,1)}, f32[8,1024]{1,0:T(8,128)S(1)}, bf16[512,512]{1,0:T(8,128)(2,1)S(1)}, f32[1,512]{1,0:T(1,128)S(1)}, f32[...) custom-call(s32[1]{0:T(128)} %bitcast.5.me_ref, ...), custom_call_target="tpu_custom_call" | custom-call | flops 8000000000 | bytes 35651584 | tf_op jit(solution)/shard_map/pallas_call | solution.py:538
  17.6 11.5 %all-to-all-start.2 = ((f32[128,4,128]{2,1,0:T(4,128)}), f32[128,4,128]{2,1,0:T(4,128)S(1)}, u32[]{:S(2)}, u32[]{:S(2)}) async-start(f32[128,4,128]{2,1,0:T(4,128)} %bitcast.32), calls=%async_computation.2 | async-start | bytes 524288 | tf_op jit(solution)/shard_map/all_to_all | solution.py:518
  34.1 6.2 %all-to-all-done.2 = f32[128,4,128]{2,1,0:T(4,128)S(1)} async-done(((f32[128,4,128]{2,1,0:T(4,128)}), f32[128,4,128]{2,1,0:T(4,128)S(1)}, u32[]{:S(2)}, u32[]{:S(2)}) %all-to-all-start.2) | async-done | bytes 262176 | tf_op jit(solution)/shard_map/all_to_all | solution.py:518
  41.9 4.3 all-to-all-start.3
  46.3 4.1 shard_map.97
  50.3 6.0 %all-to-all-done.3 = f32[128,2,128]{2,1,0:T(2,128)S(1)} async-done(((f32[128,2,128]{2,1,0:T(2,128)}), f32[128,2,128]{2,1,0:T(2,128)S(1)}, u32[]{:S(2)}, u32[]{:S(2)}) %all-to-all-start.3) | async-done | bytes 131104 | tf_op jit(solution)/shard_map/all_to_all | solution.py:518
  57.6 373.6 %while.27 = (s32[]{:T(128)}, f32[256,128]{1,0:T(8,128)}, f32[32,512]{1,0:T(8,128)S(1)}, f32[128,128]{1,0:T(8,128)S(1)}, f32[8,256]{1,0:T(8,128)S(1)}, /*index=5*...) while((s32[]{:T(128)}, f32[256,128]{1,0:T(8,128)}, ...), condition=%wide.region_1.0_spmd, body=%wide.region_0.0_spmd.sunk | while | flops 910000000 | bytes 25952516 | solution.py:643
  57.6 4.1 all-to-all-start
  65.8 6.0 %all-to-all-done = f32[128,2,128]{2,1,0:T(2,128)S(1)} async-done(((f32[128,2,128]{2,1,0:T(2,128)}), f32[128,2,128]{2,1,0:T(2,128)S(1)}, u32[]{:S(2)}, u32[]{:S(2)}) %all-to-all-start) | async-done | bytes 131104 | tf_op jit(solution)/shard_map/while/body/eval_jaxpr/all_to_all | solution.py:518
  73.2 4.1 all-to-all-start.1
  81.4 6.0 %all-to-all-done.1 = f32[128,2,128]{2,1,0:T(2,128)S(1)} async-done(((f32[128,2,128]{2,1,0:T(2,128)}), f32[128,2,128]{2,1,0:T(2,128)S(1)}, u32[]{:S(2)}, u32[]{:S(2)}) %all-to-all-start.1) | async-done | bytes 131104 | tf_op jit(solution)/shard_map/while/body/eval_jaxpr/all_to_all | solution.py:518
  88.8 4.1 all-to-all-start
  97.0 6.0 %all-to-all-done = f32[128,2,128]{2,1,0:T(2,128)S(1)} async-done(((f32[128,2,128]{2,1,0:T(2,128)}), f32[128,2,128]{2,1,0:T(2,128)S(1)}, u32[]{:S(2)}, u32[]{:S(2)}) %all-to-all-start) | async-done | bytes 131104 | tf_op jit(solution)/shard_map/while/body/eval_jaxpr/all_to_all | solution.py:518
  104.4 4.1 all-to-all-start.1
  112.6 6.0 %all-to-all-done.1 = f32[128,2,128]{2,1,0:T(2,128)S(1)} async-done(((f32[128,2,128]{2,1,0:T(2,128)}), f32[128,2,128]{2,1,0:T(2,128)S(1)}, u32[]{:S(2)}, u32[]{:S(2)}) %all-to-all-start.1) | async-done | bytes 131104 | tf_op jit(solution)/shard_map/while/body/eval_jaxpr/all_to_all | solution.py:518
  119.9 4.1 all-to-all-start
  128.1 6.0 %all-to-all-done = f32[128,2,128]{2,1,0:T(2,128)S(1)} async-done(((f32[128,2,128]{2,1,0:T(2,128)}), f32[128,2,128]{2,1,0:T(2,128)S(1)}, u32[]{:S(2)}, u32[]{:S(2)}) %all-to-all-start) | async-done | bytes 131104 | tf_op jit(solution)/shard_map/while/body/eval_jaxpr/all_to_all | solution.py:518
  135.5 4.1 all-to-all-start.1
  143.7 6.0 %all-to-all-done.1 = f32[128,2,128]{2,1,0:T(2,128)S(1)} async-done(((f32[128,2,128]{2,1,0:T(2,128)}), f32[128,2,128]{2,1,0:T(2,128)S(1)}, u32[]{:S(2)}, u32[]{:S(2)}) %all-to-all-start.1) | async-done | bytes 131104 | tf_op jit(solution)/shard_map/while/body/eval_jaxpr/all_to_all | solution.py:518
  151.0 4.1 all-to-all-start
  159.2 6.0 %all-to-all-done = f32[128,2,128]{2,1,0:T(2,128)S(1)} async-done(((f32[128,2,128]{2,1,0:T(2,128)}), f32[128,2,128]{2,1,0:T(2,128)S(1)}, u32[]{:S(2)}, u32[]{:S(2)}) %all-to-all-start) | async-done | bytes 131104 | tf_op jit(solution)/shard_map/while/body/eval_jaxpr/all_to_all | solution.py:518
  166.6 4.1 all-to-all-start.1
  170.8 4.1 eval_jaxpr.22
  174.8 6.0 %all-to-all-done.1 = f32[128,2,128]{2,1,0:T(2,128)S(1)} async-done(((f32[128,2,128]{2,1,0:T(2,128)}), f32[128,2,128]{2,1,0:T(2,128)S(1)}, u32[]{:S(2)}, u32[]{:S(2)}) %all-to-all-start.1) | async-done | bytes 131104 | tf_op jit(solution)/shard_map/while/body/eval_jaxpr/all_to_all | solution.py:518
  182.2 4.1 all-to-all-start
  190.4 6.0 %all-to-all-done = f32[128,2,128]{2,1,0:T(2,128)S(1)} async-done(((f32[128,2,128]{2,1,0:T(2,128)}), f32[128,2,128]{2,1,0:T(2,128)S(1)}, u32[]{:S(2)}, u32[]{:S(2)}) %all-to-all-start) | async-done | bytes 131104 | tf_op jit(solution)/shard_map/while/body/eval_jaxpr/all_to_all | solution.py:518
  197.8 4.1 all-to-all-start.1
  206.0 6.0 %all-to-all-done.1 = f32[128,2,128]{2,1,0:T(2,128)S(1)} async-done(((f32[128,2,128]{2,1,0:T(2,128)}), f32[128,2,128]{2,1,0:T(2,128)S(1)}, u32[]{:S(2)}, u32[]{:S(2)}) %all-to-all-start.1) | async-done | bytes 131104 | tf_op jit(solution)/shard_map/while/body/eval_jaxpr/all_to_all | solution.py:518
  213.3 4.1 all-to-all-start
  221.5 6.0 %all-to-all-done = f32[128,2,128]{2,1,0:T(2,128)S(1)} async-done(((f32[128,2,128]{2,1,0:T(2,128)}), f32[128,2,128]{2,1,0:T(2,128)S(1)}, u32[]{:S(2)}, u32[]{:S(2)}) %all-to-all-start) | async-done | bytes 131104 | tf_op jit(solution)/shard_map/while/body/eval_jaxpr/all_to_all | solution.py:518
  228.9 4.1 all-to-all-start.1
  233.0 4.1 eval_jaxpr.22
  237.1 6.0 %all-to-all-done.1 = f32[128,2,128]{2,1,0:T(2,128)S(1)} async-done(((f32[128,2,128]{2,1,0:T(2,128)}), f32[128,2,128]{2,1,0:T(2,128)S(1)}, u32[]{:S(2)}, u32[]{:S(2)}) %all-to-all-start.1) | async-done | bytes 131104 | tf_op jit(solution)/shard_map/while/body/eval_jaxpr/all_to_all | solution.py:518
  244.4 4.1 all-to-all-start
  252.6 6.0 %all-to-all-done = f32[128,2,128]{2,1,0:T(2,128)S(1)} async-done(((f32[128,2,128]{2,1,0:T(2,128)}), f32[128,2,128]{2,1,0:T(2,128)S(1)}, u32[]{:S(2)}, u32[]{:S(2)}) %all-to-all-start) | async-done | bytes 131104 | tf_op jit(solution)/shard_map/while/body/eval_jaxpr/all_to_all | solution.py:518
  260.0 4.1 all-to-all-start.1
  268.2 6.0 %all-to-all-done.1 = f32[128,2,128]{2,1,0:T(2,128)S(1)} async-done(((f32[128,2,128]{2,1,0:T(2,128)}), f32[128,2,128]{2,1,0:T(2,128)S(1)}, u32[]{:S(2)}, u32[]{:S(2)}) %all-to-all-start.1) | async-done | bytes 131104 | tf_op jit(solution)/shard_map/while/body/eval_jaxpr/all_to_all | solution.py:518
  275.5 4.1 all-to-all-start
  283.8 6.0 %all-to-all-done = f32[128,2,128]{2,1,0:T(2,128)S(1)} async-done(((f32[128,2,128]{2,1,0:T(2,128)}), f32[128,2,128]{2,1,0:T(2,128)S(1)}, u32[]{:S(2)}, u32[]{:S(2)}) %all-to-all-start) | async-done | bytes 131104 | tf_op jit(solution)/shard_map/while/body/eval_jaxpr/all_to_all | solution.py:518
  291.2 4.1 all-to-all-start.1
  299.4 6.0 %all-to-all-done.1 = f32[128,2,128]{2,1,0:T(2,128)S(1)} async-done(((f32[128,2,128]{2,1,0:T(2,128)}), f32[128,2,128]{2,1,0:T(2,128)S(1)}, u32[]{:S(2)}, u32[]{:S(2)}) %all-to-all-start.1) | async-done | bytes 131104 | tf_op jit(solution)/shard_map/while/body/eval_jaxpr/all_to_all | solution.py:518
  306.7 4.1 all-to-all-start
  314.9 6.0 %all-to-all-done = f32[128,2,128]{2,1,0:T(2,128)S(1)} async-done(((f32[128,2,128]{2,1,0:T(2,128)}), f32[128,2,128]{2,1,0:T(2,128)S(1)}, u32[]{:S(2)}, u32[]{:S(2)}) %all-to-all-start) | async-done | bytes 131104 | tf_op jit(solution)/shard_map/while/body/eval_jaxpr/all_to_all | solution.py:518
  322.3 4.1 all-to-all-start.1
  330.5 6.0 %all-to-all-done.1 = f32[128,2,128]{2,1,0:T(2,128)S(1)} async-done(((f32[128,2,128]{2,1,0:T(2,128)}), f32[128,2,128]{2,1,0:T(2,128)S(1)}, u32[]{:S(2)}, u32[]{:S(2)}) %all-to-all-start.1) | async-done | bytes 131104 | tf_op jit(solution)/shard_map/while/body/eval_jaxpr/all_to_all | solution.py:518
  337.8 4.1 all-to-all-start
  346.0 6.0 %all-to-all-done = f32[128,2,128]{2,1,0:T(2,128)S(1)} async-done(((f32[128,2,128]{2,1,0:T(2,128)}), f32[128,2,128]{2,1,0:T(2,128)S(1)}, u32[]{:S(2)}, u32[]{:S(2)}) %all-to-all-start) | async-done | bytes 131104 | tf_op jit(solution)/shard_map/while/body/eval_jaxpr/all_to_all | solution.py:518
  353.4 4.1 all-to-all-start.1
  361.6 6.0 %all-to-all-done.1 = f32[128,2,128]{2,1,0:T(2,128)S(1)} async-done(((f32[128,2,128]{2,1,0:T(2,128)}), f32[128,2,128]{2,1,0:T(2,128)S(1)}, u32[]{:S(2)}, u32[]{:S(2)}) %all-to-all-start.1) | async-done | bytes 131104 | tf_op jit(solution)/shard_map/while/body/eval_jaxpr/all_to_all | solution.py:518
  368.9 4.1 all-to-all-start
  377.1 6.0 %all-to-all-done = f32[128,2,128]{2,1,0:T(2,128)S(1)} async-done(((f32[128,2,128]{2,1,0:T(2,128)}), f32[128,2,128]{2,1,0:T(2,128)S(1)}, u32[]{:S(2)}, u32[]{:S(2)}) %all-to-all-start) | async-done | bytes 131104 | tf_op jit(solution)/shard_map/while/body/eval_jaxpr/all_to_all | solution.py:518
  384.6 4.1 all-to-all-start.1
  388.7 4.1 eval_jaxpr.22
  392.8 6.0 %all-to-all-done.1 = f32[128,2,128]{2,1,0:T(2,128)S(1)} async-done(((f32[128,2,128]{2,1,0:T(2,128)}), f32[128,2,128]{2,1,0:T(2,128)S(1)}, u32[]{:S(2)}, u32[]{:S(2)}) %all-to-all-start.1) | async-done | bytes 131104 | tf_op jit(solution)/shard_map/while/body/eval_jaxpr/all_to_all | solution.py:518
  400.1 4.1 all-to-all-start
  408.3 6.0 %all-to-all-done = f32[128,2,128]{2,1,0:T(2,128)S(1)} async-done(((f32[128,2,128]{2,1,0:T(2,128)}), f32[128,2,128]{2,1,0:T(2,128)S(1)}, u32[]{:S(2)}, u32[]{:S(2)}) %all-to-all-start) | async-done | bytes 131104 | tf_op jit(solution)/shard_map/while/body/eval_jaxpr/all_to_all | solution.py:518
  415.7 4.1 all-to-all-start.1
  423.9 6.0 %all-to-all-done.1 = f32[128,2,128]{2,1,0:T(2,128)S(1)} async-done(((f32[128,2,128]{2,1,0:T(2,128)}), f32[128,2,128]{2,1,0:T(2,128)S(1)}, u32[]{:S(2)}, u32[]{:S(2)}) %all-to-all-start.1) | async-done | bytes 131104 | tf_op jit(solution)/shard_map/while/body/eval_jaxpr/all_to_all | solution.py:518
  431.2 4.1 all-to-all-start.4
  435.3 4.5 shard_map.99
  439.9 5.5 %all-to-all-done.4 = f32[128,2,128]{2,1,0:T(2,128)S(1)} async-done(((f32[128,2,128]{2,1,0:T(2,128)}), f32[128,2,128]{2,1,0:T(2,128)S(1)}, u32[]{:S(2)}, u32[]{:S(2)}) %all-to-all-start.4) | async-done | bytes 131104 | tf_op jit(solution)/shard_map/all_to_all | solution.py:518
  447.0 4.3 all-to-all-start.5
  451.3 5.5 %shard_map.101 = f32[8,32,1024]{2,1,0:T(8,128)} custom-call(bf16[8,1024,1024]{2,1,0:T(8,128)(2,1)} %get-tuple-element.662, f32[8,32,1024]{2,1,0:T(8,128)S(1)} %get-tuple-element.663, f32[8,1024]{1,0:T(8,128)S(1)} %get-tuple-element.664, f32[8,1024]{1,0:T(8,128)S(1)} %get-tuple-element.665, ...), custom_call_target="tpu_custom_call", output_to_operand_aliasing={{}: (8, {})} | custom-call | flops 400000000 | bytes 10485760 | tf_op jit(solution)/shard_map/pallas_call | solution.py:582
  456.8 5.6 %all-to-all-done.5 = f32[128,4,128]{2,1,0:T(4,128)S(1)} async-done(((f32[128,4,128]{2,1,0:T(4,128)}), f32[128,4,128]{2,1,0:T(4,128)S(1)}, u32[]{:S(2)}, u32[]{:S(2)}) %all-to-all-start.5) | async-done | bytes 262176 | tf_op jit(solution)/shard_map/all_to_all | solution.py:518
  (57 shorter events, 128.6 us)
Async XLA Ops:
  17.6 28.6 %copy-start.1 = (f32[32,512]{1,0:T(8,128)S(1)}, f32[32,512]{1,0:T(8,128)}, u32[]{:S(2)}) copy-start(f32[32,512]{1,0:T(8,128)} %get-tuple-element.364.e_ref) | copy-start | bytes 196612
  17.6 22.7 %all-to-all-start.2 = ((f32[128,4,128]{2,1,0:T(4,128)}), f32[128,4,128]{2,1,0:T(4,128)S(1)}, u32[]{:S(2)}, u32[]{:S(2)}) async-start(f32[128,4,128]{2,1,0:T(4,128)} %bitcast.32), calls=%async_computation.2 | async-start | bytes 524288 | tf_op jit(solution)/shard_map/all_to_all | solution.py:518
  29.2 0.8 copy-start
  41.9 14.4 %all-to-all-start.3 = ((f32[128,2,128]{2,1,0:T(2,128)}), f32[128,2,128]{2,1,0:T(2,128)S(1)}, u32[]{:S(2)}, u32[]{:S(2)}) async-start(f32[128,2,128]{2,1,0:T(2,128)} %bitcast.8), calls=%async_computation.3 | async-start | bytes 262144 | tf_op jit(solution)/shard_map/all_to_all | solution.py:518
  57.6 14.2 %all-to-all-start = ((f32[128,2,128]{2,1,0:T(2,128)}), f32[128,2,128]{2,1,0:T(2,128)S(1)}, u32[]{:S(2)}, u32[]{:S(2)}) async-start(f32[128,2,128]{2,1,0:T(2,128)} %bitcast.22), calls=%async_computation | async-start | bytes 262144 | tf_op jit(solution)/shard_map/while/body/eval_jaxpr/all_to_all | solution.py:518
  73.2 14.2 %all-to-all-start.1 = ((f32[128,2,128]{2,1,0:T(2,128)}), f32[128,2,128]{2,1,0:T(2,128)S(1)}, u32[]{:S(2)}, u32[]{:S(2)}) async-start(f32[128,2,128]{2,1,0:T(2,128)} %bitcast.24), calls=%async_computation.1 | async-start | bytes 262144 | tf_op jit(solution)/shard_map/while/body/eval_jaxpr/all_to_all | solution.py:518
  88.8 14.2 %all-to-all-start = ((f32[128,2,128]{2,1,0:T(2,128)}), f32[128,2,128]{2,1,0:T(2,128)S(1)}, u32[]{:S(2)}, u32[]{:S(2)}) async-start(f32[128,2,128]{2,1,0:T(2,128)} %bitcast.22), calls=%async_computation | async-start | bytes 262144 | tf_op jit(solution)/shard_map/while/body/eval_jaxpr/all_to_all | solution.py:518
  104.4 14.2 %all-to-all-start.1 = ((f32[128,2,128]{2,1,0:T(2,128)}), f32[128,2,128]{2,1,0:T(2,128)S(1)}, u32[]{:S(2)}, u32[]{:S(2)}) async-start(f32[128,2,128]{2,1,0:T(2,128)} %bitcast.24), calls=%async_computation.1 | async-start | bytes 262144 | tf_op jit(solution)/shard_map/while/body/eval_jaxpr/all_to_all | solution.py:518
  119.9 14.2 %all-to-all-start = ((f32[128,2,128]{2,1,0:T(2,128)}), f32[128,2,128]{2,1,0:T(2,128)S(1)}, u32[]{:S(2)}, u32[]{:S(2)}) async-start(f32[128,2,128]{2,1,0:T(2,128)} %bitcast.22), calls=%async_computation | async-start | bytes 262144 | tf_op jit(solution)/shard_map/while/body/eval_jaxpr/all_to_all | solution.py:518
  135.5 14.2 %all-to-all-start.1 = ((f32[128,2,128]{2,1,0:T(2,128)}), f32[128,2,128]{2,1,0:T(2,128)S(1)}, u32[]{:S(2)}, u32[]{:S(2)}) async-start(f32[128,2,128]{2,1,0:T(2,128)} %bitcast.24), calls=%async_computation.1 | async-start | bytes 262144 | tf_op jit(solution)/shard_map/while/body/eval_jaxpr/all_to_all | solution.py:518
  151.0 14.2 %all-to-all-start = ((f32[128,2,128]{2,1,0:T(2,128)}), f32[128,2,128]{2,1,0:T(2,128)S(1)}, u32[]{:S(2)}, u32[]{:S(2)}) async-start(f32[128,2,128]{2,1,0:T(2,128)} %bitcast.22), calls=%async_computation | async-start | bytes 262144 | tf_op jit(solution)/shard_map/while/body/eval_jaxpr/all_to_all | solution.py:518
  166.6 14.2 %all-to-all-start.1 = ((f32[128,2,128]{2,1,0:T(2,128)}), f32[128,2,128]{2,1,0:T(2,128)S(1)}, u32[]{:S(2)}, u32[]{:S(2)}) async-start(f32[128,2,128]{2,1,0:T(2,128)} %bitcast.24), calls=%async_computation.1 | async-start | bytes 262144 | tf_op jit(solution)/shard_map/while/body/eval_jaxpr/all_to_all | solution.py:518
  182.2 14.2 %all-to-all-start = ((f32[128,2,128]{2,1,0:T(2,128)}), f32[128,2,128]{2,1,0:T(2,128)S(1)}, u32[]{:S(2)}, u32[]{:S(2)}) async-start(f32[128,2,128]{2,1,0:T(2,128)} %bitcast.22), calls=%async_computation | async-start | bytes 262144 | tf_op jit(solution)/shard_map/while/body/eval_jaxpr/all_to_all | solution.py:518
  197.8 14.2 %all-to-all-start.1 = ((f32[128,2,128]{2,1,0:T(2,128)}), f32[128,2,128]{2,1,0:T(2,128)S(1)}, u32[]{:S(2)}, u32[]{:S(2)}) async-start(f32[128,2,128]{2,1,0:T(2,128)} %bitcast.24), calls=%async_computation.1 | async-start | bytes 262144 | tf_op jit(solution)/shard_map/while/body/eval_jaxpr/all_to_all | solution.py:518
  213.3 14.2 %all-to-all-start = ((f32[128,2,128]{2,1,0:T(2,128)}), f32[128,2,128]{2,1,0:T(2,128)S(1)}, u32[]{:S(2)}, u32[]{:S(2)}) async-start(f32[128,2,128]{2,1,0:T(2,128)} %bitcast.22), calls=%async_computation | async-start | bytes 262144 | tf_op jit(solution)/shard_map/while/body/eval_jaxpr/all_to_all | solution.py:518
  228.9 14.2 %all-to-all-start.1 = ((f32[128,2,128]{2,1,0:T(2,128)}), f32[128,2,128]{2,1,0:T(2,128)S(1)}, u32[]{:S(2)}, u32[]{:S(2)}) async-start(f32[128,2,128]{2,1,0:T(2,128)} %bitcast.24), calls=%async_computation.1 | async-start | bytes 262144 | tf_op jit(solution)/shard_map/while/body/eval_jaxpr/all_to_all | solution.py:518
  244.4 14.2 %all-to-all-start = ((f32[128,2,128]{2,1,0:T(2,128)}), f32[128,2,128]{2,1,0:T(2,128)S(1)}, u32[]{:S(2)}, u32[]{:S(2)}) async-start(f32[128,2,128]{2,1,0:T(2,128)} %bitcast.22), calls=%async_computation | async-start | bytes 262144 | tf_op jit(solution)/shard_map/while/body/eval_jaxpr/all_to_all | solution.py:518
  260.0 14.2 %all-to-all-start.1 = ((f32[128,2,128]{2,1,0:T(2,128)}), f32[128,2,128]{2,1,0:T(2,128)S(1)}, u32[]{:S(2)}, u32[]{:S(2)}) async-start(f32[128,2,128]{2,1,0:T(2,128)} %bitcast.24), calls=%async_computation.1 | async-start | bytes 262144 | tf_op jit(solution)/shard_map/while/body/eval_jaxpr/all_to_all | solution.py:518
  275.5 14.2 %all-to-all-start = ((f32[128,2,128]{2,1,0:T(2,128)}), f32[128,2,128]{2,1,0:T(2,128)S(1)}, u32[]{:S(2)}, u32[]{:S(2)}) async-start(f32[128,2,128]{2,1,0:T(2,128)} %bitcast.22), calls=%async_computation | async-start | bytes 262144 | tf_op jit(solution)/shard_map/while/body/eval_jaxpr/all_to_all | solution.py:518
  291.2 14.2 %all-to-all-start.1 = ((f32[128,2,128]{2,1,0:T(2,128)}), f32[128,2,128]{2,1,0:T(2,128)S(1)}, u32[]{:S(2)}, u32[]{:S(2)}) async-start(f32[128,2,128]{2,1,0:T(2,128)} %bitcast.24), calls=%async_computation.1 | async-start | bytes 262144 | tf_op jit(solution)/shard_map/while/body/eval_jaxpr/all_to_all | solution.py:518
  306.7 14.2 %all-to-all-start = ((f32[128,2,128]{2,1,0:T(2,128)}), f32[128,2,128]{2,1,0:T(2,128)S(1)}, u32[]{:S(2)}, u32[]{:S(2)}) async-start(f32[128,2,128]{2,1,0:T(2,128)} %bitcast.22), calls=%async_computation | async-start | bytes 262144 | tf_op jit(solution)/shard_map/while/body/eval_jaxpr/all_to_all | solution.py:518
  322.3 14.2 %all-to-all-start.1 = ((f32[128,2,128]{2,1,0:T(2,128)}), f32[128,2,128]{2,1,0:T(2,128)S(1)}, u32[]{:S(2)}, u32[]{:S(2)}) async-start(f32[128,2,128]{2,1,0:T(2,128)} %bitcast.24), calls=%async_computation.1 | async-start | bytes 262144 | tf_op jit(solution)/shard_map/while/body/eval_jaxpr/all_to_all | solution.py:518
  337.8 14.2 %all-to-all-start = ((f32[128,2,128]{2,1,0:T(2,128)}), f32[128,2,128]{2,1,0:T(2,128)S(1)}, u32[]{:S(2)}, u32[]{:S(2)}) async-start(f32[128,2,128]{2,1,0:T(2,128)} %bitcast.22), calls=%async_computation | async-start | bytes 262144 | tf_op jit(solution)/shard_map/while/body/eval_jaxpr/all_to_all | solution.py:518
  353.4 14.2 %all-to-all-start.1 = ((f32[128,2,128]{2,1,0:T(2,128)}), f32[128,2,128]{2,1,0:T(2,128)S(1)}, u32[]{:S(2)}, u32[]{:S(2)}) async-start(f32[128,2,128]{2,1,0:T(2,128)} %bitcast.24), calls=%async_computation.1 | async-start | bytes 262144 | tf_op jit(solution)/shard_map/while/body/eval_jaxpr/all_to_all | solution.py:518
  368.9 14.2 %all-to-all-start = ((f32[128,2,128]{2,1,0:T(2,128)}), f32[128,2,128]{2,1,0:T(2,128)S(1)}, u32[]{:S(2)}, u32[]{:S(2)}) async-start(f32[128,2,128]{2,1,0:T(2,128)} %bitcast.22), calls=%async_computation | async-start | bytes 262144 | tf_op jit(solution)/shard_map/while/body/eval_jaxpr/all_to_all | solution.py:518
  384.6 14.2 %all-to-all-start.1 = ((f32[128,2,128]{2,1,0:T(2,128)}), f32[128,2,128]{2,1,0:T(2,128)S(1)}, u32[]{:S(2)}, u32[]{:S(2)}) async-start(f32[128,2,128]{2,1,0:T(2,128)} %bitcast.24), calls=%async_computation.1 | async-start | bytes 262144 | tf_op jit(solution)/shard_map/while/body/eval_jaxpr/all_to_all | solution.py:518
  400.1 14.2 %all-to-all-start = ((f32[128,2,128]{2,1,0:T(2,128)}), f32[128,2,128]{2,1,0:T(2,128)S(1)}, u32[]{:S(2)}, u32[]{:S(2)}) async-start(f32[128,2,128]{2,1,0:T(2,128)} %bitcast.22), calls=%async_computation | async-start | bytes 262144 | tf_op jit(solution)/shard_map/while/body/eval_jaxpr/all_to_all | solution.py:518
  415.7 14.2 %all-to-all-start.1 = ((f32[128,2,128]{2,1,0:T(2,128)}), f32[128,2,128]{2,1,0:T(2,128)S(1)}, u32[]{:S(2)}, u32[]{:S(2)}) async-start(f32[128,2,128]{2,1,0:T(2,128)} %bitcast.24), calls=%async_computation.1 | async-start | bytes 262144 | tf_op jit(solution)/shard_map/while/body/eval_jaxpr/all_to_all | solution.py:518
  431.2 14.2 %all-to-all-start.4 = ((f32[128,2,128]{2,1,0:T(2,128)}), f32[128,2,128]{2,1,0:T(2,128)S(1)}, u32[]{:S(2)}, u32[]{:S(2)}) async-start(f32[128,2,128]{2,1,0:T(2,128)} %bitcast.10), calls=%async_computation.4 | async-start | bytes 262144 | tf_op jit(solution)/shard_map/all_to_all | solution.py:518
  447.0 15.4 %all-to-all-start.5 = ((f32[128,4,128]{2,1,0:T(4,128)}), f32[128,4,128]{2,1,0:T(4,128)S(1)}, u32[]{:S(2)}, u32[]{:S(2)}) async-start(f32[128,4,128]{2,1,0:T(4,128)} %bitcast.12), calls=%async_computation.5 | async-start | bytes 524288 | tf_op jit(solution)/shard_map/all_to_all | solution.py:518

commit v6 on v5

--- a/solution.py
+++ b/solution.py
@@ -359,27 +359,16 @@
 
 
 def setup_kernel(
-    me_ref, counts_ref, f0_ref, f1_ref, f2_ref, f3_ref, p_hbm, load_hbm, lo_hbm, hi_hbm, inc_hbm,
+    me_ref, counts_ref, f0_ref, f1_ref, f2_ref, f3_ref, p_ref, load_ref, lo_ref, hi_ref, inc_ref,
     m_ref, diag_ref, bd_ref, bdiag_ref, load_out, lo_out, hi_out,
     place_ref, place_t_ref, live_ref, send_ref, e_ref, val_ref,
-    ft0, g0, ft1, g1, p_ref, loads, lo_ref, hi_ref, inc_ref, tag_ref, c_ref, sem,
+    ft0, g0, ft1, g1, tag_ref, c_ref,
 ):
     pair = pl.program_id(0)
     order = edge_order()
 
     @pl.when(pair == 0)
     def _():
-        pairs = (
-            (p_hbm, p_ref), (load_hbm, loads), (lo_hbm, lo_ref), (hi_hbm, hi_ref), (inc_hbm, inc_ref),
-        )
-        fetch = [
-            pltpu.make_async_copy(source, target, sem.at[n])
-            for n, (source, target) in enumerate(pairs)
-        ]
-        for copy in fetch:
-            copy.start()
-        for copy in fetch:
-            copy.wait()
         route(me_ref, counts_ref, inc_ref, place_ref, place_t_ref, tag_ref, live_ref)
         c_ref[...] = jnp.zeros_like(c_ref)
         bdiag_ref[...] = jnp.zeros_like(bdiag_ref)
@@ -392,7 +381,7 @@
     for sub, (ft, g) in enumerate(((ft0, g0), (ft1, g1))):
         area = 2 * pair + sub
         piv = p_ref[pl.ds(area, 1), :]
-        load = loads[area]
+        load = load_ref[sub]
         load = jnp.concatenate([pick(load[:, :128], order), load[:, 128:]], axis=1)
         load_out[sub] = load
         found.append(
@@ -539,21 +528,16 @@
         setup_kernel,
         tuple(shape for shape, _ in outs),
         grid=(AREA // 2,),
-        in_specs=[SMEM, SMEM] + [stripe(i) for i in range(4)] + [HBM] * 5,
+        in_specs=[SMEM, SMEM] + [stripe(i) for i in range(4)]
+        + [whole(AREA, K), area_block(S), whole(AREA, K), whole(AREA, K), whole(AREA, NB)],
         out_specs=tuple(spec for _, spec in outs),
         scratch_shapes=[
             pltpu.VMEM((K, K), BF16),
             pltpu.VMEM((K, K), BF16),
             pltpu.VMEM((K, K), BF16),
             pltpu.VMEM((K, K), BF16),
-            pltpu.VMEM((AREA, K), F32),
-            pltpu.VMEM((AREA, S, K), F32),
-            pltpu.VMEM((AREA, K), F32),
-            pltpu.VMEM((AREA, K), F32),
-            pltpu.VMEM((AREA, NB), jnp.int32),
             pltpu.VMEM((2, ITEMS), F32),
             pltpu.VMEM((S, wide), F32),
-            pltpu.SemaphoreType.DMA((5,)),
         ],
         cost_estimate=cost(8 * 10**9, 34 * 2**20),
         limit=60,

time: 465 us -> 463 us (level)
  no operation moved by 1% of the time
where the time goes in v6:
time: 463 us; the launch traced here: 462 us
  Pallas kernels  170 us (37%)
  waiting for transfers between devices  167 us (36%)
  starting transfers between devices  123 us (27%)
    all_to_all x28, waiting for transfers between devices, on_device(): lax.all_to_all(x, BOTH, split_axis=0, concat_axis=0, tiled=True)  167 us
    all_to_all x28, starting transfers between devices, on_device(): lax.all_to_all(x, BOTH, split_axis=0, concat_axis=0, tiled=True)  123 us
    pallas_call x26, Pallas kernels, run_areas(): call(functools.partial(area_kernel, first), (part_shape, struct((S, wide)...  106 us
    pallas_call x12, Pallas kernels, iterate(): owner_mid(at, got, tags_at, inverse, tie, z, u_far, rec)  17 us
    pallas_call x13, Pallas kernels, iterate(): send, e, val = run_slots(z_back, place, place_t, live, val, c, bd, bd_diag)  16.8 us
    pallas_call x1, Pallas kernels, on_device(): call(setup_kernel, tuple((shape for shape, _ in outs)), grid=(AREA // 2,)...  15.5 us
    pallas_call x2, Pallas kernels, run_last(): call(functools.partial(last_kernel, first), x_shape if first else (x_shap...  10.1 us
  transfers between devices with their start and end apart: 28, of which 28 were waited for; matrix products, arithmetic and copies ran while one was open for 0% of the time, Pallas kernels for 25%

profile of v6, /device:TPU:1, one launch (start us, length us, event | category | flops | bytes accessed | tf_op | source)
XLA Modules:
  0.0 462.1 jit_solution(15262940274205289023)
XLA Ops:
  0.6 15.5 %shard_map.94 = (bf16[8,1024,1024]{2,1,0:T(8,128)(2,1)}, f32[8,1024]{1,0:T(8,128)S(1)}, bf16[512,512]{1,0:T(8,128)(2,1)S(1)}, f32[1,512]{1,0:T(1,128)S(1)}, f32[...) custom-call(s32[1]{0:T(128)} %bitcast.5.me_ref, ...), custom_call_target="tpu_custom_call" | custom-call | flops 8000000000 | bytes 35651584 | tf_op jit(solution)/shard_map/pallas_call | solution.py:527
  16.2 11.5 %all-to-all-start.2 = ((f32[128,4,128]{2,1,0:T(4,128)}), f32[128,4,128]{2,1,0:T(4,128)S(1)}, u32[]{:S(2)}, u32[]{:S(2)}) async-start(f32[128,4,128]{2,1,0:T(4,128)} %bitcast.32), calls=%async_computation.2 | async-start | bytes 524288 | tf_op jit(solution)/shard_map/all_to_all | solution.py:507
  32.7 6.2 %all-to-all-done.2 = f32[128,4,128]{2,1,0:T(4,128)S(1)} async-done(((f32[128,4,128]{2,1,0:T(4,128)}), f32[128,4,128]{2,1,0:T(4,128)S(1)}, u32[]{:S(2)}, u32[]{:S(2)}) %all-to-all-start.2) | async-done | bytes 262176 | tf_op jit(solution)/shard_map/all_to_all | solution.py:507
  40.5 4.3 all-to-all-start.3
  48.9 6.0 %all-to-all-done.3 = f32[128,2,128]{2,1,0:T(2,128)S(1)} async-done(((f32[128,2,128]{2,1,0:T(2,128)}), f32[128,2,128]{2,1,0:T(2,128)S(1)}, u32[]{:S(2)}, u32[]{:S(2)}) %all-to-all-start.3) | async-done | bytes 131104 | tf_op jit(solution)/shard_map/all_to_all | solution.py:507
  56.2 373.6 %while.27 = (s32[]{:T(128)}, f32[256,128]{1,0:T(8,128)}, f32[32,512]{1,0:T(8,128)S(1)}, f32[128,128]{1,0:T(8,128)S(1)}, f32[8,256]{1,0:T(8,128)S(1)}, /*index=5*...) while((s32[]{:T(128)}, f32[256,128]{1,0:T(8,128)}, ...), condition=%wide.region_1.0_spmd, body=%wide.region_0.0_spmd.sunk | while | flops 910000000 | bytes 25952516 | solution.py:627
  56.2 4.1 all-to-all-start
  64.4 6.0 %all-to-all-done = f32[128,2,128]{2,1,0:T(2,128)S(1)} async-done(((f32[128,2,128]{2,1,0:T(2,128)}), f32[128,2,128]{2,1,0:T(2,128)S(1)}, u32[]{:S(2)}, u32[]{:S(2)}) %all-to-all-start) | async-done | bytes 131104 | tf_op jit(solution)/shard_map/while/body/eval_jaxpr/all_to_all | solution.py:507
  71.8 4.1 all-to-all-start.1
  80.0 6.0 %all-to-all-done.1 = f32[128,2,128]{2,1,0:T(2,128)S(1)} async-done(((f32[128,2,128]{2,1,0:T(2,128)}), f32[128,2,128]{2,1,0:T(2,128)S(1)}, u32[]{:S(2)}, u32[]{:S(2)}) %all-to-all-start.1) | async-done | bytes 131104 | tf_op jit(solution)/shard_map/while/body/eval_jaxpr/all_to_all | solution.py:507
  87.3 4.1 all-to-all-start
  95.5 6.0 %all-to-all-done = f32[128,2,128]{2,1,0:T(2,128)S(1)} async-done(((f32[128,2,128]{2,1,0:T(2,128)}), f32[128,2,128]{2,1,0:T(2,128)S(1)}, u32[]{:S(2)}, u32[]{:S(2)}) %all-to-all-start) | async-done | bytes 131104 | tf_op jit(solution)/shard_map/while/body/eval_jaxpr/all_to_all | solution.py:507
  102.9 4.1 all-to-all-start.1
  111.1 6.0 %all-to-all-done.1 = f32[128,2,128]{2,1,0:T(2,128)S(1)} async-done(((f32[128,2,128]{2,1,0:T(2,128)}), f32[128,2,128]{2,1,0:T(2,128)S(1)}, u32[]{:S(2)}, u32[]{:S(2)}) %all-to-all-start.1) | async-done | bytes 131104 | tf_op jit(solution)/shard_map/while/body/eval_jaxpr/all_to_all | solution.py:507
  118.4 4.1 all-to-all-start
  126.6 6.0 %all-to-all-done = f32[128,2,128]{2,1,0:T(2,128)S(1)} async-done(((f32[128,2,128]{2,1,0:T(2,128)}), f32[128,2,128]{2,1,0:T(2,128)S(1)}, u32[]{:S(2)}, u32[]{:S(2)}) %all-to-all-start) | async-done | bytes 131104 | tf_op jit(solution)/shard_map/while/body/eval_jaxpr/all_to_all | solution.py:507
  134.0 4.1 all-to-all-start.1
  142.2 6.0 %all-to-all-done.1 = f32[128,2,128]{2,1,0:T(2,128)S(1)} async-done(((f32[128,2,128]{2,1,0:T(2,128)}), f32[128,2,128]{2,1,0:T(2,128)S(1)}, u32[]{:S(2)}, u32[]{:S(2)}) %all-to-all-start.1) | async-done | bytes 131104 | tf_op jit(solution)/shard_map/while/body/eval_jaxpr/all_to_all | solution.py:507
  149.6 4.1 all-to-all-start
  157.8 6.0 %all-to-all-done = f32[128,2,128]{2,1,0:T(2,128)S(1)} async-done(((f32[128,2,128]{2,1,0:T(2,128)}), f32[128,2,128]{2,1,0:T(2,128)S(1)}, u32[]{:S(2)}, u32[]{:S(2)}) %all-to-all-start) | async-done | bytes 131104 | tf_op jit(solution)/shard_map/while/body/eval_jaxpr/all_to_all | solution.py:507
  165.2 4.1 all-to-all-start.1
  173.4 6.0 %all-to-all-done.1 = f32[128,2,128]{2,1,0:T(2,128)S(1)} async-done(((f32[128,2,128]{2,1,0:T(2,128)}), f32[128,2,128]{2,1,0:T(2,128)S(1)}, u32[]{:S(2)}, u32[]{:S(2)}) %all-to-all-start.1) | async-done | bytes 131104 | tf_op jit(solution)/shard_map/while/body/eval_jaxpr/all_to_all | solution.py:507
  180.7 4.1 all-to-all-start
  188.9 6.0 %all-to-all-done = f32[128,2,128]{2,1,0:T(2,128)S(1)} async-done(((f32[128,2,128]{2,1,0:T(2,128)}), f32[128,2,128]{2,1,0:T(2,128)S(1)}, u32[]{:S(2)}, u32[]{:S(2)}) %all-to-all-start) | async-done | bytes 131104 | tf_op jit(solution)/shard_map/while/body/eval_jaxpr/all_to_all | solution.py:507
  196.3 4.1 all-to-all-start.1
  200.4 4.1 eval_jaxpr.22
  204.5 6.0 %all-to-all-done.1 = f32[128,2,128]{2,1,0:T(2,128)S(1)} async-done(((f32[128,2,128]{2,1,0:T(2,128)}), f32[128,2,128]{2,1,0:T(2,128)S(1)}, u32[]{:S(2)}, u32[]{:S(2)}) %all-to-all-start.1) | async-done | bytes 131104 | tf_op jit(solution)/shard_map/while/body/eval_jaxpr/all_to_all | solution.py:507
  211.8 4.1 all-to-all-start
  220.0 6.0 %all-to-all-done = f32[128,2,128]{2,1,0:T(2,128)S(1)} async-done(((f32[128,2,128]{2,1,0:T(2,128)}), f32[128,2,128]{2,1,0:T(2,128)S(1)}, u32[]{:S(2)}, u32[]{:S(2)}) %all-to-all-start) | async-done | bytes 131104 | tf_op jit(solution)/shard_map/while/body/eval_jaxpr/all_to_all | solution.py:507
  227.4 4.1 all-to-all-start.1
  235.6 6.0 %all-to-all-done.1 = f32[128,2,128]{2,1,0:T(2,128)S(1)} async-done(((f32[128,2,128]{2,1,0:T(2,128)}), f32[128,2,128]{2,1,0:T(2,128)S(1)}, u32[]{:S(2)}, u32[]{:S(2)}) %all-to-all-start.1) | async-done | bytes 131104 | tf_op jit(solution)/shard_map/while/body/eval_jaxpr/all_to_all | solution.py:507
  243.0 4.1 all-to-all-start
  251.2 6.0 %all-to-all-done = f32[128,2,128]{2,1,0:T(2,128)S(1)} async-done(((f32[128,2,128]{2,1,0:T(2,128)}), f32[128,2,128]{2,1,0:T(2,128)S(1)}, u32[]{:S(2)}, u32[]{:S(2)}) %all-to-all-start) | async-done | bytes 131104 | tf_op jit(solution)/shard_map/while/body/eval_jaxpr/all_to_all | solution.py:507
  258.6 4.1 all-to-all-start.1
  262.7 4.1 eval_jaxpr.22
  266.8 6.0 %all-to-all-done.1 = f32[128,2,128]{2,1,0:T(2,128)S(1)} async-done(((f32[128,2,128]{2,1,0:T(2,128)}), f32[128,2,128]{2,1,0:T(2,128)S(1)}, u32[]{:S(2)}, u32[]{:S(2)}) %all-to-all-start.1) | async-done | bytes 131104 | tf_op jit(solution)/shard_map/while/body/eval_jaxpr/all_to_all | solution.py:507
  274.1 4.1 all-to-all-start
  282.3 6.0 %all-to-all-done = f32[128,2,128]{2,1,0:T(2,128)S(1)} async-done(((f32[128,2,128]{2,1,0:T(2,128)}), f32[128,2,128]{2,1,0:T(2,128)S(1)}, u32[]{:S(2)}, u32[]{:S(2)}) %all-to-all-start) | async-done | bytes 131104 | tf_op jit(solution)/shard_map/while/body/eval_jaxpr/all_to_all | solution.py:507
  289.7 4.1 all-to-all-start.1
  297.9 6.0 %all-to-all-done.1 = f32[128,2,128]{2,1,0:T(2,128)S(1)} async-done(((f32[128,2,128]{2,1,0:T(2,128)}), f32[128,2,128]{2,1,0:T(2,128)S(1)}, u32[]{:S(2)}, u32[]{:S(2)}) %all-to-all-start.1) | async-done | bytes 131104 | tf_op jit(solution)/shard_map/while/body/eval_jaxpr/all_to_all | solution.py:507
  305.2 4.1 all-to-all-start
  313.4 6.0 %all-to-all-done = f32[128,2,128]{2,1,0:T(2,128)S(1)} async-done(((f32[128,2,128]{2,1,0:T(2,128)}), f32[128,2,128]{2,1,0:T(2,128)S(1)}, u32[]{:S(2)}, u32[]{:S(2)}) %all-to-all-start) | async-done | bytes 131104 | tf_op jit(solution)/shard_map/while/body/eval_jaxpr/all_to_all | solution.py:507
  320.8 4.1 all-to-all-start.1
  329.0 6.0 %all-to-all-done.1 = f32[128,2,128]{2,1,0:T(2,128)S(1)} async-done(((f32[128,2,128]{2,1,0:T(2,128)}), f32[128,2,128]{2,1,0:T(2,128)S(1)}, u32[]{:S(2)}, u32[]{:S(2)}) %all-to-all-start.1) | async-done | bytes 131104 | tf_op jit(solution)/shard_map/while/body/eval_jaxpr/all_to_all | solution.py:507
  336.3 4.1 all-to-all-start
  344.6 6.0 %all-to-all-done = f32[128,2,128]{2,1,0:T(2,128)S(1)} async-done(((f32[128,2,128]{2,1,0:T(2,128)}), f32[128,2,128]{2,1,0:T(2,128)S(1)}, u32[]{:S(2)}, u32[]{:S(2)}) %all-to-all-start) | async-done | bytes 131104 | tf_op jit(solution)/shard_map/while/body/eval_jaxpr/all_to_all | solution.py:507
  352.0 4.1 all-to-all-start.1
  356.1 4.1 eval_jaxpr.22
  360.2 6.0 %all-to-all-done.1 = f32[128,2,128]{2,1,0:T(2,128)S(1)} async-done(((f32[128,2,128]{2,1,0:T(2,128)}), f32[128,2,128]{2,1,0:T(2,128)S(1)}, u32[]{:S(2)}, u32[]{:S(2)}) %all-to-all-start.1) | async-done | bytes 131104 | tf_op jit(solution)/shard_map/while/body/eval_jaxpr/all_to_all | solution.py:507
  367.5 4.1 all-to-all-start
  375.7 6.0 %all-to-all-done = f32[128,2,128]{2,1,0:T(2,128)S(1)} async-done(((f32[128,2,128]{2,1,0:T(2,128)}), f32[128,2,128]{2,1,0:T(2,128)S(1)}, u32[]{:S(2)}, u32[]{:S(2)}) %all-to-all-start) | async-done | bytes 131104 | tf_op jit(solution)/shard_map/while/body/eval_jaxpr/all_to_all | solution.py:507
  383.1 4.1 all-to-all-start.1
  391.3 6.0 %all-to-all-done.1 = f32[128,2,128]{2,1,0:T(2,128)S(1)} async-done(((f32[128,2,128]{2,1,0:T(2,128)}), f32[128,2,128]{2,1,0:T(2,128)S(1)}, u32[]{:S(2)}, u32[]{:S(2)}) %all-to-all-start.1) | async-done | bytes 131104 | tf_op jit(solution)/shard_map/while/body/eval_jaxpr/all_to_all | solution.py:507
  398.6 4.1 all-to-all-start
  406.8 6.0 %all-to-all-done = f32[128,2,128]{2,1,0:T(2,128)S(1)} async-done(((f32[128,2,128]{2,1,0:T(2,128)}), f32[128,2,128]{2,1,0:T(2,128)S(1)}, u32[]{:S(2)}, u32[]{:S(2)}) %all-to-all-start) | async-done | bytes 131104 | tf_op jit(solution)/shard_map/while/body/eval_jaxpr/all_to_all | solution.py:507
  414.2 4.1 all-to-all-start.1
  418.4 4.1 eval_jaxpr.22
  422.4 6.0 %all-to-all-done.1 = f32[128,2,128]{2,1,0:T(2,128)S(1)} async-done(((f32[128,2,128]{2,1,0:T(2,128)}), f32[128,2,128]{2,1,0:T(2,128)S(1)}, u32[]{:S(2)}, u32[]{:S(2)}) %all-to-all-start.1) | async-done | bytes 131104 | tf_op jit(solution)/shard_map/while/body/eval_jaxpr/all_to_all | solution.py:507
  429.7 4.1 all-to-all-start.4
  433.9 4.5 shard_map.99
  438.4 5.5 %all-to-all-done.4 = f32[128,2,128]{2,1,0:T(2,128)S(1)} async-done(((f32[128,2,128]{2,1,0:T(2,128)}), f32[128,2,128]{2,1,0:T(2,128)S(1)}, u32[]{:S(2)}, u32[]{:S(2)}) %all-to-all-start.4) | async-done | bytes 131104 | tf_op jit(solution)/shard_map/all_to_all | solution.py:507
  445.5 4.3 all-to-all-start.5
  449.8 5.5 %shard_map.101 = f32[8,32,1024]{2,1,0:T(8,128)} custom-call(bf16[8,1024,1024]{2,1,0:T(8,128)(2,1)} %get-tuple-element.662, f32[8,32,1024]{2,1,0:T(8,128)S(1)} %get-tuple-element.663, f32[8,1024]{1,0:T(8,128)S(1)} %get-tuple-element.664, f32[8,1024]{1,0:T(8,128)S(1)} %get-tuple-element.665, ...), custom_call_target="tpu_custom_call", output_to_operand_aliasing={{}: (8, {})} | custom-call | flops 400000000 | bytes 10485760 | tf_op jit(solution)/shard_map/pallas_call | solution.py:566
  455.4 5.6 %all-to-all-done.5 = f32[128,4,128]{2,1,0:T(4,128)S(1)} async-done(((f32[128,4,128]{2,1,0:T(4,128)}), f32[128,4,128]{2,1,0:T(4,128)S(1)}, u32[]{:S(2)}, u32[]{:S(2)}) %all-to-all-start.5) | async-done | bytes 262176 | tf_op jit(solution)/shard_map/all_to_all | solution.py:507
  (57 shorter events, 128.6 us)
Async XLA Ops:
  16.2 28.6 %copy-start.1 = (f32[32,512]{1,0:T(8,128)S(1)}, f32[32,512]{1,0:T(8,128)}, u32[]{:S(2)}) copy-start(f32[32,512]{1,0:T(8,128)} %get-tuple-element.364.e_ref) | copy-start | bytes 196612
  16.2 22.7 %all-to-all-start.2 = ((f32[128,4,128]{2,1,0:T(4,128)}), f32[128,4,128]{2,1,0:T(4,128)S(1)}, u32[]{:S(2)}, u32[]{:S(2)}) async-start(f32[128,4,128]{2,1,0:T(4,128)} %bitcast.32), calls=%async_computation.2 | async-start | bytes 524288 | tf_op jit(solution)/shard_map/all_to_all | solution.py:507
  27.7 0.8 copy-start
  40.5 14.4 %all-to-all-start.3 = ((f32[128,2,128]{2,1,0:T(2,128)}), f32[128,2,128]{2,1,0:T(2,128)S(1)}, u32[]{:S(2)}, u32[]{:S(2)}) async-start(f32[128,2,128]{2,1,0:T(2,128)} %bitcast.8), calls=%async_computation.3 | async-start | bytes 262144 | tf_op jit(solution)/shard_map/all_to_all | solution.py:507
  56.2 14.2 %all-to-all-start = ((f32[128,2,128]{2,1,0:T(2,128)}), f32[128,2,128]{2,1,0:T(2,128)S(1)}, u32[]{:S(2)}, u32[]{:S(2)}) async-start(f32[128,2,128]{2,1,0:T(2,128)} %bitcast.22), calls=%async_computation | async-start | bytes 262144 | tf_op jit(solution)/shard_map/while/body/eval_jaxpr/all_to_all | solution.py:507
  71.8 14.2 %all-to-all-start.1 = ((f32[128,2,128]{2,1,0:T(2,128)}), f32[128,2,128]{2,1,0:T(2,128)S(1)}, u32[]{:S(2)}, u32[]{:S(2)}) async-start(f32[128,2,128]{2,1,0:T(2,128)} %bitcast.24), calls=%async_computation.1 | async-start | bytes 262144 | tf_op jit(solution)/shard_map/while/body/eval_jaxpr/all_to_all | solution.py:507
  87.3 14.2 %all-to-all-start = ((f32[128,2,128]{2,1,0:T(2,128)}), f32[128,2,128]{2,1,0:T(2,128)S(1)}, u32[]{:S(2)}, u32[]{:S(2)}) async-start(f32[128,2,128]{2,1,0:T(2,128)} %bitcast.22), calls=%async_computation | async-start | bytes 262144 | tf_op jit(solution)/shard_map/while/body/eval_jaxpr/all_to_all | solution.py:507
  102.9 14.2 %all-to-all-start.1 = ((f32[128,2,128]{2,1,0:T(2,128)}), f32[128,2,128]{2,1,0:T(2,128)S(1)}, u32[]{:S(2)}, u32[]{:S(2)}) async-start(f32[128,2,128]{2,1,0:T(2,128)} %bitcast.24), calls=%async_computation.1 | async-start | bytes 262144 | tf_op jit(solution)/shard_map/while/body/eval_jaxpr/all_to_all | solution.py:507
  118.4 14.2 %all-to-all-start = ((f32[128,2,128]{2,1,0:T(2,128)}), f32[128,2,128]{2,1,0:T(2,128)S(1)}, u32[]{:S(2)}, u32[]{:S(2)}) async-start(f32[128,2,128]{2,1,0:T(2,128)} %bitcast.22), calls=%async_computation | async-start | bytes 262144 | tf_op jit(solution)/shard_map/while/body/eval_jaxpr/all_to_all | solution.py:507
  134.0 14.2 %all-to-all-start.1 = ((f32[128,2,128]{2,1,0:T(2,128)}), f32[128,2,128]{2,1,0:T(2,128)S(1)}, u32[]{:S(2)}, u32[]{:S(2)}) async-start(f32[128,2,128]{2,1,0:T(2,128)} %bitcast.24), calls=%async_computation.1 | async-start | bytes 262144 | tf_op jit(solution)/shard_map/while/body/eval_jaxpr/all_to_all | solution.py:507
  149.6 14.2 %all-to-all-start = ((f32[128,2,128]{2,1,0:T(2,128)}), f32[128,2,128]{2,1,0:T(2,128)S(1)}, u32[]{:S(2)}, u32[]{:S(2)}) async-start(f32[128,2,128]{2,1,0:T(2,128)} %bitcast.22), calls=%async_computation | async-start | bytes 262144 | tf_op jit(solution)/shard_map/while/body/eval_jaxpr/all_to_all | solution.py:507
  165.2 14.2 %all-to-all-start.1 = ((f32[128,2,128]{2,1,0:T(2,128)}), f32[128,2,128]{2,1,0:T(2,128)S(1)}, u32[]{:S(2)}, u32[]{:S(2)}) async-start(f32[128,2,128]{2,1,0:T(2,128)} %bitcast.24), calls=%async_computation.1 | async-start | bytes 262144 | tf_op jit(solution)/shard_map/while/body/eval_jaxpr/all_to_all | solution.py:507
  180.7 14.2 %all-to-all-start = ((f32[128,2,128]{2,1,0:T(2,128)}), f32[128,2,128]{2,1,0:T(2,128)S(1)}, u32[]{:S(2)}, u32[]{:S(2)}) async-start(f32[128,2,128]{2,1,0:T(2,128)} %bitcast.22), calls=%async_computation | async-start | bytes 262144 | tf_op jit(solution)/shard_map/while/body/eval_jaxpr/all_to_all | solution.py:507
  196.3 14.2 %all-to-all-start.1 = ((f32[128,2,128]{2,1,0:T(2,128)}), f32[128,2,128]{2,1,0:T(2,128)S(1)}, u32[]{:S(2)}, u32[]{:S(2)}) async-start(f32[128,2,128]{2,1,0:T(2,128)} %bitcast.24), calls=%async_computation.1 | async-start | bytes 262144 | tf_op jit(solution)/shard_map/while/body/eval_jaxpr/all_to_all | solution.py:507
  211.8 14.2 %all-to-all-start = ((f32[128,2,128]{2,1,0:T(2,128)}), f32[128,2,128]{2,1,0:T(2,128)S(1)}, u32[]{:S(2)}, u32[]{:S(2)}) async-start(f32[128,2,128]{2,1,0:T(2,128)} %bitcast.22), calls=%async_computation | async-start | bytes 262144 | tf_op jit(solution)/shard_map/while/body/eval_jaxpr/all_to_all | solution.py:507
  227.4 14.2 %all-to-all-start.1 = ((f32[128,2,128]{2,1,0:T(2,128)}), f32[128,2,128]{2,1,0:T(2,128)S(1)}, u32[]{:S(2)}, u32[]{:S(2)}) async-start(f32[128,2,128]{2,1,0:T(2,128)} %bitcast.24), calls=%async_computation.1 | async-start | bytes 262144 | tf_op jit(solution)/shard_map/while/body/eval_jaxpr/all_to_all | solution.py:507
  243.0 14.2 %all-to-all-start = ((f32[128,2,128]{2,1,0:T(2,128)}), f32[128,2,128]{2,1,0:T(2,128)S(1)}, u32[]{:S(2)}, u32[]{:S(2)}) async-start(f32[128,2,128]{2,1,0:T(2,128)} %bitcast.22), calls=%async_computation | async-start | bytes 262144 | tf_op jit(solution)/shard_map/while/body/eval_jaxpr/all_to_all | solution.py:507
  258.6 14.2 %all-to-all-start.1 = ((f32[128,2,128]{2,1,0:T(2,128)}), f32[128,2,128]{2,1,0:T(2,128)S(1)}, u32[]{:S(2)}, u32[]{:S(2)}) async-start(f32[128,2,128]{2,1,0:T(2,128)} %bitcast.24), calls=%async_computation.1 | async-start | bytes 262144 | tf_op jit(solution)/shard_map/while/body/eval_jaxpr/all_to_all | solution.py:507
  274.1 14.2 %all-to-all-start = ((f32[128,2,128]{2,1,0:T(2,128)}), f32[128,2,128]{2,1,0:T(2,128)S(1)}, u32[]{:S(2)}, u32[]{:S(2)}) async-start(f32[128,2,128]{2,1,0:T(2,128)} %bitcast.22), calls=%async_computation | async-start | bytes 262144 | tf_op jit(solution)/shard_map/while/body/eval_jaxpr/all_to_all | solution.py:507
  289.7 14.2 %all-to-all-start.1 = ((f32[128,2,128]{2,1,0:T(2,128)}), f32[128,2,128]{2,1,0:T(2,128)S(1)}, u32[]{:S(2)}, u32[]{:S(2)}) async-start(f32[128,2,128]{2,1,0:T(2,128)} %bitcast.24), calls=%async_computation.1 | async-start | bytes 262144 | tf_op jit(solution)/shard_map/while/body/eval_jaxpr/all_to_all | solution.py:507
  305.2 14.2 %all-to-all-start = ((f32[128,2,128]{2,1,0:T(2,128)}), f32[128,2,128]{2,1,0:T(2,128)S(1)}, u32[]{:S(2)}, u32[]{:S(2)}) async-start(f32[128,2,128]{2,1,0:T(2,128)} %bitcast.22), calls=%async_computation | async-start | bytes 262144 | tf_op jit(solution)/shard_map/while/body/eval_jaxpr/all_to_all | solution.py:507
  320.8 14.2 %all-to-all-start.1 = ((f32[128,2,128]{2,1,0:T(2,128)}), f32[128,2,128]{2,1,0:T(2,128)S(1)}, u32[]{:S(2)}, u32[]{:S(2)}) async-start(f32[128,2,128]{2,1,0:T(2,128)} %bitcast.24), calls=%async_computation.1 | async-start | bytes 262144 | tf_op jit(solution)/shard_map/while/body/eval_jaxpr/all_to_all | solution.py:507
  336.3 14.2 %all-to-all-start = ((f32[128,2,128]{2,1,0:T(2,128)}), f32[128,2,128]{2,1,0:T(2,128)S(1)}, u32[]{:S(2)}, u32[]{:S(2)}) async-start(f32[128,2,128]{2,1,0:T(2,128)} %bitcast.22), calls=%async_computation | async-start | bytes 262144 | tf_op jit(solution)/shard_map/while/body/eval_jaxpr/all_to_all | solution.py:507
  352.0 14.2 %all-to-all-start.1 = ((f32[128,2,128]{2,1,0:T(2,128)}), f32[128,2,128]{2,1,0:T(2,128)S(1)}, u32[]{:S(2)}, u32[]{:S(2)}) async-start(f32[128,2,128]{2,1,0:T(2,128)} %bitcast.24), calls=%async_computation.1 | async-start | bytes 262144 | tf_op jit(solution)/shard_map/while/body/eval_jaxpr/all_to_all | solution.py:507
  367.5 14.2 %all-to-all-start = ((f32[128,2,128]{2,1,0:T(2,128)}), f32[128,2,128]{2,1,0:T(2,128)S(1)}, u32[]{:S(2)}, u32[]{:S(2)}) async-start(f32[128,2,128]{2,1,0:T(2,128)} %bitcast.22), calls=%async_computation | async-start | bytes 262144 | tf_op jit(solution)/shard_map/while/body/eval_jaxpr/all_to_all | solution.py:507
  383.1 14.2 %all-to-all-start.1 = ((f32[128,2,128]{2,1,0:T(2,128)}), f32[128,2,128]{2,1,0:T(2,128)S(1)}, u32[]{:S(2)}, u32[]{:S(2)}) async-start(f32[128,2,128]{2,1,0:T(2,128)} %bitcast.24), calls=%async_computation.1 | async-start | bytes 262144 | tf_op jit(solution)/shard_map/while/body/eval_jaxpr/all_to_all | solution.py:507
  398.6 14.2 %all-to-all-start = ((f32[128,2,128]{2,1,0:T(2,128)}), f32[128,2,128]{2,1,0:T(2,128)S(1)}, u32[]{:S(2)}, u32[]{:S(2)}) async-start(f32[128,2,128]{2,1,0:T(2,128)} %bitcast.22), calls=%async_computation | async-start | bytes 262144 | tf_op jit(solution)/shard_map/while/body/eval_jaxpr/all_to_all | solution.py:507
  414.2 14.2 %all-to-all-start.1 = ((f32[128,2,128]{2,1,0:T(2,128)}), f32[128,2,128]{2,1,0:T(2,128)S(1)}, u32[]{:S(2)}, u32[]{:S(2)}) async-start(f32[128,2,128]{2,1,0:T(2,128)} %bitcast.24), calls=%async_computation.1 | async-start | bytes 262144 | tf_op jit(solution)/shard_map/while/body/eval_jaxpr/all_to_all | solution.py:507
  429.7 14.2 %all-to-all-start.4 = ((f32[128,2,128]{2,1,0:T(2,128)}), f32[128,2,128]{2,1,0:T(2,128)S(1)}, u32[]{:S(2)}, u32[]{:S(2)}) async-start(f32[128,2,128]{2,1,0:T(2,128)} %bitcast.10), calls=%async_computation.4 | async-start | bytes 262144 | tf_op jit(solution)/shard_map/all_to_all | solution.py:507
  445.5 15.4 %all-to-all-start.5 = ((f32[128,4,128]{2,1,0:T(4,128)}), f32[128,4,128]{2,1,0:T(4,128)S(1)}, u32[]{:S(2)}, u32[]{:S(2)}) async-start(f32[128,4,128]{2,1,0:T(4,128)} %bitcast.12), calls=%async_computation.5 | async-start | bytes 524288 | tf_op jit(solution)/shard_map/all_to_all | solution.py:507

commit v7 on v6

--- a/solution.py
+++ b/solution.py
@@ -45,6 +45,14 @@
     count = x.shape[0]
     got = dot(jnp.concatenate(split3(x), axis=0), onehot)
     return got[:count] + got[count : 2 * count] + got[2 * count :]
+
+
+def place_by(x, onehot):
+    count = x.shape[0]
+    high = x.astype(BF16)
+    low = (x - high.astype(F32)).astype(BF16)
+    got = dot(jnp.concatenate([high, low], axis=0), onehot)
+    return got[:count] + got[count:]
 
 
 def iota(shape, dim):
@@ -275,7 +283,7 @@
 def take_means(z_ref, pt_ref, width):
     near = z_ref[pl.ds(0, WORLD, stride=width), :]
     far = z_ref[pl.ds(1, WORLD, stride=width), :]
-    return pick(jnp.concatenate([near, far], axis=1), pt_ref[...])
+    return place_by(jnp.concatenate([near, far], axis=1), pt_ref[...])
 
 
 def slot_kernel(
@@ -291,7 +299,7 @@
     edge = c_ref[...] + e * bdiag_ref[...] + both[:S] + both[S:]
     val = by_row(edge) + u
     val_ref[...] = val
-    send = pick(val, p_ref[...])
+    send = place_by(val, p_ref[...])
     send_ref[pl.ds(0, WORLD, stride=2), :] = send[:, :128]
     send_ref[pl.ds(1, WORLD, stride=2), :] = send[:, 128:]
 

time: 463 us -> 462 us (level)
  no operation moved by 1% of the time
where the time goes in v7:
time: 462 us; the launch traced here: 460 us
  Pallas kernels  168 us (36%)
  waiting for transfers between devices  167 us (36%)
  starting transfers between devices  123 us (27%)
    all_to_all x28, waiting for transfers between devices, on_device(): lax.all_to_all(x, BOTH, split_axis=0, concat_axis=0, tiled=True)  167 us
    all_to_all x28, starting transfers between devices, on_device(): lax.all_to_all(x, BOTH, split_axis=0, concat_axis=0, tiled=True)  123 us
    pallas_call x26, Pallas kernels, run_areas(): call(functools.partial(area_kernel, first), (part_shape, struct((S, wide)...  106 us
    pallas_call x12, Pallas kernels, iterate(): owner_mid(at, got, tags_at, inverse, tie, z, u_far, rec)  17 us
    pallas_call x1, Pallas kernels, on_device(): call(setup_kernel, tuple((shape for shape, _ in outs)), grid=(AREA // 2,)...  15.5 us
    pallas_call x13, Pallas kernels, iterate(): send, e, val = run_slots(z_back, place, place_t, live, val, c, bd, bd_diag)  15.3 us
    pallas_call x2, Pallas kernels, run_last(): call(functools.partial(last_kernel, first), x_shape if first else (x_shap...  10.1 us
  transfers between devices with their start and end apart: 28, of which 28 were waited for; matrix products, arithmetic and copies ran while one was open for 0% of the time, Pallas kernels for 25%

profile of v7, /device:TPU:1, one launch (start us, length us, event | category | flops | bytes accessed | tf_op | source)
XLA Modules:
  0.0 460.5 jit_solution(14011053537395407936)
XLA Ops:
  0.6 15.5 %shard_map.94 = (bf16[8,1024,1024]{2,1,0:T(8,128)(2,1)}, f32[8,1024]{1,0:T(8,128)S(1)}, bf16[512,512]{1,0:T(8,128)(2,1)S(1)}, f32[1,512]{1,0:T(1,128)S(1)}, f32[...) custom-call(s32[1]{0:T(128)} %bitcast.5.me_ref, ...), custom_call_target="tpu_custom_call" | custom-call | flops 8000000000 | bytes 35651584 | tf_op jit(solution)/shard_map/pallas_call | solution.py:535
  16.2 11.5 %all-to-all-start.2 = ((f32[128,4,128]{2,1,0:T(4,128)}), f32[128,4,128]{2,1,0:T(4,128)S(1)}, u32[]{:S(2)}, u32[]{:S(2)}) async-start(f32[128,4,128]{2,1,0:T(4,128)} %bitcast.32), calls=%async_computation.2 | async-start | bytes 524288 | tf_op jit(solution)/shard_map/all_to_all | solution.py:515
  32.7 6.2 %all-to-all-done.2 = f32[128,4,128]{2,1,0:T(4,128)S(1)} async-done(((f32[128,4,128]{2,1,0:T(4,128)}), f32[128,4,128]{2,1,0:T(4,128)S(1)}, u32[]{:S(2)}, u32[]{:S(2)}) %all-to-all-start.2) | async-done | bytes 262176 | tf_op jit(solution)/shard_map/all_to_all | solution.py:515
  40.5 4.3 all-to-all-start.3
  48.9 6.0 %all-to-all-done.3 = f32[128,2,128]{2,1,0:T(2,128)S(1)} async-done(((f32[128,2,128]{2,1,0:T(2,128)}), f32[128,2,128]{2,1,0:T(2,128)S(1)}, u32[]{:S(2)}, u32[]{:S(2)}) %all-to-all-start.3) | async-done | bytes 131104 | tf_op jit(solution)/shard_map/all_to_all | solution.py:515
  56.0 372.1 %while.27 = (s32[]{:T(128)}, f32[256,128]{1,0:T(8,128)}, f32[32,512]{1,0:T(8,128)S(1)}, f32[128,128]{1,0:T(8,128)S(1)}, f32[8,256]{1,0:T(8,128)S(1)}, /*index=5*...) while((s32[]{:T(128)}, f32[256,128]{1,0:T(8,128)}, ...), condition=%wide.region_1.0_spmd, body=%wide.region_0.0_spmd.sunk | while | flops 910000000 | bytes 25952516 | solution.py:635
  56.1 4.1 all-to-all-start
  64.3 6.0 %all-to-all-done = f32[128,2,128]{2,1,0:T(2,128)S(1)} async-done(((f32[128,2,128]{2,1,0:T(2,128)}), f32[128,2,128]{2,1,0:T(2,128)S(1)}, u32[]{:S(2)}, u32[]{:S(2)}) %all-to-all-start) | async-done | bytes 131104 | tf_op jit(solution)/shard_map/while/body/eval_jaxpr/all_to_all | solution.py:515
  71.7 4.1 all-to-all-start.1
  75.8 4.1 eval_jaxpr.22
  79.9 6.0 %all-to-all-done.1 = f32[128,2,128]{2,1,0:T(2,128)S(1)} async-done(((f32[128,2,128]{2,1,0:T(2,128)}), f32[128,2,128]{2,1,0:T(2,128)S(1)}, u32[]{:S(2)}, u32[]{:S(2)}) %all-to-all-start.1) | async-done | bytes 131104 | tf_op jit(solution)/shard_map/while/body/eval_jaxpr/all_to_all | solution.py:515
  87.1 4.1 all-to-all-start
  91.2 4.1 eval_jaxpr.20
  95.3 6.0 %all-to-all-done = f32[128,2,128]{2,1,0:T(2,128)S(1)} async-done(((f32[128,2,128]{2,1,0:T(2,128)}), f32[128,2,128]{2,1,0:T(2,128)S(1)}, u32[]{:S(2)}, u32[]{:S(2)}) %all-to-all-start) | async-done | bytes 131104 | tf_op jit(solution)/shard_map/while/body/eval_jaxpr/all_to_all | solution.py:515
  102.7 4.1 all-to-all-start.1
  110.9 6.0 %all-to-all-done.1 = f32[128,2,128]{2,1,0:T(2,128)S(1)} async-done(((f32[128,2,128]{2,1,0:T(2,128)}), f32[128,2,128]{2,1,0:T(2,128)S(1)}, u32[]{:S(2)}, u32[]{:S(2)}) %all-to-all-start.1) | async-done | bytes 131104 | tf_op jit(solution)/shard_map/while/body/eval_jaxpr/all_to_all | solution.py:515
  118.1 4.1 all-to-all-start
  126.3 6.0 %all-to-all-done = f32[128,2,128]{2,1,0:T(2,128)S(1)} async-done(((f32[128,2,128]{2,1,0:T(2,128)}), f32[128,2,128]{2,1,0:T(2,128)S(1)}, u32[]{:S(2)}, u32[]{:S(2)}) %all-to-all-start) | async-done | bytes 131104 | tf_op jit(solution)/shard_map/while/body/eval_jaxpr/all_to_all | solution.py:515
  133.7 4.1 all-to-all-start.1
  141.9 6.0 %all-to-all-done.1 = f32[128,2,128]{2,1,0:T(2,128)S(1)} async-done(((f32[128,2,128]{2,1,0:T(2,128)}), f32[128,2,128]{2,1,0:T(2,128)S(1)}, u32[]{:S(2)}, u32[]{:S(2)}) %all-to-all-start.1) | async-done | bytes 131104 | tf_op jit(solution)/shard_map/while/body/eval_jaxpr/all_to_all | solution.py:515
  149.1 4.1 all-to-all-start
  157.3 6.0 %all-to-all-done = f32[128,2,128]{2,1,0:T(2,128)S(1)} async-done(((f32[128,2,128]{2,1,0:T(2,128)}), f32[128,2,128]{2,1,0:T(2,128)S(1)}, u32[]{:S(2)}, u32[]{:S(2)}) %all-to-all-start) | async-done | bytes 131104 | tf_op jit(solution)/shard_map/while/body/eval_jaxpr/all_to_all | solution.py:515
  164.7 4.1 all-to-all-start.1
  172.9 6.0 %all-to-all-done.1 = f32[128,2,128]{2,1,0:T(2,128)S(1)} async-done(((f32[128,2,128]{2,1,0:T(2,128)}), f32[128,2,128]{2,1,0:T(2,128)S(1)}, u32[]{:S(2)}, u32[]{:S(2)}) %all-to-all-start.1) | async-done | bytes 131104 | tf_op jit(solution)/shard_map/while/body/eval_jaxpr/all_to_all | solution.py:515
  180.1 4.1 all-to-all-start
  188.3 6.0 %all-to-all-done = f32[128,2,128]{2,1,0:T(2,128)S(1)} async-done(((f32[128,2,128]{2,1,0:T(2,128)}), f32[128,2,128]{2,1,0:T(2,128)S(1)}, u32[]{:S(2)}, u32[]{:S(2)}) %all-to-all-start) | async-done | bytes 131104 | tf_op jit(solution)/shard_map/while/body/eval_jaxpr/all_to_all | solution.py:515
  195.7 4.1 all-to-all-start.1
  203.9 6.0 %all-to-all-done.1 = f32[128,2,128]{2,1,0:T(2,128)S(1)} async-done(((f32[128,2,128]{2,1,0:T(2,128)}), f32[128,2,128]{2,1,0:T(2,128)S(1)}, u32[]{:S(2)}, u32[]{:S(2)}) %all-to-all-start.1) | async-done | bytes 131104 | tf_op jit(solution)/shard_map/while/body/eval_jaxpr/all_to_all | solution.py:515
  211.1 4.1 all-to-all-start
  219.3 6.0 %all-to-all-done = f32[128,2,128]{2,1,0:T(2,128)S(1)} async-done(((f32[128,2,128]{2,1,0:T(2,128)}), f32[128,2,128]{2,1,0:T(2,128)S(1)}, u32[]{:S(2)}, u32[]{:S(2)}) %all-to-all-start) | async-done | bytes 131104 | tf_op jit(solution)/shard_map/while/body/eval_jaxpr/all_to_all | solution.py:515
  226.7 4.1 all-to-all-start.1
  234.9 6.0 %all-to-all-done.1 = f32[128,2,128]{2,1,0:T(2,128)S(1)} async-done(((f32[128,2,128]{2,1,0:T(2,128)}), f32[128,2,128]{2,1,0:T(2,128)S(1)}, u32[]{:S(2)}, u32[]{:S(2)}) %all-to-all-start.1) | async-done | bytes 131104 | tf_op jit(solution)/shard_map/while/body/eval_jaxpr/all_to_all | solution.py:515
  242.1 4.1 all-to-all-start
  250.3 6.0 %all-to-all-done = f32[128,2,128]{2,1,0:T(2,128)S(1)} async-done(((f32[128,2,128]{2,1,0:T(2,128)}), f32[128,2,128]{2,1,0:T(2,128)S(1)}, u32[]{:S(2)}, u32[]{:S(2)}) %all-to-all-start) | async-done | bytes 131104 | tf_op jit(solution)/shard_map/while/body/eval_jaxpr/all_to_all | solution.py:515
  257.7 4.1 all-to-all-start.1
  261.9 4.1 eval_jaxpr.22
  265.9 6.0 %all-to-all-done.1 = f32[128,2,128]{2,1,0:T(2,128)S(1)} async-done(((f32[128,2,128]{2,1,0:T(2,128)}), f32[128,2,128]{2,1,0:T(2,128)S(1)}, u32[]{:S(2)}, u32[]{:S(2)}) %all-to-all-start.1) | async-done | bytes 131104 | tf_op jit(solution)/shard_map/while/body/eval_jaxpr/all_to_all | solution.py:515
  273.1 4.1 all-to-all-start
  281.3 6.0 %all-to-all-done = f32[128,2,128]{2,1,0:T(2,128)S(1)} async-done(((f32[128,2,128]{2,1,0:T(2,128)}), f32[128,2,128]{2,1,0:T(2,128)S(1)}, u32[]{:S(2)}, u32[]{:S(2)}) %all-to-all-start) | async-done | bytes 131104 | tf_op jit(solution)/shard_map/while/body/eval_jaxpr/all_to_all | solution.py:515
  288.7 4.1 all-to-all-start.1
  296.9 6.0 %all-to-all-done.1 = f32[128,2,128]{2,1,0:T(2,128)S(1)} async-done(((f32[128,2,128]{2,1,0:T(2,128)}), f32[128,2,128]{2,1,0:T(2,128)S(1)}, u32[]{:S(2)}, u32[]{:S(2)}) %all-to-all-start.1) | async-done | bytes 131104 | tf_op jit(solution)/shard_map/while/body/eval_jaxpr/all_to_all | solution.py:515
  304.1 4.1 all-to-all-start
  312.3 6.0 %all-to-all-done = f32[128,2,128]{2,1,0:T(2,128)S(1)} async-done(((f32[128,2,128]{2,1,0:T(2,128)}), f32[128,2,128]{2,1,0:T(2,128)S(1)}, u32[]{:S(2)}, u32[]{:S(2)}) %all-to-all-start) | async-done | bytes 131104 | tf_op jit(solution)/shard_map/while/body/eval_jaxpr/all_to_all | solution.py:515
  319.8 4.1 all-to-all-start.1
  328.0 6.0 %all-to-all-done.1 = f32[128,2,128]{2,1,0:T(2,128)S(1)} async-done(((f32[128,2,128]{2,1,0:T(2,128)}), f32[128,2,128]{2,1,0:T(2,128)S(1)}, u32[]{:S(2)}, u32[]{:S(2)}) %all-to-all-start.1) | async-done | bytes 131104 | tf_op jit(solution)/shard_map/while/body/eval_jaxpr/all_to_all | solution.py:515
  335.2 4.1 all-to-all-start
  343.4 6.0 %all-to-all-done = f32[128,2,128]{2,1,0:T(2,128)S(1)} async-done(((f32[128,2,128]{2,1,0:T(2,128)}), f32[128,2,128]{2,1,0:T(2,128)S(1)}, u32[]{:S(2)}, u32[]{:S(2)}) %all-to-all-start) | async-done | bytes 131104 | tf_op jit(solution)/shard_map/while/body/eval_jaxpr/all_to_all | solution.py:515
  350.8 4.1 all-to-all-start.1
  354.9 4.1 eval_jaxpr.22
  359.0 6.0 %all-to-all-done.1 = f32[128,2,128]{2,1,0:T(2,128)S(1)} async-done(((f32[128,2,128]{2,1,0:T(2,128)}), f32[128,2,128]{2,1,0:T(2,128)S(1)}, u32[]{:S(2)}, u32[]{:S(2)}) %all-to-all-start.1) | async-done | bytes 131104 | tf_op jit(solution)/shard_map/while/body/eval_jaxpr/all_to_all | solution.py:515
  366.2 4.1 all-to-all-start
  374.4 6.0 %all-to-all-done = f32[128,2,128]{2,1,0:T(2,128)S(1)} async-done(((f32[128,2,128]{2,1,0:T(2,128)}), f32[128,2,128]{2,1,0:T(2,128)S(1)}, u32[]{:S(2)}, u32[]{:S(2)}) %all-to-all-start) | async-done | bytes 131104 | tf_op jit(solution)/shard_map/while/body/eval_jaxpr/all_to_all | solution.py:515
  381.8 4.1 all-to-all-start.1
  390.0 6.0 %all-to-all-done.1 = f32[128,2,128]{2,1,0:T(2,128)S(1)} async-done(((f32[128,2,128]{2,1,0:T(2,128)}), f32[128,2,128]{2,1,0:T(2,128)S(1)}, u32[]{:S(2)}, u32[]{:S(2)}) %all-to-all-start.1) | async-done | bytes 131104 | tf_op jit(solution)/shard_map/while/body/eval_jaxpr/all_to_all | solution.py:515
  397.2 4.1 all-to-all-start
  405.4 6.0 %all-to-all-done = f32[128,2,128]{2,1,0:T(2,128)S(1)} async-done(((f32[128,2,128]{2,1,0:T(2,128)}), f32[128,2,128]{2,1,0:T(2,128)S(1)}, u32[]{:S(2)}, u32[]{:S(2)}) %all-to-all-start) | async-done | bytes 131104 | tf_op jit(solution)/shard_map/while/body/eval_jaxpr/all_to_all | solution.py:515
  412.8 4.1 all-to-all-start.1
  421.0 6.0 %all-to-all-done.1 = f32[128,2,128]{2,1,0:T(2,128)S(1)} async-done(((f32[128,2,128]{2,1,0:T(2,128)}), f32[128,2,128]{2,1,0:T(2,128)S(1)}, u32[]{:S(2)}, u32[]{:S(2)}) %all-to-all-start.1) | async-done | bytes 131104 | tf_op jit(solution)/shard_map/while/body/eval_jaxpr/all_to_all | solution.py:515
  428.2 4.1 all-to-all-start.4
  432.3 4.5 shard_map.99
  436.9 5.5 %all-to-all-done.4 = f32[128,2,128]{2,1,0:T(2,128)S(1)} async-done(((f32[128,2,128]{2,1,0:T(2,128)}), f32[128,2,128]{2,1,0:T(2,128)S(1)}, u32[]{:S(2)}, u32[]{:S(2)}) %all-to-all-start.4) | async-done | bytes 131104 | tf_op jit(solution)/shard_map/all_to_all | solution.py:515
  444.0 4.3 all-to-all-start.5
  448.3 5.5 %shard_map.101 = f32[8,32,1024]{2,1,0:T(8,128)} custom-call(bf16[8,1024,1024]{2,1,0:T(8,128)(2,1)} %get-tuple-element.662, f32[8,32,1024]{2,1,0:T(8,128)S(1)} %get-tuple-element.663, f32[8,1024]{1,0:T(8,128)S(1)} %get-tuple-element.664, f32[8,1024]{1,0:T(8,128)S(1)} %get-tuple-element.665, ...), custom_call_target="tpu_custom_call", output_to_operand_aliasing={{}: (8, {})} | custom-call | flops 400000000 | bytes 10485760 | tf_op jit(solution)/shard_map/pallas_call | solution.py:574
  453.8 5.6 %all-to-all-done.5 = f32[128,4,128]{2,1,0:T(4,128)S(1)} async-done(((f32[128,4,128]{2,1,0:T(4,128)}), f32[128,4,128]{2,1,0:T(4,128)S(1)}, u32[]{:S(2)}, u32[]{:S(2)}) %all-to-all-start.5) | async-done | bytes 262176 | tf_op jit(solution)/shard_map/all_to_all | solution.py:515
  (57 shorter events, 127.0 us)
Async XLA Ops:
  16.2 28.6 %copy-start.1 = (f32[32,512]{1,0:T(8,128)S(1)}, f32[32,512]{1,0:T(8,128)}, u32[]{:S(2)}) copy-start(f32[32,512]{1,0:T(8,128)} %get-tuple-element.364.e_ref) | copy-start | bytes 196612
  16.2 22.7 %all-to-all-start.2 = ((f32[128,4,128]{2,1,0:T(4,128)}), f32[128,4,128]{2,1,0:T(4,128)S(1)}, u32[]{:S(2)}, u32[]{:S(2)}) async-start(f32[128,4,128]{2,1,0:T(4,128)} %bitcast.32), calls=%async_computation.2 | async-start | bytes 524288 | tf_op jit(solution)/shard_map/all_to_all | solution.py:515
  27.7 0.8 copy-start
  40.5 14.4 %all-to-all-start.3 = ((f32[128,2,128]{2,1,0:T(2,128)}), f32[128,2,128]{2,1,0:T(2,128)S(1)}, u32[]{:S(2)}, u32[]{:S(2)}) async-start(f32[128,2,128]{2,1,0:T(2,128)} %bitcast.8), calls=%async_computation.3 | async-start | bytes 262144 | tf_op jit(solution)/shard_map/all_to_all | solution.py:515
  56.1 14.2 %all-to-all-start = ((f32[128,2,128]{2,1,0:T(2,128)}), f32[128,2,128]{2,1,0:T(2,128)S(1)}, u32[]{:S(2)}, u32[]{:S(2)}) async-start(f32[128,2,128]{2,1,0:T(2,128)} %bitcast.22), calls=%async_computation | async-start | bytes 262144 | tf_op jit(solution)/shard_map/while/body/eval_jaxpr/all_to_all | solution.py:515
  71.7 14.2 %all-to-all-start.1 = ((f32[128,2,128]{2,1,0:T(2,128)}), f32[128,2,128]{2,1,0:T(2,128)S(1)}, u32[]{:S(2)}, u32[]{:S(2)}) async-start(f32[128,2,128]{2,1,0:T(2,128)} %bitcast.24), calls=%async_computation.1 | async-start | bytes 262144 | tf_op jit(solution)/shard_map/while/body/eval_jaxpr/all_to_all | solution.py:515
  87.1 14.2 %all-to-all-start = ((f32[128,2,128]{2,1,0:T(2,128)}), f32[128,2,128]{2,1,0:T(2,128)S(1)}, u32[]{:S(2)}, u32[]{:S(2)}) async-start(f32[128,2,128]{2,1,0:T(2,128)} %bitcast.22), calls=%async_computation | async-start | bytes 262144 | tf_op jit(solution)/shard_map/while/body/eval_jaxpr/all_to_all | solution.py:515
  102.7 14.2 %all-to-all-start.1 = ((f32[128,2,128]{2,1,0:T(2,128)}), f32[128,2,128]{2,1,0:T(2,128)S(1)}, u32[]{:S(2)}, u32[]{:S(2)}) async-start(f32[128,2,128]{2,1,0:T(2,128)} %bitcast.24), calls=%async_computation.1 | async-start | bytes 262144 | tf_op jit(solution)/shard_map/while/body/eval_jaxpr/all_to_all | solution.py:515
  118.1 14.2 %all-to-all-start = ((f32[128,2,128]{2,1,0:T(2,128)}), f32[128,2,128]{2,1,0:T(2,128)S(1)}, u32[]{:S(2)}, u32[]{:S(2)}) async-start(f32[128,2,128]{2,1,0:T(2,128)} %bitcast.22), calls=%async_computation | async-start | bytes 262144 | tf_op jit(solution)/shard_map/while/body/eval_jaxpr/all_to_all | solution.py:515
  133.7 14.2 %all-to-all-start.1 = ((f32[128,2,128]{2,1,0:T(2,128)}), f32[128,2,128]{2,1,0:T(2,128)S(1)}, u32[]{:S(2)}, u32[]{:S(2)}) async-start(f32[128,2,128]{2,1,0:T(2,128)} %bitcast.24), calls=%async_computation.1 | async-start | bytes 262144 | tf_op jit(solution)/shard_map/while/body/eval_jaxpr/all_to_all | solution.py:515
  149.1 14.2 %all-to-all-start = ((f32[128,2,128]{2,1,0:T(2,128)}), f32[128,2,128]{2,1,0:T(2,128)S(1)}, u32[]{:S(2)}, u32[]{:S(2)}) async-start(f32[128,2,128]{2,1,0:T(2,128)} %bitcast.22), calls=%async_computation | async-start | bytes 262144 | tf_op jit(solution)/shard_map/while/body/eval_jaxpr/all_to_all | solution.py:515
  164.7 14.2 %all-to-all-start.1 = ((f32[128,2,128]{2,1,0:T(2,128)}), f32[128,2,128]{2,1,0:T(2,128)S(1)}, u32[]{:S(2)}, u32[]{:S(2)}) async-start(f32[128,2,128]{2,1,0:T(2,128)} %bitcast.24), calls=%async_computation.1 | async-start | bytes 262144 | tf_op jit(solution)/shard_map/while/body/eval_jaxpr/all_to_all | solution.py:515
  180.1 14.2 %all-to-all-start = ((f32[128,2,128]{2,1,0:T(2,128)}), f32[128,2,128]{2,1,0:T(2,128)S(1)}, u32[]{:S(2)}, u32[]{:S(2)}) async-start(f32[128,2,128]{2,1,0:T(2,128)} %bitcast.22), calls=%async_computation | async-start | bytes 262144 | tf_op jit(solution)/shard_map/while/body/eval_jaxpr/all_to_all | solution.py:515
  195.7 14.2 %all-to-all-start.1 = ((f32[128,2,128]{2,1,0:T(2,128)}), f32[128,2,128]{2,1,0:T(2,128)S(1)}, u32[]{:S(2)}, u32[]{:S(2)}) async-start(f32[128,2,128]{2,1,0:T(2,128)} %bitcast.24), calls=%async_computation.1 | async-start | bytes 262144 | tf_op jit(solution)/shard_map/while/body/eval_jaxpr/all_to_all | solution.py:515
  211.1 14.2 %all-to-all-start = ((f32[128,2,128]{2,1,0:T(2,128)}), f32[128,2,128]{2,1,0:T(2,128)S(1)}, u32[]{:S(2)}, u32[]{:S(2)}) async-start(f32[128,2,128]{2,1,0:T(2,128)} %bitcast.22), calls=%async_computation | async-start | bytes 262144 | tf_op jit(solution)/shard_map/while/body/eval_jaxpr/all_to_all | solution.py:515
  226.7 14.2 %all-to-all-start.1 = ((f32[128,2,128]{2,1,0:T(2,128)}), f32[128,2,128]{2,1,0:T(2,128)S(1)}, u32[]{:S(2)}, u32[]{:S(2)}) async-start(f32[128,2,128]{2,1,0:T(2,128)} %bitcast.24), calls=%async_computation.1 | async-start | bytes 262144 | tf_op jit(solution)/shard_map/while/body/eval_jaxpr/all_to_all | solution.py:515
  242.1 14.2 %all-to-all-start = ((f32[128,2,128]{2,1,0:T(2,128)}), f32[128,2,128]{2,1,0:T(2,128)S(1)}, u32[]{:S(2)}, u32[]{:S(2)}) async-start(f32[128,2,128]{2,1,0:T(2,128)} %bitcast.22), calls=%async_computation | async-start | bytes 262144 | tf_op jit(solution)/shard_map/while/body/eval_jaxpr/all_to_all | solution.py:515
  257.7 14.2 %all-to-all-start.1 = ((f32[128,2,128]{2,1,0:T(2,128)}), f32[128,2,128]{2,1,0:T(2,128)S(1)}, u32[]{:S(2)}, u32[]{:S(2)}) async-start(f32[128,2,128]{2,1,0:T(2,128)} %bitcast.24), calls=%async_computation.1 | async-start | bytes 262144 | tf_op jit(solution)/shard_map/while/body/eval_jaxpr/all_to_all | solution.py:515
  273.1 14.2 %all-to-all-start = ((f32[128,2,128]{2,1,0:T(2,128)}), f32[128,2,128]{2,1,0:T(2,128)S(1)}, u32[]{:S(2)}, u32[]{:S(2)}) async-start(f32[128,2,128]{2,1,0:T(2,128)} %bitcast.22), calls=%async_computation | async-start | bytes 262144 | tf_op jit(solution)/shard_map/while/body/eval_jaxpr/all_to_all | solution.py:515
  288.7 14.2 %all-to-all-start.1 = ((f32[128,2,128]{2,1,0:T(2,128)}), f32[128,2,128]{2,1,0:T(2,128)S(1)}, u32[]{:S(2)}, u32[]{:S(2)}) async-start(f32[128,2,128]{2,1,0:T(2,128)} %bitcast.24), calls=%async_computation.1 | async-start | bytes 262144 | tf_op jit(solution)/shard_map/while/body/eval_jaxpr/all_to_all | solution.py:515
  304.1 14.2 %all-to-all-start = ((f32[128,2,128]{2,1,0:T(2,128)}), f32[128,2,128]{2,1,0:T(2,128)S(1)}, u32[]{:S(2)}, u32[]{:S(2)}) async-start(f32[128,2,128]{2,1,0:T(2,128)} %bitcast.22), calls=%async_computation | async-start | bytes 262144 | tf_op jit(solution)/shard_map/while/body/eval_jaxpr/all_to_all | solution.py:515
  319.8 14.2 %all-to-all-start.1 = ((f32[128,2,128]{2,1,0:T(2,128)}), f32[128,2,128]{2,1,0:T(2,128)S(1)}, u32[]{:S(2)}, u32[]{:S(2)}) async-start(f32[128,2,128]{2,1,0:T(2,128)} %bitcast.24), calls=%async_computation.1 | async-start | bytes 262144 | tf_op jit(solution)/shard_map/while/body/eval_jaxpr/all_to_all | solution.py:515
  335.2 14.2 %all-to-all-start = ((f32[128,2,128]{2,1,0:T(2,128)}), f32[128,2,128]{2,1,0:T(2,128)S(1)}, u32[]{:S(2)}, u32[]{:S(2)}) async-start(f32[128,2,128]{2,1,0:T(2,128)} %bitcast.22), calls=%async_computation | async-start | bytes 262144 | tf_op jit(solution)/shard_map/while/body/eval_jaxpr/all_to_all | solution.py:515
  350.8 14.2 %all-to-all-start.1 = ((f32[128,2,128]{2,1,0:T(2,128)}), f32[128,2,128]{2,1,0:T(2,128)S(1)}, u32[]{:S(2)}, u32[]{:S(2)}) async-start(f32[128,2,128]{2,1,0:T(2,128)} %bitcast.24), calls=%async_computation.1 | async-start | bytes 262144 | tf_op jit(solution)/shard_map/while/body/eval_jaxpr/all_to_all | solution.py:515
  366.2 14.2 %all-to-all-start = ((f32[128,2,128]{2,1,0:T(2,128)}), f32[128,2,128]{2,1,0:T(2,128)S(1)}, u32[]{:S(2)}, u32[]{:S(2)}) async-start(f32[128,2,128]{2,1,0:T(2,128)} %bitcast.22), calls=%async_computation | async-start | bytes 262144 | tf_op jit(solution)/shard_map/while/body/eval_jaxpr/all_to_all | solution.py:515
  381.8 14.2 %all-to-all-start.1 = ((f32[128,2,128]{2,1,0:T(2,128)}), f32[128,2,128]{2,1,0:T(2,128)S(1)}, u32[]{:S(2)}, u32[]{:S(2)}) async-start(f32[128,2,128]{2,1,0:T(2,128)} %bitcast.24), calls=%async_computation.1 | async-start | bytes 262144 | tf_op jit(solution)/shard_map/while/body/eval_jaxpr/all_to_all | solution.py:515
  397.2 14.2 %all-to-all-start = ((f32[128,2,128]{2,1,0:T(2,128)}), f32[128,2,128]{2,1,0:T(2,128)S(1)}, u32[]{:S(2)}, u32[]{:S(2)}) async-start(f32[128,2,128]{2,1,0:T(2,128)} %bitcast.22), calls=%async_computation | async-start | bytes 262144 | tf_op jit(solution)/shard_map/while/body/eval_jaxpr/all_to_all | solution.py:515
  412.8 14.2 %all-to-all-start.1 = ((f32[128,2,128]{2,1,0:T(2,128)}), f32[128,2,128]{2,1,0:T(2,128)S(1)}, u32[]{:S(2)}, u32[]{:S(2)}) async-start(f32[128,2,128]{2,1,0:T(2,128)} %bitcast.24), calls=%async_computation.1 | async-start | bytes 262144 | tf_op jit(solution)/shard_map/while/body/eval_jaxpr/all_to_all | solution.py:515
  428.2 14.2 %all-to-all-start.4 = ((f32[128,2,128]{2,1,0:T(2,128)}), f32[128,2,128]{2,1,0:T(2,128)S(1)}, u32[]{:S(2)}, u32[]{:S(2)}) async-start(f32[128,2,128]{2,1,0:T(2,128)} %bitcast.10), calls=%async_computation.4 | async-start | bytes 262144 | tf_op jit(solution)/shard_map/all_to_all | solution.py:515
  444.0 15.4 %all-to-all-start.5 = ((f32[128,4,128]{2,1,0:T(4,128)}), f32[128,4,128]{2,1,0:T(4,128)S(1)}, u32[]{:S(2)}, u32[]{:S(2)}) async-start(f32[128,4,128]{2,1,0:T(4,128)} %bitcast.12), calls=%async_computation.5 | async-start | bytes 524288 | tf_op jit(solution)/shard_map/all_to_all | solution.py:515
